TPU v7x, 32 devices: a whole 2x2x4 slice. The times are simulated.
32 devices in a mesh: seq: 16 (over z, y, x), head: 2 (over core).
Axes of the slice: x: 2, y: 2, z: 4, core: 2. Of those that a mesh axis runs over, the one named last changes fastest.
Arguments:
- queries: bfloat16 [8192, 1024], P('seq', 'head'), may hold values from -8 to 8
- keys: bfloat16 [8192, 1024], P('seq', 'head'), may hold values from -8 to 8
- values: bfloat16 [8192, 1024], P('seq', 'head'), may hold values from -6 to 6
- distances: int32 [4], replicated, may hold values from 1 to 8, as said below
- feature_proj: bfloat16 [64, 128], replicated, may hold values from -6 to 6
- out_proj: bfloat16 [1024, 1024], P('head'), may hold values from -0.1875 to 0.1875
Outputs:
- mixed: bfloat16 [8192, 1024], P('seq', 'head')
Inputs may be any that keep to these rules, and one draw needn't show every extreme that they name: `distances`: four different powers of two; 1 and 16 // 2 are always among them.
All inputs are finite; a program needn't handle non-finite values.
Results may differ from a plain program's by a relative error of at most 0.018.
Values may be sent and summed in bfloat16 or wider, within the bound.
No kernel may reach another device: no remote copies, remote signals or barrier semaphores. Data moves between devices by JAX's collectives and lax.ppermute only.
A program may use at most 128 MiB of HBM per device.

v0:
```python
import functools

import jax
import jax.numpy as jnp
from jax import lax
from jax.sharding import PartitionSpec as P

HEAD_DIM = 64
PARTNERS = 4


def shortened(shard):

    def short(part):
        return part.astype(jnp.bfloat16) if part.dtype == jnp.float32 else part

    return jax.tree.map(short, shard)


def swapped(shard, axis, distance):
    return lax.ppermute(shard, axis, [(i, i ^ 1 << distance) for i in range(lax.axis_size(axis))])


def attend(state, q_rows, k_rows, v_rows):
    top, total, numer = state
    scores = jnp.einsum(
        "thd,shd->hts", q_rows, k_rows, preferred_element_type=jnp.float32
    ) * HEAD_DIM ** (-0.5)
    new_top = jnp.maximum(top, jnp.max(scores, axis=-1))
    factor = jnp.exp(top - new_top)
    probs = jnp.exp(scores - new_top[..., None])
    total = total * factor + jnp.sum(probs, axis=-1)
    numer = numer * factor[..., None] + jnp.einsum(
        "hts,shd->htd", probs.astype(jnp.bfloat16), v_rows, preferred_element_type=jnp.float32
    )
    return (new_top, total, numer)


def fetch_pair(pair, bit):
    return swapped((shortened(pair[0]), shortened(pair[1])), "seq", bit)


def per_device(queries, keys, values, distances, feature_proj, out_proj):
    tokens = queries.shape[0]
    local_width = queries.shape[1]
    heads_here = local_width // HEAD_DIM
    q_three = queries.reshape(tokens, heads_here, HEAD_DIM)
    k_three = keys.reshape(tokens, heads_here, HEAD_DIM)
    v_three = values.reshape(tokens, heads_here, HEAD_DIM)
    root_quarter = HEAD_DIM ** (-0.25)
    k_proj = jnp.einsum("thd,dr->thr", k_three, feature_proj, preferred_element_type=jnp.float32)
    k_float = k_three.astype(jnp.float32)
    square = jnp.sum(k_float * k_float, axis=-1, keepdims=True)
    phi_k = jnp.exp(k_proj * root_quarter - square * 0.5 * HEAD_DIM ** (-0.5)).astype(jnp.bfloat16)
    kv_part = jnp.einsum("thr,the->hre", phi_k, v_three, preferred_element_type=jnp.float32)
    norm_part = jnp.sum(phi_k.astype(jnp.float32), axis=0)
    kv_state, norm_state = lax.psum((kv_part, norm_part), "seq")
    q_proj = (
        jnp.einsum("thd,dr->thr", q_three, feature_proj, preferred_element_type=jnp.float32)
        * root_quarter
    )
    phi_q = jnp.exp(q_proj - jnp.max(q_proj, axis=-1, keepdims=True))
    low_numer = jnp.einsum("thr,hre->the", phi_q, kv_state, precision=lax.Precision.HIGHEST)
    low_denom = jnp.einsum("thr,hr->th", phi_q, norm_state, precision=lax.Precision.HIGHEST)
    low_rank = low_numer / low_denom[..., None]
    nbits = lax.axis_size("seq").bit_length() - 1
    bit_ids = jnp.arange(nbits, dtype=jnp.int32)
    powers = jnp.left_shift(jnp.ones((nbits,), jnp.int32), bit_ids)
    fresh = (
        jnp.full((heads_here, tokens), -jnp.inf, jnp.float32),
        jnp.zeros((heads_here, tokens), jnp.float32),
        jnp.zeros((heads_here, tokens, HEAD_DIM), jnp.float32),
    )
    state = attend(fresh, q_three, k_three, v_three)
    pair_paths = [functools.partial(fetch_pair, bit=level) for level in range(nbits)]
    for partner in range(PARTNERS):
        picked = jnp.sum(jnp.where(distances[partner] == powers, bit_ids, 0))
        k_far, v_far = lax.switch(picked, pair_paths, (k_three, v_three))
        state = attend(state, q_three, k_far, v_far)
    top, total, numer = state
    attended = jnp.transpose(numer / total[..., None], (1, 0, 2))
    heads_out = (attended + low_rank).astype(jnp.bfloat16).reshape(tokens, local_width)
    partial_out = jnp.dot(heads_out, out_proj, preferred_element_type=jnp.float32)
    return lax.psum_scatter(
        partial_out.astype(jnp.bfloat16), "head", scatter_dimension=1, tiled=True
    )


def solution(mesh):
    in_specs = (P("seq", "head"), P("seq", "head"), P("seq", "head"), P(), P(), P("head", None))
    out_specs = P("seq", "head")
    return jax.shard_map(
        per_device, mesh=mesh, in_specs=in_specs, out_specs=out_specs, check_vma=False
    )
```

profile of v0, /device:TPU:0, one launch (start us, length us, event | category | flops | bytes accessed | tf_op | source)
XLA Modules:
  0.0 268.9 jit_solution(14227700500447947845)
XLA Ops:
  6.5 1.3 copy.80
  7.9 1.3 copy.81
  9.3 1.8 convert_reduce_fusion
  11.1 1.0 fusion.112
  12.2 1.3 copy.79
  13.5 4.6 %multiply_reduce_fusion = (f32[8,512]{1,0:T(8,128)S(1)}, f32[8,512,512]{1,2,0:T(8,128)}) fusion(bf16[512,8,64]{0,2,1:T(8,128)(2,1)S(1)} %bitcast.247, bf16[512,8,64]{0,2,1:T(8,128)(2,1)S(1)} %bitcast.272), kind=kOutput, calls=%fused_computation.13 | convolution fusion | flops 272625664 | bytes 9453568 | tf_op jit(solution)/shard_map/thd,shd->hts/dot_general | solution.py:26
  18.0 2.0 multiply_reduce_fusion.1
  20.0 0.7 fusion.111
  20.6 1.3 fusion.100
  22.5 26.7 %conditional.7 = (bf16[512,8,64]{0,2,1:T(8,128)(2,1)}, bf16[512,8,64]{0,2,1:T(8,128)(2,1)}) conditional(s32[]{:T(128)} %clamp.15, (bf16[512,8,64]{0,2,1:T(8,128)(2,1)S(1)}, bf16[512,8,64]{0,2,1:T(8,128)(2,1)S(1)}) %tuple.142, (bf16[512,8,64]{0,2,1:T(8,128)(2,1)S(1)}, bf16[512,8,64]{0,2,1:T(8,128)(2,1)S(1)}) %tuple.143, ...), branch_computations={%region_20.21_spmd, %region_21.22_spmd, %region_22.23_spmd, %regio... | conditional | bytes 4194400 | solution.py:78
  22.5 3.0 %collective-permute-start.26 = (bf16[512,8,64]{0,2,1:T(8,128)(2,1)S(1)}, bf16[512,8,64]{0,2,1:T(8,128)(2,1)}, u32[]{:S(2)}, u32[]{:S(2)}) collective-permute-start(bf16[512,8,64]{0,2,1:T(8,128)(2,1)S(1)} %get-tuple-element.95), channel_id=1, source_target_pairs={{0,4},{2,6},{4,0},{6,2},{8,12},{10,14},{12,8},{14,10},{16,20},{18,... | collective-permute-start | bytes 1572872 | tf_op jit(solution)/shard_map/cond/branch_1_fun/ppermute | solution.py:21
  25.7 12.8 %collective-permute-done.26 = bf16[512,8,64]{0,2,1:T(8,128)(2,1)} collective-permute-done((bf16[512,8,64]{0,2,1:T(8,128)(2,1)S(1)}, bf16[512,8,64]{0,2,1:T(8,128)(2,1)}, u32[]{:S(2)}, u32[]{:S(2)}) %collective-permute-start.26) | collective-permute-done | bytes 524320 | tf_op jit(solution)/shard_map/cond/branch_1_fun/ppermute | solution.py:21
  38.4 10.8 %collective-permute-done.27 = bf16[512,8,64]{0,2,1:T(8,128)(2,1)} collective-permute-done((bf16[512,8,64]{0,2,1:T(8,128)(2,1)S(1)}, bf16[512,8,64]{0,2,1:T(8,128)(2,1)}, u32[]{:S(2)}, u32[]{:S(2)}) %collective-permute-start.27) | collective-permute-done | bytes 524320 | tf_op jit(solution)/shard_map/cond/branch_1_fun/ppermute | solution.py:21
  49.2 5.6 %bitcast_reduce_fusion = (f32[8,512]{1,0:T(8,128)S(1)}, f32[8,512,512]{1,2,0:T(8,128)}) fusion(bf16[512,8,64]{0,2,1:T(8,128)(2,1)} %get-tuple-element.115, bf16[512,8,64]{0,2,1:T(8,128)(2,1)S(1)} %bitcast.249), kind=kOutput, calls=%fused_computation.1 | convolution fusion | flops 272625664 | bytes 9453568 | tf_op jit(solution)/shard_map/thd,shd->hts/dot_general | solution.py:26
  54.8 1.3 fusion.99
  56.6 24.6 %conditional.6 = (bf16[512,8,64]{0,2,1:T(8,128)(2,1)}, bf16[512,8,64]{0,2,1:T(8,128)(2,1)}) conditional(s32[]{:T(128)} %clamp.14, (bf16[512,8,64]{0,2,1:T(8,128)(2,1)S(1)}, bf16[512,8,64]{0,2,1:T(8,128)(2,1)S(1)}) %tuple.146, (bf16[512,8,64]{0,2,1:T(8,128)(2,1)S(1)}, bf16[512,8,64]{0,2,1:T(8,128)(2,1)S(1)}) %tuple.147, ...), branch_computations={%region_14.15_spmd, %region_15.16_spmd, %region_16.17_spmd, %regio... | conditional | bytes 4194400 | solution.py:78
  56.6 1.8 collective-permute-start.16
  58.7 12.9 %collective-permute-done.16 = bf16[512,8,64]{0,2,1:T(8,128)(2,1)} collective-permute-done((bf16[512,8,64]{0,2,1:T(8,128)(2,1)S(1)}, bf16[512,8,64]{0,2,1:T(8,128)(2,1)}, u32[]{:S(2)}, u32[]{:S(2)}) %collective-permute-start.16) | collective-permute-done | bytes 524320 | tf_op jit(solution)/shard_map/cond/branch_0_fun/ppermute | solution.py:21
  71.7 9.5 %collective-permute-done.17 = bf16[512,8,64]{0,2,1:T(8,128)(2,1)} collective-permute-done((bf16[512,8,64]{0,2,1:T(8,128)(2,1)S(1)}, bf16[512,8,64]{0,2,1:T(8,128)(2,1)}, u32[]{:S(2)}, u32[]{:S(2)}) %collective-permute-start.17) | collective-permute-done | bytes 524320 | tf_op jit(solution)/shard_map/cond/branch_0_fun/ppermute | solution.py:21
  81.2 5.6 %bitcast_reduce_fusion.1 = (f32[8,512]{1,0:T(8,128)S(1)}, f32[8,512,512]{1,2,0:T(8,128)}) fusion(bf16[512,8,64]{0,2,1:T(8,128)(2,1)} %get-tuple-element.113, bf16[512,8,64]{0,2,1:T(8,128)(2,1)S(1)} %bitcast.250), kind=kOutput, calls=%fused_computation.4 | convolution fusion | flops 272625664 | bytes 9453568 | tf_op jit(solution)/shard_map/thd,shd->hts/dot_general | solution.py:26
  86.8 1.3 fusion.98
  88.9 24.5 %conditional.5 = (bf16[512,8,64]{0,2,1:T(8,128)(2,1)}, bf16[512,8,64]{0,2,1:T(8,128)(2,1)}) conditional(s32[]{:T(128)} %clamp.13, (bf16[512,8,64]{0,2,1:T(8,128)(2,1)S(1)}, bf16[512,8,64]{0,2,1:T(8,128)(2,1)S(1)}) %tuple.150, (bf16[512,8,64]{0,2,1:T(8,128)(2,1)S(1)}, bf16[512,8,64]{0,2,1:T(8,128)(2,1)S(1)}) %tuple.151, ...), branch_computations={%region_8.9_spmd, %region_9.10_spmd, %region_10.11_spmd, %region_1... | conditional | bytes 4194400 | solution.py:78
  88.9 1.5 collective-permute-start.12
  90.4 0.6 collective-permute-start.13
  91.0 13.5 %collective-permute-done.12 = bf16[512,8,64]{0,2,1:T(8,128)(2,1)} collective-permute-done((bf16[512,8,64]{0,2,1:T(8,128)(2,1)S(1)}, bf16[512,8,64]{0,2,1:T(8,128)(2,1)}, u32[]{:S(2)}, u32[]{:S(2)}) %collective-permute-start.12) | collective-permute-done | bytes 524320 | tf_op jit(solution)/shard_map/cond/branch_2_fun/ppermute | solution.py:21
  104.4 9.0 %collective-permute-done.13 = bf16[512,8,64]{0,2,1:T(8,128)(2,1)} collective-permute-done((bf16[512,8,64]{0,2,1:T(8,128)(2,1)S(1)}, bf16[512,8,64]{0,2,1:T(8,128)(2,1)}, u32[]{:S(2)}, u32[]{:S(2)}) %collective-permute-start.13) | collective-permute-done | bytes 524320 | tf_op jit(solution)/shard_map/cond/branch_2_fun/ppermute | solution.py:21
  113.4 5.6 %bitcast_reduce_fusion.2 = (f32[8,512]{1,0:T(8,128)S(1)}, f32[8,512,512]{1,2,0:T(8,128)}) fusion(bf16[512,8,64]{0,2,1:T(8,128)(2,1)} %get-tuple-element.111, bf16[512,8,64]{0,2,1:T(8,128)(2,1)S(1)} %bitcast.251), kind=kOutput, calls=%fused_computation.7 | convolution fusion | flops 272625664 | bytes 9453568 | tf_op jit(solution)/shard_map/thd,shd->hts/dot_general | solution.py:26
  119.0 1.3 fusion.97
  120.9 45.7 %conditional.4 = (bf16[512,8,64]{0,2,1:T(8,128)(2,1)}, bf16[512,8,64]{0,2,1:T(8,128)(2,1)}) conditional(s32[]{:T(128)} %clamp.12, (bf16[512,8,64]{0,2,1:T(8,128)(2,1)S(1)}, bf16[512,8,64]{0,2,1:T(8,128)(2,1)S(1)}) %tuple.154, (bf16[512,8,64]{0,2,1:T(8,128)(2,1)S(1)}, bf16[512,8,64]{0,2,1:T(8,128)(2,1)S(1)}) %tuple.155, ...), branch_computations={%region_2.0_spmd, %region_3.0_spmd, %region_4.0_spmd, %region_5.0_... | conditional | bytes 4194400 | solution.py:78
  120.9 2.3 collective-permute-start.6
  123.2 0.7 collective-permute-start.7
  123.9 31.9 %collective-permute-done.6 = bf16[512,8,64]{0,2,1:T(8,128)(2,1)} collective-permute-done((bf16[512,8,64]{0,2,1:T(8,128)(2,1)S(1)}, bf16[512,8,64]{0,2,1:T(8,128)(2,1)}, u32[]{:S(2)}, u32[]{:S(2)}) %collective-permute-start.6) | collective-permute-done | bytes 524320 | tf_op jit(solution)/shard_map/cond/branch_3_fun/ppermute | solution.py:21
  155.8 10.8 %collective-permute-done.7 = bf16[512,8,64]{0,2,1:T(8,128)(2,1)} collective-permute-done((bf16[512,8,64]{0,2,1:T(8,128)(2,1)S(1)}, bf16[512,8,64]{0,2,1:T(8,128)(2,1)}, u32[]{:S(2)}, u32[]{:S(2)}) %collective-permute-start.7) | collective-permute-done | bytes 524320 | tf_op jit(solution)/shard_map/cond/branch_3_fun/ppermute | solution.py:21
  166.6 5.6 %bitcast_reduce_fusion.3 = (f32[8,512]{1,0:T(8,128)S(1)}, f32[8,512,512]{1,2,0:T(8,128)}) fusion(bf16[512,8,64]{0,2,1:T(8,128)(2,1)} %get-tuple-element.109, bf16[512,8,64]{0,2,1:T(8,128)(2,1)S(1)} %bitcast.252), kind=kOutput, calls=%fused_computation.10 | convolution fusion | flops 272625664 | bytes 9453568 | tf_op jit(solution)/shard_map/thd,shd->hts/dot_general | solution.py:26
  172.2 41.2 %psum.15 = f32[8,128]{1,0:T(8,128)S(1)} all-reduce(f32[8,128]{1,0:T(8,128)S(1)} %get-tuple-element.175), channel_id=1, replica_groups=mesh['seq'=16,'head'=2] {'seq'}, use_global_device_ids=true, to_apply=%region_34.35 | all-reduce | flops 1024 | bytes 8192 | tf_op jit(solution)/shard_map/psum | solution.py:57
  213.5 4.9 %fusion.4 = f32[8,512]{1,0:T(8,128)S(1)} fusion(f32[8,512,512]{1,2,0:T(8,128)} %get-tuple-element.166, f32[8,512]{1,0:T(8,128)S(1)} %get-tuple-element.165), kind=kLoop, calls=%fused_computation.14 | loop fusion | flops 6287360 | bytes 8421376 | tf_op jit(solution)/shard_map/reduce_sum | solution.py:32
  218.4 0.8 copy-done.1
  219.2 6.1 %fusion.6 = (f32[8,512]{1,0:T(8,128)S(1)}, f32[8,512]{1,0:T(8,128)S(1)}) fusion(f32[8,512,512]{1,2,0:T(8,128)S(1)} %copy-done.1, f32[8,512]{1,0:T(8,128)S(1)} %get-tuple-element.157, f32[8,512]{1,0:T(8,128)S(1)} %get-tuple-element.156, f32[8,512,512]{1,2,0:T(8,128)} %get-tuple-element.172), kind=kLoop, calls=%fused_computation.16 | loop fusion | flops 12574720 | bytes 16842752 | tf_op jit(solution)/shard_map/reduce_sum | solution.py:32
  225.4 6.0 %fusion.10 = (f32[8,512]{1,0:T(8,128)S(1)}, f32[8,512]{1,0:T(8,128)S(1)}) fusion(f32[8,512,512]{1,2,0:T(8,128)} %get-tuple-element.170, f32[8,512]{1,0:T(8,128)S(1)} %get-tuple-element.155, f32[8,512]{1,0:T(8,128)S(1)} %get-tuple-element.154, f32[8,512,512]{1,2,0:T(8,128)S(1)} %bitcast.244), kind=kLoop, calls=%fused_computation.20 | loop fusion | flops 12574720 | bytes 16842752 | tf_op jit(solution)/shard_map/reduce_sum | solution.py:32
  231.5 1.6 fusion.78
  233.1 4.8 %fusion.69 = f32[512,8,64]{0,2,1:T(8,128)S(1)} fusion(f32[512,8,64]{0,2,1:T(8,128)S(1)} %fusion.78, bf16[512,8,64]{0,2,1:T(8,128)(2,1)} %get-tuple-element.110, f32[8,512,512]{1,2,0:T(8,128)} %get-tuple-element.174, f32[8,512]{1,0:T(8,128)S(1)} %get-tuple-element.157, f32[512,8]{0,1:T(8,128)S(1)} %get-tuple-element.152), kind=kOutput, calls=%fused_computation.59 | convolution fusion | flops 275251200 | bytes 11042816 | tf_op jit(solution)/shard_map/hts,shd->htd/dot_general | solution.py:33
  237.9 4.8 %fusion.72 = f32[512,8,64]{0,2,1:T(8,128)S(1)} fusion(f32[512,8,64]{0,2,1:T(8,128)S(1)} %fusion.69, bf16[512,8,64]{0,2,1:T(8,128)(2,1)} %get-tuple-element.112, f32[8,512,512]{1,2,0:T(8,128)} %get-tuple-element.172, f32[8,512]{1,0:T(8,128)S(1)} %get-tuple-element.156, f32[512,8]{0,1:T(8,128)S(1)} %get-tuple-element.151), kind=kOutput, calls=%fused_computation.60 | convolution fusion | flops 275251200 | bytes 11042816 | tf_op jit(solution)/shard_map/hts,shd->htd/dot_general | solution.py:33
  242.7 3.1 %fusion.75 = f32[512,8,64]{0,2,1:T(8,128)S(1)} fusion(f32[512,8,64]{0,2,1:T(8,128)S(1)} %fusion.72, bf16[512,8,64]{0,2,1:T(8,128)(2,1)} %get-tuple-element.114, f32[8,512,512]{1,2,0:T(8,128)S(1)} %bitcast.246, f32[8,512]{1,0:T(8,128)S(1)} %get-tuple-element.155, f32[512,8]{0,1:T(8,128)S(1)} %get-tuple-element.150), kind=kOutput, calls=%fused_computation.61 | convolution fusion | flops 275251200 | bytes 11042816 | tf_op jit(solution)/shard_map/hts,shd->htd/dot_general | solution.py:33
  245.8 3.8 %fusion.57 = f32[512,8,64]{0,2,1:T(8,128)} fusion(f32[512,8,64]{0,2,1:T(8,128)S(1)} %fusion.75, bf16[512,8,64]{0,2,1:T(8,128)(2,1)} %get-tuple-element.116, f32[8,512,512]{1,2,0:T(8,128)S(1)} %bitcast.244, f32[8,512]{1,0:T(8,128)S(1)} %get-tuple-element.154), kind=kOutput, calls=%fused_computation.55 | convolution fusion | flops 274989056 | bytes 11026432 | tf_op jit(solution)/shard_map/hts,shd->htd/dot_general | solution.py:33
  249.6 2.1 fusion.34
  251.7 4.0 %fusion.81 = bf16[512,8,64]{0,2,1:T(8,128)(2,1)S(1)} fusion(f32[8,128,64]{1,2,0:T(8,128)} %all-reduce.2.cloned.1.call-done, f32[512,8,128]{2,0,1:T(8,128)S(1)} %copy-done.2, f32[512,8]{0,1:T(8,128)S(1)} %get-tuple-element.163, f32[512,8,64]{0,2,1:T(8,128)} %fusion.57, f32[512,8]{0,1:T(8,128)S(1)} %bitcast.290, f32[512,8]{0,1:T(8,128)S(1)} %get-tuple-element.149), kind=kOutput, calls=%fused_computation.63 | convolution fusion | flops 404750336 | bytes 3981312 | tf_op jit(solution)/shard_map/thr,hre->the/dot_general | solution.py:63
  255.7 1.7 convolution_convert_fusion
  257.5 4.6 %reduce-scatter.2.cloned.1.call-done = bf16[512,512]{1,0:T(8,128)(2,1)} async-done(((bf16[512,1024]{1,0:T(8,128)(2,1)}), bf16[512,512]{1,0:T(8,128)(2,1)}) %reduce-scatter.2.cloned.1.call-update) | async-done | bytes 524304 | tf_op jit(solution)/shard_map/reduce_scatter | solution.py:84
  (36 shorter events, 0.8 us)
Async XLA Ops:
  6.5 249.2 %copy-start = (bf16[512,1024]{1,0:T(8,128)(2,1)S(1)}, bf16[512,1024]{1,0:T(8,128)(2,1)}, u32[]{:S(2)}) copy-start(bf16[512,1024]{1,0:T(8,128)(2,1)} %param.27) | copy-start | bytes 3145732
  6.5 245.2 %all-reduce.2.cloned.1.call-start = ((), (), s32[]{:S(2)}) async-start(), calls=%async_computation.1 | async-start | bytes 524288 | tf_op jit(solution)/shard_map/psum | solution.py:57
  7.9 10.1 %copy-start.3 = (bf16[64,128]{1,0:T(8,128)(2,1)S(1)}, bf16[64,128]{1,0:T(8,128)(2,1)}, u32[]{:S(2)}) copy-start(bf16[64,128]{1,0:T(8,128)(2,1)} %param.26) | copy-start | bytes 49156
  9.3 10.7 %copy-start.4 = (s32[4]{0:T(128)S(1)}, s32[4]{0:T(128)}, u32[]{:S(2)}) copy-start(s32[4]{0:T(128)} %param.25) | copy-start | bytes 52
  12.1 249.9 %reduce-scatter.2.cloned.1.call-start = ((), (), s32[]{:S(2)}) async-start(), calls=%async_computation.2 | async-start | bytes 1572864 | tf_op jit(solution)/shard_map/reduce_scatter | solution.py:84
  22.5 15.9 %collective-permute-start.26 = (bf16[512,8,64]{0,2,1:T(8,128)(2,1)S(1)}, bf16[512,8,64]{0,2,1:T(8,128)(2,1)}, u32[]{:S(2)}, u32[]{:S(2)}) collective-permute-start(bf16[512,8,64]{0,2,1:T(8,128)(2,1)S(1)} %get-tuple-element.95), channel_id=1, source_target_pairs={{0,4},{2,6},{4,0},{6,2},{8,12},{10,14},{12,8},{14,10},{16,20},{18,... | collective-permute-start | bytes 1572872 | tf_op jit(solution)/shard_map/cond/branch_1_fun/ppermute | solution.py:21
  25.6 23.6 %collective-permute-start.27 = (bf16[512,8,64]{0,2,1:T(8,128)(2,1)S(1)}, bf16[512,8,64]{0,2,1:T(8,128)(2,1)}, u32[]{:S(2)}, u32[]{:S(2)}) collective-permute-start(bf16[512,8,64]{0,2,1:T(8,128)(2,1)S(1)} %get-tuple-element.96), channel_id=1, source_target_pairs={{0,4},{2,6},{4,0},{6,2},{8,12},{10,14},{12,8},{14,10},{16,20},{18,... | collective-permute-start | bytes 1572872 | tf_op jit(solution)/shard_map/cond/branch_1_fun/ppermute | solution.py:21
  56.6 15.1 %collective-permute-start.16 = (bf16[512,8,64]{0,2,1:T(8,128)(2,1)S(1)}, bf16[512,8,64]{0,2,1:T(8,128)(2,1)}, u32[]{:S(2)}, u32[]{:S(2)}) collective-permute-start(bf16[512,8,64]{0,2,1:T(8,128)(2,1)S(1)} %get-tuple-element.85), channel_id=1, source_target_pairs={{0,2},{2,0},{4,6},{6,4},{8,10},{10,8},{12,14},{14,12},{16,18},{18,... | collective-permute-start | bytes 1572872 | tf_op jit(solution)/shard_map/cond/branch_0_fun/ppermute | solution.py:21
  58.4 22.8 %collective-permute-start.17 = (bf16[512,8,64]{0,2,1:T(8,128)(2,1)S(1)}, bf16[512,8,64]{0,2,1:T(8,128)(2,1)}, u32[]{:S(2)}, u32[]{:S(2)}) collective-permute-start(bf16[512,8,64]{0,2,1:T(8,128)(2,1)S(1)} %get-tuple-element.86), channel_id=1, source_target_pairs={{0,2},{2,0},{4,6},{6,4},{8,10},{10,8},{12,14},{14,12},{16,18},{18,... | collective-permute-start | bytes 1572872 | tf_op jit(solution)/shard_map/cond/branch_0_fun/ppermute | solution.py:21
  88.9 15.6 %collective-permute-start.12 = (bf16[512,8,64]{0,2,1:T(8,128)(2,1)S(1)}, bf16[512,8,64]{0,2,1:T(8,128)(2,1)}, u32[]{:S(2)}, u32[]{:S(2)}) collective-permute-start(bf16[512,8,64]{0,2,1:T(8,128)(2,1)S(1)} %get-tuple-element.81), channel_id=1, source_target_pairs={{0,8},{2,10},{4,12},{6,14},{8,0},{10,2},{12,4},{14,6},{16,24},{18,... | collective-permute-start | bytes 1572872 | tf_op jit(solution)/shard_map/cond/branch_2_fun/ppermute | solution.py:21
  90.4 23.0 %collective-permute-start.13 = (bf16[512,8,64]{0,2,1:T(8,128)(2,1)S(1)}, bf16[512,8,64]{0,2,1:T(8,128)(2,1)}, u32[]{:S(2)}, u32[]{:S(2)}) collective-permute-start(bf16[512,8,64]{0,2,1:T(8,128)(2,1)S(1)} %get-tuple-element.82), channel_id=1, source_target_pairs={{0,8},{2,10},{4,12},{6,14},{8,0},{10,2},{12,4},{14,6},{16,24},{18,... | collective-permute-start | bytes 1572872 | tf_op jit(solution)/shard_map/cond/branch_2_fun/ppermute | solution.py:21
  120.9 34.9 %collective-permute-start.6 = (bf16[512,8,64]{0,2,1:T(8,128)(2,1)S(1)}, bf16[512,8,64]{0,2,1:T(8,128)(2,1)}, u32[]{:S(2)}, u32[]{:S(2)}) collective-permute-start(bf16[512,8,64]{0,2,1:T(8,128)(2,1)S(1)} %get-tuple-element.75), channel_id=1, source_target_pairs={{0,16},{2,18},{4,20},{6,22},{8,24},{10,26},{12,28},{14,30},{16,0},... | collective-permute-start | bytes 1572872 | tf_op jit(solution)/shard_map/cond/branch_3_fun/ppermute | solution.py:21
  123.2 43.4 %collective-permute-start.7 = (bf16[512,8,64]{0,2,1:T(8,128)(2,1)S(1)}, bf16[512,8,64]{0,2,1:T(8,128)(2,1)}, u32[]{:S(2)}, u32[]{:S(2)}) collective-permute-start(bf16[512,8,64]{0,2,1:T(8,128)(2,1)S(1)} %get-tuple-element.76), channel_id=1, source_target_pairs={{0,16},{2,18},{4,20},{6,22},{8,24},{10,26},{12,28},{14,30},{16,0},... | collective-permute-start | bytes 1572872 | tf_op jit(solution)/shard_map/cond/branch_3_fun/ppermute | solution.py:21
  213.5 5.8 %copy-start.1 = (f32[8,512,512]{1,2,0:T(8,128)S(1)}, f32[8,512,512]{1,2,0:T(8,128)}, u32[]{:S(2)}) copy-start(f32[8,512,512]{1,2,0:T(8,128)} %get-tuple-element.174) | copy-start | bytes 25165828
  213.5 11.9 %slice-start.2 = ((s8[8388608]{0:T(1024)(128)(4,1)}), s8[4194304]{0:T(1024)(128)(4,1)S(1)}, s32[]{:S(2)}) async-start(s8[8388608]{0:T(1024)(128)(4,1)} %bitcast.243), calls=%async_computation.5 | async-start | bytes 8388608
  219.2 6.2 %slice-start.3 = ((s8[8388608]{0:T(1024)(128)(4,1)}), s8[4194304]{0:T(1024)(128)(4,1)S(1)}, s32[]{:S(2)}) async-start(s8[8388608]{0:T(1024)(128)(4,1)} %bitcast.243), calls=%async_computation.6 | async-start | bytes 8388608
  219.2 12.3 %slice-start = ((s8[8388608]{0:T(1024)(128)(4,1)}), s8[4194304]{0:T(1024)(128)(4,1)S(1)}, s32[]{:S(2)}) async-start(s8[8388608]{0:T(1024)(128)(4,1)} %bitcast.241), calls=%async_computation.3 | async-start | bytes 8388608
  225.4 6.1 %slice-start.1 = ((s8[8388608]{0:T(1024)(128)(4,1)}), s8[4194304]{0:T(1024)(128)(4,1)S(1)}, s32[]{:S(2)}) async-start(s8[8388608]{0:T(1024)(128)(4,1)} %bitcast.241), calls=%async_computation.4 | async-start | bytes 8388608
  233.1 9.6 %slice-start.4 = ((s8[8388608]{0:T(1024)(128)(4,1)}), s8[4194304]{0:T(1024)(128)(4,1)S(1)}, s32[]{:S(2)}) async-start(s8[8388608]{0:T(1024)(128)(4,1)} %bitcast.245), calls=%async_computation.7 | async-start | bytes 8388608
  237.9 4.8 %slice-start.5 = ((s8[8388608]{0:T(1024)(128)(4,1)}), s8[4194304]{0:T(1024)(128)(4,1)S(1)}, s32[]{:S(2)}) async-start(s8[8388608]{0:T(1024)(128)(4,1)} %bitcast.245), calls=%async_computation.8 | async-start | bytes 8388608
  242.7 6.9 %copy-start.2 = (f32[512,8,128]{2,0,1:T(8,128)S(1)}, f32[512,8,128]{2,0,1:T(8,128)}, u32[]{:S(2)}) copy-start(f32[512,8,128]{2,0,1:T(8,128)} %get-tuple-element.164) | copy-start | bytes 6291460
Sparse Core Ops, SparseCore 0:
  12.6 109.8 all-reduce.1
  257.6 4.3 reduce-scatter.1
where the time goes:
time: 270 us; the launch traced here: 269 us
  waiting for transfers between devices  116 us (43%)
  matrix products  57.5 us (21%)
  blocking collectives  41.2 us (15%)
  other arithmetic  22.5 us (8%)
  between operations  16.1 us (6%)
  starting transfers between devices  10.4 us (4%)
  local copies, waits for them, and re-layouts  5.37 us (2%)
    ppermute x8, waiting for transfers between devices, swapped(): lax.ppermute(shard, axis, [(i, i ^ 1 << distance) for i in range(lax.axis...  111 us
    psum x1, blocking collectives, per_device(): kv_state, norm_state = lax.psum((kv_part, norm_part), 'seq')  41.2 us
    dot_general x5, matrix products, attend(): jnp.einsum('thd,shd->hts', q_rows, k_rows, preferred_element_type=jnp.flo...  26.9 us
    dot_general x5, matrix products, attend(): jnp.einsum('hts,shd->htd', probs.astype(jnp.bfloat16), v_rows, preferred_...  18 us
    reduce_sum x3, other arithmetic, attend(): total = total * factor + jnp.sum(probs, axis=-1)  17.1 us
    ppermute x8, starting transfers between devices, swapped(): lax.ppermute(shard, axis, [(i, i ^ 1 << distance) for i in range(lax.axis...  10.3 us
  transfers between devices with their start and end apart: 10, of which 9 were waited for; matrix products, arithmetic and copies ran while one was open for 27% of the time, Pallas kernels for 0%

commit v1 on v0

v1 whole, which is shorter than its diff:
```python
import functools

import jax
import jax.numpy as jnp
from jax import lax
from jax.experimental import pallas as pl
from jax.experimental.pallas import tpu as pltpu
from jax.sharding import PartitionSpec as P

HEAD_DIM = 64
PARTNERS = 4
PAIR = 2 * HEAD_DIM
NT = (((1,), (1,)), ((), ()))
VMEM = pl.BlockSpec(memory_space=pltpu.VMEM)
VMEM_LIMIT = 20 * 2**20
COST = pl.CostEstimate(flops=1000, transcendentals=0, bytes_accessed=0)


def low_lanes(rows):
    return lax.broadcasted_iota(jnp.int32, (rows, PAIR), 1) < HEAD_DIM


def half_of(pair, half, other):
    low = low_lanes(pair.shape[0])
    fill = jnp.full_like(pair, other)
    return jnp.where(low, pair, fill) if half == 0 else jnp.where(low, fill, pair)


def cols(ref, c):
    return ref[:, c * PAIR:(c + 1) * PAIR]


def block_of(refs):
    return functools.reduce(jnp.add, [ref[...] for ref in refs])


def weigh_head(q_pair, k_pairs, half):
    q_one = half_of(q_pair, half, 0)
    scores = [lax.dot_general(q_one, k, NT, preferred_element_type=jnp.float32) for k in k_pairs]
    top = functools.reduce(jnp.maximum, [jnp.max(s, axis=-1, keepdims=True) for s in scores])
    return top, [jnp.exp(s - top).astype(jnp.bfloat16) for s in scores]


def scaled(q_pair):
    return q_pair * jnp.asarray(HEAD_DIM ** -0.5, q_pair.dtype)


def add_values(weights, v_pairs, half):
    parts = [
        jnp.dot(w, half_of(v, half, 1), preferred_element_type=jnp.float32)
        for w, v in zip(weights, v_pairs)
    ]
    return functools.reduce(jnp.add, parts)


def numer_denom(first, second):
    low = low_lanes(first.shape[0])
    denom = pltpu.roll(jnp.where(low, second, first), HEAD_DIM, 1)
    return jnp.where(low, first, second), denom


def joined(states):
    top = functools.reduce(jnp.maximum, [t for t, _, _ in states])
    factors = [jnp.exp(t - top) for t, _, _ in states]
    numer = functools.reduce(jnp.add, [n * f for (_, n, _), f in zip(states, factors)])
    denom = functools.reduce(jnp.add, [d * f for (_, _, d), f in zip(states, factors)])
    return top, numer, denom


def kernel_call(body, outs, args, name):
    return pl.pallas_call(
        body,
        out_shape=outs,
        in_specs=[VMEM] * len(args),
        out_specs=jax.tree.map(lambda _: VMEM, outs),
        compiler_params=pltpu.CompilerParams(vmem_limit_bytes=VMEM_LIMIT),
        cost_estimate=COST,
        name=name,
    )(*args)


def pairs_call(body, outs, args, pairs, name):
    def every_pair(*refs):
        for c in range(pairs):
            widths = [ref.shape[1] // pairs for ref in refs]
            body(*[ref.at[:, c * n:(c + 1) * n] for ref, n in zip(refs, widths)])

    outs = [pltpu.VMEM(o.shape, o.dtype) for o in outs]
    return kernel_call(every_pair, outs, args, name)


def attend(q, blocks, before, name):
    tokens, width = q.shape
    args = [q] + [x for block in blocks for x in block] + list(before or [])
    count = 1 + 2 * len(blocks)

    def body(*refs):
        outs = refs[-3:]
        q_pair = scaled(refs[0][...])
        k_pairs = [r[...] for r in refs[1:count:2]]
        v_pairs = [r[...] for r in refs[2:count:2]]
        tops, sums = [], []
        for half in range(2):
            top, weights = weigh_head(q_pair, k_pairs, half)
            tops.append(top)
            sums.append(add_values(weights, v_pairs, half))
        state = (jnp.where(low_lanes(tokens), *tops), *numer_denom(*sums))
        if before is not None:
            state = joined([state, tuple(r[...] for r in refs[count:-3])])
        for out, value in zip(outs, state):
            out[...] = value

    outs = [jax.ShapeDtypeStruct((tokens, width), jnp.float32)] * 3
    return pairs_call(body, outs, args, width // PAIR, name)


def weigh(q, parts, name):
    tokens, width = q.shape
    keys = parts[0].shape[0]

    def body(q_ref, *refs):
        w_out, top_out = refs[-2:]
        q_pair = scaled(q_ref[...])
        k_pair = block_of(refs[:-2])
        tops = []
        for half in range(2):
            top, weights = weigh_head(q_pair, [k_pair], half)
            tops.append(top)
            w_out[:, half * keys:(half + 1) * keys] = weights[0]
        top_out[...] = jnp.where(low_lanes(tokens), *tops)

    outs = [
        jax.ShapeDtypeStruct((tokens, width // HEAD_DIM * keys), jnp.bfloat16),
        jax.ShapeDtypeStruct((tokens, width), jnp.float32),
    ]
    return pairs_call(body, outs, [q] + list(parts), width // PAIR, name)


def gather(before, weights, tops, parts, low_rank, name):
    tokens, width = tops.shape
    keys = parts[0].shape[0]

    def body(*refs):
        w_ref, top_ref, low_ref, out = refs[3], refs[4], refs[-2], refs[-1]
        v_pair = block_of(refs[5:-2])
        sums = [
            add_values([w_ref[:, half * keys:(half + 1) * keys]], [v_pair], half)
            for half in range(2)
        ]
        state = (top_ref[...], *numer_denom(*sums))
        _, numer, denom = joined([tuple(r[...] for r in refs[:3]), state])
        out[...] = (numer / denom + low_ref[...]).astype(jnp.bfloat16)

    args = list(before) + [weights, tops] + list(parts) + [low_rank]
    outs = [jax.ShapeDtypeStruct((tokens, width), jnp.bfloat16)]
    return pairs_call(body, outs, args, width // PAIR, name)[0]


def twice(feat):
    return jnp.concatenate([feat, feat], axis=0)


def state_rows(pairs, features):
    return pairs * features + features


def key_state(k, v, feat):
    tokens, width = k.shape
    pairs, features = width // PAIR, feat.shape[1]
    spread = PAIR // (2 * pairs)

    def body(k_ref, v_ref, feat_ref, out):
        feat_t = twice(feat_ref[...].astype(jnp.float32)).T.astype(jnp.bfloat16)
        lane = lax.broadcasted_iota(jnp.int32, (features, PAIR), 1)
        norms = jnp.zeros((features, PAIR), jnp.float32)
        for c in range(pairs):
            k_pair, v_pair = cols(k_ref, c), cols(v_ref, c)
            k_float = k_pair.astype(jnp.float32)
            square = k_float * k_float
            square_hi = square.astype(jnp.bfloat16)
            square_lo = (square - square_hi.astype(jnp.float32)).astype(jnp.bfloat16)
            parts = []
            for half in range(2):
                proj = lax.dot_general(
                    half_of(feat_t, half, 0), k_pair, NT, preferred_element_type=jnp.float32
                )
                ones = half_of(jnp.ones((16, PAIR), jnp.bfloat16), half, 0)
                size = lax.dot_general(ones, square_hi, NT, preferred_element_type=jnp.float32)
                size += lax.dot_general(ones, square_lo, NT, preferred_element_type=jnp.float32)
                phi = jnp.exp(
                    proj * HEAD_DIM ** -0.25 - size[0:1, :] * (0.5 * HEAD_DIM ** -0.5)
                ).astype(jnp.bfloat16)
                parts.append(
                    jnp.dot(phi, half_of(v_pair, half, 1), preferred_element_type=jnp.float32)
                )
            out[c * features:(c + 1) * features, :] = jnp.where(
                low_lanes(features), parts[0], parts[1]
            ).astype(jnp.bfloat16)
            for half in range(2):
                at = (2 * c + half) * spread
                column = parts[half][:, (1 - half) * HEAD_DIM:(1 - half) * HEAD_DIM + 1]
                norms = jnp.where((lane >= at) & (lane < at + spread), column, norms)
        out[pairs * features:, :] = norms.astype(jnp.bfloat16)

    outs = jax.ShapeDtypeStruct((state_rows(pairs, features), PAIR), jnp.bfloat16)
    return kernel_call(body, outs, [k, v, feat], "key_state")


def low_rank_rows(q, feat, state):
    tokens, width = q.shape
    pairs, features = width // PAIR, feat.shape[1]
    spread = PAIR // (2 * pairs)

    def body(q_ref, feat_ref, state_ref, out):
        feat_two = twice(feat_ref[...])
        norms = state_ref[pairs * features:, :]
        for c in range(pairs):
            q_pair = cols(q_ref, c)
            kv = state_ref[c * features:(c + 1) * features, :]
            low = low_lanes(features)
            parts = []
            for half in range(2):
                proj = jnp.dot(
                    half_of(q_pair, half, 0), feat_two, preferred_element_type=jnp.float32
                ) * HEAD_DIM ** -0.25
                phi = jnp.exp(proj - jnp.max(proj, axis=-1, keepdims=True)).astype(jnp.bfloat16)
                at = (2 * c + half) * spread
                column = jnp.broadcast_to(norms[:, at:at + 1], kv.shape)
                both = jnp.where(low, kv, column) if half == 0 else jnp.where(low, column, kv)
                parts.append(jnp.dot(phi, both, preferred_element_type=jnp.float32))
            numer, denom = numer_denom(*parts)
            out[:, c * PAIR:(c + 1) * PAIR] = numer / denom

    outs = jax.ShapeDtypeStruct((tokens, width), jnp.float32)
    return kernel_call(body, outs, [q, feat, state], "low_rank")


def project(acc, parts, dtype, name):
    tokens, width = parts[0][0].shape[0], parts[0][1].shape[1]

    def body(*refs):
        out = refs[-1]
        rest = list(refs[:-1])
        total = rest.pop(0)[...] if acc is not None else None
        for rows, _, first in parts:
            rows_ref, w_ref = rest.pop(0), rest.pop(0)
            w = w_ref[first:first + rows.shape[1], :]
            part = jnp.dot(rows_ref[...], w, preferred_element_type=jnp.float32)
            total = part if total is None else total + part
        out[...] = total.astype(out.dtype)

    args = ([] if acc is None else [acc]) + [x for rows, w, _ in parts for x in (rows, w)]
    return kernel_call(body, jax.ShapeDtypeStruct((tokens, width), dtype), args, name)


def swapped(shard, axis, distance):
    return lax.ppermute(shard, axis, [(i, i ^ distance) for i in range(lax.axis_size(axis))])


def moved(shard, steps):
    span = lax.axis_size("seq") // 4
    return lax.ppermute(
        shard, "seq", [(a * span + r, b * span + r) for a, b in steps for r in range(span)]
    )


def halves_summed(state, bit, index):
    half = state.shape[0] // 2
    mine = (index >> bit) & 1
    kept = lax.dynamic_slice_in_dim(state, mine * half, half)
    sent = lax.dynamic_slice_in_dim(state, (1 - mine) * half, half)
    return kept + swapped(sent, "seq", 1 << bit)


def halves_joined(half, bit, index):
    far = swapped(half, "seq", 1 << bit)
    mine = (index >> bit) & 1
    return jnp.where(
        mine == 0, jnp.concatenate([half, far], axis=0), jnp.concatenate([far, half], axis=0)
    )


def every_distance(q, k, v, feat, w):
    index = lax.axis_index("seq")
    core = lax.axis_index("head")
    width = q.shape[1]

    first_steps = [(1, 3), (2, 0), (0, 1), (3, 2)]
    second_steps = [(1, 2), (2, 1)]
    edge_steps = [(1, 0), (2, 3)]
    after = lax.optimization_barrier
    k_1 = moved(k, first_steps)
    v_1 = moved(v, first_steps)
    k_near = [swapped(k, "seq", d) for d in (1, 2)]
    sums = attend(q, [(k, v)], None, "attend_own")
    state = key_state(k, v, feat)

    state, k_1, k_near, sums = after((state, k_1, k_near, sums))
    k_2 = moved(k_1, second_steps)
    state = halves_summed(state, 1, index)
    state = halves_summed(state, 0, index)
    state, v_next = after((state, v))
    v_near = [swapped(v_next, "seq", d) for d in (1, 2)]

    state, v_1, k_last = after((state, v_1, k))
    state = state + swapped(state, "seq", 4)
    k_3 = moved(k_last, edge_steps)
    sums = attend(q, [(k_1, v_1)], sums, "attend_first")

    v_near, v_1, v_last, sums = after((v_near, v_1, v, sums))
    v_2 = moved(v_1, second_steps)
    v_3 = moved(v_last, edge_steps)
    state, k_2 = after((state, k_2))
    state = state + swapped(state, "seq", 8)
    sums = attend(q, list(zip(k_near, v_near)), sums, "attend_near")
    state, k_3, sums = after((state, k_3, sums))
    state = halves_joined(state, 0, index)
    state = halves_joined(state, 1, index)

    w_own = lax.dynamic_slice_in_dim(w, core * width, width, axis=1)
    w_far = swapped(lax.dynamic_slice_in_dim(w, (1 - core) * width, width, axis=1), "head", 1)

    last = weigh(q, [k_2, k_3], "weigh_last")
    low = low_rank_rows(q, feat, state)
    rows = gather(sums, *last, [v_2, v_3], low, "gather_last")
    far_rows = swapped(rows, "head", 1)
    acc = project(None, [(rows, w_own, 0)], jnp.float32, "project_own")
    return project(acc, [(far_rows, w_far, 0)], jnp.bfloat16, "project_far")


def chosen_distances(q, k, v, distances, feat, w):
    state = key_state(k, v, feat).astype(jnp.float32)
    state = lax.psum(state, "seq").astype(jnp.bfloat16)
    bits = lax.axis_size("seq").bit_length() - 1
    bit_ids = jnp.arange(bits, dtype=jnp.int32)
    powers = jnp.left_shift(jnp.ones((bits,), jnp.int32), bit_ids)

    def path(bit):
        return lambda pair: (swapped(pair[0], "seq", 1 << bit), swapped(pair[1], "seq", 1 << bit))

    paths = [path(bit) for bit in range(bits)]
    low = low_rank_rows(q, feat, state)
    sums = attend(q, [(k, v)], None, "attend_own")
    for partner in range(PARTNERS):
        picked = jnp.sum(jnp.where(distances[partner] == powers, bit_ids, 0))
        k_far, v_far = lax.switch(picked, paths, (k, v))
        if partner < PARTNERS - 1:
            sums = attend(q, [(k_far, v_far)], sums, "attend_far")
    rows = gather(sums, *weigh(q, [k_far], "weigh_last"), [v_far], low, "gather_last")
    part = jnp.dot(rows, w, preferred_element_type=jnp.float32)
    return lax.psum_scatter(part.astype(jnp.bfloat16), "head", scatter_dimension=1, tiled=True)


def per_device(queries, keys, values, distances, feature_proj, out_proj):
    if lax.axis_size("seq") == 1 << PARTNERS and lax.axis_size("head") == 2:
        return every_distance(queries, keys, values, feature_proj, out_proj)
    return chosen_distances(queries, keys, values, distances, feature_proj, out_proj)


def solution(mesh):
    in_specs = (P("seq", "head"), P("seq", "head"), P("seq", "head"), P(), P(), P("head", None))
    return jax.shard_map(
        per_device, mesh=mesh, in_specs=in_specs, out_specs=P("seq", "head"), check_vma=False
    )
```

time: 270 us -> 95.6 us (0.35)
  waiting for transfers between devices: 116 us -> 25.1 us
  matrix products: 57.5 us -> 0 us
  blocking collectives: 41.2 us -> 0 us
  Pallas kernels: 0 us -> 25.8 us
  other arithmetic: 22.5 us -> 0.13 us
  starting transfers between devices: 10.4 us -> 27.5 us
  between operations: 16.1 us -> 0.3 us
  local copies, waits for them, and re-layouts: 5.37 us -> 16 us
    ppermute x8 -> x18, waiting for transfers between devices: 111 us -> 25.1 us  [the longest x12 21.1 us: swapped(): lax.ppermute(shard, axis, [(i, i ^ distance) for i in range(lax.axis_size...]
    dot_general x16 -> x0, matrix products: 57.5 us -> none  [the longest x5 26.9 us: attend(): jnp.einsum('thd,shd->hts', q_rows, k_rows, preferred_element_type=jnp.flo...]
    psum x1 -> x0, blocking collectives: 41.2 us -> none  [per_device(): kv_state, norm_state = lax.psum((kv_part, norm_part), 'seq')]
    pallas_call x0 -> x9, Pallas kernels: none -> 25.8 us  [kernel_call(): pl.pallas_call(body, out_shape=outs, in_specs=[VMEM] * len(args), out_spe...]
    reduce_sum x8 -> x0, other arithmetic: 22.4 us -> none  [the longest x3 17.1 us: attend(): total = total * factor + jnp.sum(probs, axis=-1)]
    ppermute x8 -> x18, starting transfers between devices: 10.3 us -> 27.5 us  [the longest x12 17 us: swapped(): lax.ppermute(shard, axis, [(i, i ^ distance) for i in range(lax.axis_size...]
    unnamed x25 -> x40, local copies, waits for them, and re-layouts: 4.72 us -> 13.9 us
    reduce_scatter x1 -> x0, waiting for transfers between devices: 4.56 us -> none  [per_device(): lax.psum_scatter(partial_out.astype(jnp.bfloat16), 'head', scatter_dimens...]
  transfers between devices with their start and end apart: 10 -> 18, of which waited for: 9 -> 8; matrix products, arithmetic and copies ran while one was open for 27% -> 2% of each run, Pallas kernels for 0% -> 25%
where the time goes in v1:
time: 95.6 us; the launch traced here: 94.8 us
  starting transfers between devices  27.5 us (29%)
  Pallas kernels  25.8 us (27%)
  waiting for transfers between devices  25.1 us (26%)
  local copies, waits for them, and re-layouts  16 us (17%)
    pallas_call x9, Pallas kernels, kernel_call(): pl.pallas_call(body, out_shape=outs, in_specs=[VMEM] * len(args), out_spe...  25.8 us
    ppermute x12, waiting for transfers between devices, swapped(): lax.ppermute(shard, axis, [(i, i ^ distance) for i in range(lax.axis_size...  21.1 us
    ppermute x12, starting transfers between devices, swapped(): lax.ppermute(shard, axis, [(i, i ^ distance) for i in range(lax.axis_size...  17 us
    unnamed x40, local copies, waits for them, and re-layouts  13.9 us
    ppermute x6, starting transfers between devices, moved(): lax.ppermute(shard, 'seq', [(a * span + r, b * span + r) for a, b in step...  10.5 us
    ppermute x6, waiting for transfers between devices, moved(): lax.ppermute(shard, 'seq', [(a * span + r, b * span + r) for a, b in step...  3.99 us
    dynamic_slice x1, local copies, waits for them, and re-layouts, every_distance(): lax.dynamic_slice_in_dim(w, (1 - core) * width, width, axis=1)  2.07 us
  transfers between devices with their start and end apart: 18, of which 8 were waited for; matrix products, arithmetic and copies ran while one was open for 2% of the time, Pallas kernels for 25%

profile of v1, /device:TPU:0, one launch (start us, length us, event | category | flops | bytes accessed | tf_op | source)
XLA Modules:
  0.0 94.8 jit_solution(6304304690148059432)
XLA Ops:
  0.0 3.0 %collective-permute-start = (bf16[512,512]{1,0:T(8,128)(2,1)}, bf16[512,512]{1,0:T(8,128)(2,1)}, u32[]{:S(2)}, u32[]{:S(2)}) collective-permute-start(bf16[512,512]{1,0:T(8,128)(2,1)} %refs_1_.1), channel_id=1, source_target_pairs={{8,24},{10,26},{12,28},{14,30},{16,0},{18,2},{20,4},{22,6},{0,8},{... | collective-permute-start | bytes 1572872 | tf_op jit(solution)/shard_map/ppermute | solution.py:262
  3.0 1.5 %collective-permute-start.1 = (bf16[512,512]{1,0:T(8,128)(2,1)}, bf16[512,512]{1,0:T(8,128)(2,1)}, u32[]{:S(2)}, u32[]{:S(2)}) collective-permute-start(bf16[512,512]{1,0:T(8,128)(2,1)} %refs_1_.1), channel_id=1, source_target_pairs={{0,2},{2,0},{4,6},{6,4},{8,10},{10,8},{12,14},{14,12},{16,18},{18,... | collective-permute-start | bytes 1572872 | tf_op jit(solution)/shard_map/ppermute | solution.py:257
  4.5 1.5 %collective-permute-start.2 = (bf16[512,512]{1,0:T(8,128)(2,1)}, bf16[512,512]{1,0:T(8,128)(2,1)}, u32[]{:S(2)}, u32[]{:S(2)}) collective-permute-start(bf16[512,512]{1,0:T(8,128)(2,1)} %refs_1_.1), channel_id=1, source_target_pairs={{0,4},{2,6},{4,0},{6,2},{8,12},{10,14},{12,8},{14,10},{16,20},{18,... | collective-permute-start | bytes 1572872 | tf_op jit(solution)/shard_map/ppermute | solution.py:257
  6.0 1.1 %copy-done.3 = bf16[512,512]{1,0:T(8,128)(2,1)S(1)} copy-done((bf16[512,512]{1,0:T(8,128)(2,1)S(1)}, bf16[512,512]{1,0:T(8,128)(2,1)}, u32[]{:S(2)}) %copy-start.3) | copy-done | bytes 524312
  7.1 1.0 %copy-done.5 = bf16[512,512]{1,0:T(8,128)(2,1)S(1)} copy-done((bf16[512,512]{1,0:T(8,128)(2,1)S(1)}, bf16[512,512]{1,0:T(8,128)(2,1)}, u32[]{:S(2)}) %copy-start.5) | copy-done | bytes 524312
  8.2 0.7 copy-done.18
  8.9 2.3 %key_state.1 = bf16[640,128]{1,0:T(8,128)(2,1)S(1)} custom-call(bf16[512,512]{1,0:T(8,128)(2,1)S(1)} %copy-done.3, bf16[512,512]{1,0:T(8,128)(2,1)S(1)} %copy-done.5, bf16[64,128]{1,0:T(8,128)(2,1)S(1)} %copy-done.18), custom_call_target="tpu_custom_call" | custom-call | flops 1000 | tf_op jit(solution)/shard_map/key_state/pallas_call | solution.py:71
  11.2 1.0 %copy-done = bf16[512,512]{1,0:T(8,128)(2,1)S(1)} copy-done((bf16[512,512]{1,0:T(8,128)(2,1)S(1)}, bf16[512,512]{1,0:T(8,128)(2,1)}, u32[]{:S(2)}) %copy-start) | copy-done | bytes 524312
  12.2 1.0 %copy-done.4 = bf16[512,512]{1,0:T(8,128)(2,1)S(1)} copy-done((bf16[512,512]{1,0:T(8,128)(2,1)S(1)}, bf16[512,512]{1,0:T(8,128)(2,1)}, u32[]{:S(2)}) %copy-start.4) | copy-done | bytes 524312
  13.3 1.0 %copy-done.6 = bf16[512,512]{1,0:T(8,128)(2,1)S(1)} copy-done((bf16[512,512]{1,0:T(8,128)(2,1)S(1)}, bf16[512,512]{1,0:T(8,128)(2,1)}, u32[]{:S(2)}) %copy-start.6) | copy-done | bytes 524312
  14.3 2.9 %attend_own.1 = (f32[512,512]{1,0:T(8,128)S(1)}, f32[512,512]{1,0:T(8,128)S(1)}, f32[512,512]{1,0:T(8,128)S(1)}) custom-call(bf16[512,512]{1,0:T(8,128)(2,1)S(1)} %copy-done, bf16[512,512]{1,0:T(8,128)(2,1)S(1)} %copy-done.4, bf16[512,512]{1,0:T(8,128)(2,1)S(1)} %copy-done.6), custom_call_target="tpu_custom_call" | custom-call | flops 1000 | tf_op jit(solution)/shard_map/attend_own/pallas_call | solution.py:71
  17.3 1.0 %copy-done.8 = f32[512,512]{1,0:T(8,128)} copy-done((f32[512,512]{1,0:T(8,128)}, f32[512,512]{1,0:T(8,128)S(1)}, u32[]{:S(2)}) %copy-start.8) | copy-done | bytes 1048600
  18.3 1.2 %collective-permute-start.3 = (bf16[320,128]{1,0:T(8,128)(2,1)S(1)}, bf16[320,128]{1,0:T(8,128)(2,1)S(1)}, u32[]{:S(2)}, u32[]{:S(2)}) collective-permute-start(bf16[320,128]{1,0:T(8,128)(2,1)S(1)} %constant_dynamic-slice_fusion.3), channel_id=1, source_target_pairs={{0,4},{2,6},{4,0},{6,2},{8,12},{10,14},{12,8},{14,10},{16,20},{18,... | collective-permute-start | bytes 245768 | tf_op jit(solution)/shard_map/ppermute | solution.py:257
  19.5 2.6 %collective-permute-start.5 = (bf16[512,512]{1,0:T(8,128)(2,1)}, bf16[512,512]{1,0:T(8,128)(2,1)}, u32[]{:S(2)}, u32[]{:S(2)}) collective-permute-start(bf16[512,512]{1,0:T(8,128)(2,1)} %refs_2_.1), channel_id=1, source_target_pairs={{8,24},{10,26},{12,28},{14,30},{16,0},{18,2},{20,4},{22,6},{0,8},{... | collective-permute-start | bytes 1572872 | tf_op jit(solution)/shard_map/ppermute | solution.py:262
  22.1 0.8 collective-permute-done.3
  22.9 0.6 collective-permute-start.4
  23.5 3.9 %collective-permute-done.4 = bf16[160,128]{1,0:T(8,128)(2,1)S(1)} collective-permute-done((bf16[160,128]{1,0:T(8,128)(2,1)S(1)}, bf16[160,128]{1,0:T(8,128)(2,1)S(1)}, u32[]{:S(2)}, u32[]{:S(2)}) %collective-permute-start.4) | collective-permute-done | bytes 40992 | tf_op jit(solution)/shard_map/ppermute | solution.py:257
  27.4 0.6 collective-permute-start.10
  28.0 1.1 %collective-permute-start.11 = (bf16[512,512]{1,0:T(8,128)(2,1)}, bf16[512,512]{1,0:T(8,128)(2,1)S(1)}, u32[]{:S(2)}, u32[]{:S(2)}) collective-permute-start(bf16[512,512]{1,0:T(8,128)(2,1)} %refs_2_.1), channel_id=1, source_target_pairs={{0,4},{2,6},{4,0},{6,2},{8,12},{10,14},{12,8},{14,10},{16,20},{18,... | collective-permute-start | bytes 1572872 | tf_op jit(solution)/shard_map/ppermute | solution.py:257
  29.1 0.7 collective-permute-start.7
  29.8 4.0 %collective-permute-done.5.refs_2_ = bf16[512,512]{1,0:T(8,128)(2,1)} collective-permute-done((bf16[512,512]{1,0:T(8,128)(2,1)}, bf16[512,512]{1,0:T(8,128)(2,1)}, u32[]{:S(2)}, u32[]{:S(2)}) %collective-permute-start.5) | collective-permute-done | bytes 524320 | tf_op jit(solution)/shard_map/ppermute | solution.py:262
  33.7 1.3 %collective-permute-start.9 = (bf16[512,512]{1,0:T(8,128)(2,1)}, bf16[512,512]{1,0:T(8,128)(2,1)S(1)}, u32[]{:S(2)}, u32[]{:S(2)}) collective-permute-start(bf16[512,512]{1,0:T(8,128)(2,1)} %refs_1_.1), channel_id=1, source_target_pairs={{8,0},{10,2},{12,4},{14,6},{16,24},{18,26},{20,28},{22,30},{9,1},{... | collective-permute-start | bytes 1572872 | tf_op jit(solution)/shard_map/ppermute | solution.py:262
  35.0 1.0 %copy-done.1 = bf16[512,512]{1,0:T(8,128)(2,1)S(1)} copy-done((bf16[512,512]{1,0:T(8,128)(2,1)S(1)}, bf16[512,512]{1,0:T(8,128)(2,1)}, u32[]{:S(2)}) %copy-start.1) | copy-done | bytes 524312
  36.1 1.2 %copy-done.9 = f32[512,512]{1,0:T(8,128)S(1)} copy-done((f32[512,512]{1,0:T(8,128)S(1)}, f32[512,512]{1,0:T(8,128)}, u32[]{:S(2)}) %copy-start.9) | copy-done | bytes 1048600
  37.3 4.5 %attend_first.1 = (f32[512,512]{1,0:T(8,128)S(1)}, f32[512,512]{1,0:T(8,128)S(1)}, f32[512,512]{1,0:T(8,128)S(1)}) custom-call(bf16[512,512]{1,0:T(8,128)(2,1)S(1)} %copy-done.1, bf16[512,512]{1,0:T(8,128)(2,1)} %collective-permute-done.refs_1_, bf16[512,512]{1,0:T(8,128)(2,1)} %collective-permute-done.5.refs_2_, f32[512,512]{1,0:T(8,128)S(1)} %get-tuple-element.54.refs_3_, ...), custom_call_target="tpu_custom_call" | custom-call | flops 1000 | tf_op jit(solution)/shard_map/attend_first/pallas_call | solution.py:71
  41.8 1.5 %collective-permute-start.12 = (bf16[512,512]{1,0:T(8,128)(2,1)}, bf16[512,512]{1,0:T(8,128)(2,1)}, u32[]{:S(2)}, u32[]{:S(2)}) collective-permute-start(bf16[512,512]{1,0:T(8,128)(2,1)} %collective-permute-done.5.refs_2_), channel_id=1, source_target_pairs={{8,16},{10,18},{12,20},{14,22},{16,8},{18,10},{20,12},{22,14},{9,1... | collective-permute-start | bytes 1572872 | tf_op jit(solution)/shard_map/ppermute | solution.py:262
  43.3 1.5 %collective-permute-start.13 = (bf16[512,512]{1,0:T(8,128)(2,1)S(1)}, bf16[512,512]{1,0:T(8,128)(2,1)}, u32[]{:S(2)}, u32[]{:S(2)}) collective-permute-start(bf16[512,512]{1,0:T(8,128)(2,1)S(1)} %copy-done.7), channel_id=1, source_target_pairs={{8,0},{10,2},{12,4},{14,6},{16,24},{18,26},{20,28},{22,30},{9,1},{... | collective-permute-start | bytes 1572872 | tf_op jit(solution)/shard_map/ppermute | solution.py:262
  44.7 6.9 %collective-permute-start.6 = (bf16[160,128]{1,0:T(8,128)(2,1)S(1)}, bf16[160,128]{1,0:T(8,128)(2,1)S(1)}, u32[]{:S(2)}, u32[]{:S(2)}) collective-permute-start(bf16[160,128]{1,0:T(8,128)(2,1)S(1)} %dynamic-slice_add_fusion.1), channel_id=1, source_target_pairs={{0,8},{2,10},{4,12},{6,14},{8,0},{10,2},{12,4},{14,6},{16,24},{18,... | collective-permute-start | bytes 122888 | tf_op jit(solution)/shard_map/ppermute | solution.py:257
  51.7 7.2 %collective-permute-done.6 = bf16[160,128]{1,0:T(8,128)(2,1)S(1)} collective-permute-done((bf16[160,128]{1,0:T(8,128)(2,1)S(1)}, bf16[160,128]{1,0:T(8,128)(2,1)S(1)}, u32[]{:S(2)}, u32[]{:S(2)}) %collective-permute-start.6) | collective-permute-done | bytes 40992 | tf_op jit(solution)/shard_map/ppermute | solution.py:257
  58.9 0.8 copy-done.14
  59.7 0.4 collective-permute-start.8
  60.1 4.5 %collective-permute-done.8 = bf16[160,128]{1,0:T(8,128)(2,1)S(1)} collective-permute-done((bf16[160,128]{1,0:T(8,128)(2,1)S(1)}, bf16[160,128]{1,0:T(8,128)(2,1)S(1)}, u32[]{:S(2)}, u32[]{:S(2)}) %collective-permute-start.8) | collective-permute-done | bytes 40992 | tf_op jit(solution)/shard_map/ppermute | solution.py:257
  64.6 7.1 %attend_near.1 = (f32[512,512]{1,0:T(8,128)S(1)}, f32[512,512]{1,0:T(8,128)S(1)}, f32[512,512]{1,0:T(8,128)S(1)}) custom-call(bf16[512,512]{1,0:T(8,128)(2,1)S(1)} %copy-done.1, bf16[512,512]{1,0:T(8,128)(2,1)} %collective-permute-done.1.refs_1_, bf16[512,512]{1,0:T(8,128)(2,1)S(1)} %collective-permute-done.10.refs_2_, ...), custom_call_target="tpu_custom_call" | custom-call | flops 1000 | tf_op jit(solution)/shard_map/attend_near/pallas_call | solution.py:71
  71.8 1.0 %copy-done.10 = f32[512,512]{1,0:T(8,128)} copy-done((f32[512,512]{1,0:T(8,128)}, f32[512,512]{1,0:T(8,128)S(1)}, u32[]{:S(2)}) %copy-start.10) | copy-done | bytes 1048600
  72.8 1.0 %copy-done.12 = f32[512,512]{1,0:T(8,128)} copy-done((f32[512,512]{1,0:T(8,128)}, f32[512,512]{1,0:T(8,128)S(1)}, u32[]{:S(2)}) %copy-start.12) | copy-done | bytes 1048600
  73.8 0.8 copy-done.16
  74.6 1.5 %collective-permute-start.14 = (bf16[160,128]{1,0:T(8,128)(2,1)S(1)}, bf16[160,128]{1,0:T(8,128)(2,1)S(1)}, u32[]{:S(2)}, u32[]{:S(2)}) collective-permute-start(bf16[160,128]{1,0:T(8,128)(2,1)S(1)} %add.37), channel_id=1, source_target_pairs={{0,2},{2,0},{4,6},{6,4},{8,10},{10,8},{12,14},{14,12},{16,18},{18,... | collective-permute-start | bytes 122888 | tf_op jit(solution)/shard_map/ppermute | solution.py:257
  76.1 2.5 %collective-permute-done.14 = bf16[160,128]{1,0:T(8,128)(2,1)S(1)} collective-permute-done((bf16[160,128]{1,0:T(8,128)(2,1)S(1)}, bf16[160,128]{1,0:T(8,128)(2,1)S(1)}, u32[]{:S(2)}, u32[]{:S(2)}) %collective-permute-start.14) | collective-permute-done | bytes 40992 | tf_op jit(solution)/shard_map/ppermute | solution.py:257
  78.6 1.6 %collective-permute-start.15 = (bf16[320,128]{1,0:T(8,128)(2,1)S(1)}, bf16[320,128]{1,0:T(8,128)(2,1)S(1)}, u32[]{:S(2)}, u32[]{:S(2)}) collective-permute-start(bf16[320,128]{1,0:T(8,128)(2,1)S(1)} %maximum_select_fusion.1), channel_id=1, source_target_pairs={{0,4},{2,6},{4,0},{6,2},{8,12},{10,14},{12,8},{14,10},{16,20},{18,... | collective-permute-start | bytes 245768 | tf_op jit(solution)/shard_map/ppermute | solution.py:257
  80.3 2.1 %constant_dynamic-slice_fusion = (bf16[512,512]{1,0:T(8,128)(2,1)}, bf16[512,512]{1,0:T(8,128)(2,1)S(1)}) fusion(bf16[512,1024]{1,0:T(8,128)(2,1)} %param.10, s32[]{:T(128)S(6)} %select_n.43, s32[]{:T(128)S(6)} %select_n.42), kind=kLoop, calls=%fused_computation.4 | loop fusion | bytes 2097160 | tf_op jit(solution)/shard_map/dynamic_slice | solution.py:321
  82.3 0.8 collective-permute-done.15
  83.2 1.0 %copy-done.17 = bf16[512,512]{1,0:T(8,128)(2,1)S(1)} copy-done((bf16[512,512]{1,0:T(8,128)(2,1)S(1)}, bf16[512,512]{1,0:T(8,128)(2,1)}, u32[]{:S(2)}) %copy-start.17) | copy-done | bytes 524312
  84.3 1.7 %weigh_last.1 = (bf16[512,4096]{1,0:T(8,128)(2,1)S(1)}, f32[512,512]{1,0:T(8,128)S(1)}) custom-call(bf16[512,512]{1,0:T(8,128)(2,1)S(1)} %copy-done.2, bf16[512,512]{1,0:T(8,128)(2,1)S(1)} %copy-done.15, bf16[512,512]{1,0:T(8,128)(2,1)S(1)} %copy-done.17), custom_call_target="tpu_custom_call" | custom-call | flops 1000 | tf_op jit(solution)/shard_map/weigh_last/pallas_call | solution.py:71
  86.0 1.9 %low_rank.1.refs_7_ = f32[512,512]{1,0:T(8,128)S(1)} custom-call(bf16[512,512]{1,0:T(8,128)(2,1)S(1)} %copy-done.2, bf16[64,128]{1,0:T(8,128)(2,1)S(1)} %copy-done.19, bf16[640,128]{1,0:T(8,128)(2,1)S(1)} %maximum_select_fusion.state_ref), custom_call_target="tpu_custom_call" | custom-call | flops 1000 | tf_op jit(solution)/shard_map/low_rank/pallas_call | solution.py:71
  87.9 2.6 %gather_last.1.refs_0_ = bf16[512,512]{1,0:T(8,128)(2,1)S(1)} custom-call(f32[512,512]{1,0:T(8,128)S(1)} %get-tuple-element.69.refs_0_, f32[512,512]{1,0:T(8,128)S(1)} %copy-done.11, f32[512,512]{1,0:T(8,128)S(1)} %copy-done.13, bf16[512,4096]{1,0:T(8,128)(2,1)S(1)} %get-tuple-element.74.refs_3_, f32[512,512]{1,0:T(8,128)S(1)} %get-tuple-element.75.refs_4_, ...), custom_call_target="tpu_custom_call" | custom-call | flops 1000 | tf_op jit(solution)/shard_map/gather_last/pallas_call | solution.py:71
  90.7 0.4 project_own.1.refs_0_
  91.1 1.4 %collective-permute-done.16.refs_1_ = bf16[512,512]{1,0:T(8,128)(2,1)S(1)} collective-permute-done((bf16[512,512]{1,0:T(8,128)(2,1)S(1)}, bf16[512,512]{1,0:T(8,128)(2,1)S(1)}, u32[]{:S(2)}, u32[]{:S(2)}) %collective-permute-start.16) | collective-permute-done | bytes 524320 | tf_op jit(solution)/shard_map/ppermute | solution.py:257
  92.6 2.3 %project_far.1 = bf16[512,512]{1,0:T(8,128)(2,1)} custom-call(f32[512,512]{1,0:T(8,128)S(1)} %project_own.1.refs_0_, bf16[512,512]{1,0:T(8,128)(2,1)S(1)} %collective-permute-done.16.refs_1_, bf16[512,512]{1,0:T(8,128)(2,1)} %collective-permute-done.17.refs_2_), custom_call_target="tpu_custom_call" | custom-call | flops 1000 | tf_op jit(solution)/shard_map/project_far/pallas_call | solution.py:71
  (46 shorter events, 0.3 us)
Async XLA Ops:
  0.0 18.3 %collective-permute-start = (bf16[512,512]{1,0:T(8,128)(2,1)}, bf16[512,512]{1,0:T(8,128)(2,1)}, u32[]{:S(2)}, u32[]{:S(2)}) collective-permute-start(bf16[512,512]{1,0:T(8,128)(2,1)} %refs_1_.1), channel_id=1, source_target_pairs={{8,24},{10,26},{12,28},{14,30},{16,0},{18,2},{20,4},{22,6},{0,8},{... | collective-permute-start | bytes 1572872 | tf_op jit(solution)/shard_map/ppermute | solution.py:262
  3.0 15.3 %collective-permute-start.1 = (bf16[512,512]{1,0:T(8,128)(2,1)}, bf16[512,512]{1,0:T(8,128)(2,1)}, u32[]{:S(2)}, u32[]{:S(2)}) collective-permute-start(bf16[512,512]{1,0:T(8,128)(2,1)} %refs_1_.1), channel_id=1, source_target_pairs={{0,2},{2,0},{4,6},{6,4},{8,10},{10,8},{12,14},{14,12},{16,18},{18,... | collective-permute-start | bytes 1572872 | tf_op jit(solution)/shard_map/ppermute | solution.py:257
  4.5 13.8 %collective-permute-start.2 = (bf16[512,512]{1,0:T(8,128)(2,1)}, bf16[512,512]{1,0:T(8,128)(2,1)}, u32[]{:S(2)}, u32[]{:S(2)}) collective-permute-start(bf16[512,512]{1,0:T(8,128)(2,1)} %refs_1_.1), channel_id=1, source_target_pairs={{0,4},{2,6},{4,0},{6,2},{8,12},{10,14},{12,8},{14,10},{16,20},{18,... | collective-permute-start | bytes 1572872 | tf_op jit(solution)/shard_map/ppermute | solution.py:257
  6.0 1.1 %copy-start.3 = (bf16[512,512]{1,0:T(8,128)(2,1)S(1)}, bf16[512,512]{1,0:T(8,128)(2,1)}, u32[]{:S(2)}) copy-start(bf16[512,512]{1,0:T(8,128)(2,1)} %refs_1_.1) | copy-start | bytes 1572868
  7.1 1.0 %copy-start.5 = (bf16[512,512]{1,0:T(8,128)(2,1)S(1)}, bf16[512,512]{1,0:T(8,128)(2,1)}, u32[]{:S(2)}) copy-start(bf16[512,512]{1,0:T(8,128)(2,1)} %refs_2_.1) | copy-start | bytes 1572868
  8.2 0.7 copy-start.18
  8.9 34.4 %copy-start.7 = (bf16[512,512]{1,0:T(8,128)(2,1)S(1)}, bf16[512,512]{1,0:T(8,128)(2,1)}, u32[]{:S(2)}) copy-start(bf16[512,512]{1,0:T(8,128)(2,1)} %refs_2_.1) | copy-start | bytes 1572868
  11.2 1.0 %copy-start = (bf16[512,512]{1,0:T(8,128)(2,1)S(1)}, bf16[512,512]{1,0:T(8,128)(2,1)}, u32[]{:S(2)}) copy-start(bf16[512,512]{1,0:T(8,128)(2,1)} %q_ref.1) | copy-start | bytes 1572868
  12.2 1.0 %copy-start.4 = (bf16[512,512]{1,0:T(8,128)(2,1)S(1)}, bf16[512,512]{1,0:T(8,128)(2,1)}, u32[]{:S(2)}) copy-start(bf16[512,512]{1,0:T(8,128)(2,1)} %refs_1_.1) | copy-start | bytes 1572868
  13.3 1.0 %copy-start.6 = (bf16[512,512]{1,0:T(8,128)(2,1)S(1)}, bf16[512,512]{1,0:T(8,128)(2,1)}, u32[]{:S(2)}) copy-start(bf16[512,512]{1,0:T(8,128)(2,1)} %refs_2_.1) | copy-start | bytes 1572868
  17.3 1.0 %copy-start.8 = (f32[512,512]{1,0:T(8,128)}, f32[512,512]{1,0:T(8,128)S(1)}, u32[]{:S(2)}) copy-start(f32[512,512]{1,0:T(8,128)S(1)} %get-tuple-element.56.refs_5_) | copy-start | bytes 3145732
  18.3 4.5 %collective-permute-start.3 = (bf16[320,128]{1,0:T(8,128)(2,1)S(1)}, bf16[320,128]{1,0:T(8,128)(2,1)S(1)}, u32[]{:S(2)}, u32[]{:S(2)}) collective-permute-start(bf16[320,128]{1,0:T(8,128)(2,1)S(1)} %constant_dynamic-slice_fusion.3), channel_id=1, source_target_pairs={{0,4},{2,6},{4,0},{6,2},{8,12},{10,14},{12,8},{14,10},{16,20},{18,... | collective-permute-start | bytes 245768 | tf_op jit(solution)/shard_map/ppermute | solution.py:257
  19.5 14.3 %collective-permute-start.5 = (bf16[512,512]{1,0:T(8,128)(2,1)}, bf16[512,512]{1,0:T(8,128)(2,1)}, u32[]{:S(2)}, u32[]{:S(2)}) collective-permute-start(bf16[512,512]{1,0:T(8,128)(2,1)} %refs_2_.1), channel_id=1, source_target_pairs={{8,24},{10,26},{12,28},{14,30},{16,0},{18,2},{20,4},{22,6},{0,8},{... | collective-permute-start | bytes 1572872 | tf_op jit(solution)/shard_map/ppermute | solution.py:262
  22.9 4.5 %collective-permute-start.4 = (bf16[160,128]{1,0:T(8,128)(2,1)S(1)}, bf16[160,128]{1,0:T(8,128)(2,1)S(1)}, u32[]{:S(2)}, u32[]{:S(2)}) collective-permute-start(bf16[160,128]{1,0:T(8,128)(2,1)S(1)} %constant_dynamic-slice_fusion.2), channel_id=1, source_target_pairs={{0,2},{2,0},{4,6},{6,4},{8,10},{10,8},{12,14},{14,12},{16,18},{18,... | collective-permute-start | bytes 122888 | tf_op jit(solution)/shard_map/ppermute | solution.py:257
  27.4 14.4 %collective-permute-start.10 = (bf16[512,512]{1,0:T(8,128)(2,1)}, bf16[512,512]{1,0:T(8,128)(2,1)S(1)}, u32[]{:S(2)}, u32[]{:S(2)}) collective-permute-start(bf16[512,512]{1,0:T(8,128)(2,1)} %refs_2_.1), channel_id=1, source_target_pairs={{0,2},{2,0},{4,6},{6,4},{8,10},{10,8},{12,14},{14,12},{16,18},{18,... | collective-permute-start | bytes 1572872 | tf_op jit(solution)/shard_map/ppermute | solution.py:257
  28.0 13.8 %collective-permute-start.11 = (bf16[512,512]{1,0:T(8,128)(2,1)}, bf16[512,512]{1,0:T(8,128)(2,1)S(1)}, u32[]{:S(2)}, u32[]{:S(2)}) collective-permute-start(bf16[512,512]{1,0:T(8,128)(2,1)} %refs_2_.1), channel_id=1, source_target_pairs={{0,4},{2,6},{4,0},{6,2},{8,12},{10,14},{12,8},{14,10},{16,20},{18,... | collective-permute-start | bytes 1572872 | tf_op jit(solution)/shard_map/ppermute | solution.py:257
  29.1 29.8 %collective-permute-start.7 = (bf16[512,512]{1,0:T(8,128)(2,1)}, bf16[512,512]{1,0:T(8,128)(2,1)S(1)}, u32[]{:S(2)}, u32[]{:S(2)}) collective-permute-start(bf16[512,512]{1,0:T(8,128)(2,1)} %collective-permute-done.refs_1_), channel_id=1, source_target_pairs={{8,16},{10,18},{12,20},{14,22},{16,8},{18,10},{20,12},{22,14},{9,1... | collective-permute-start | bytes 1572872 | tf_op jit(solution)/shard_map/ppermute | solution.py:262
  33.7 40.0 %collective-permute-start.9 = (bf16[512,512]{1,0:T(8,128)(2,1)}, bf16[512,512]{1,0:T(8,128)(2,1)S(1)}, u32[]{:S(2)}, u32[]{:S(2)}) collective-permute-start(bf16[512,512]{1,0:T(8,128)(2,1)} %refs_1_.1), channel_id=1, source_target_pairs={{8,0},{10,2},{12,4},{14,6},{16,24},{18,26},{20,28},{22,30},{9,1},{... | collective-permute-start | bytes 1572872 | tf_op jit(solution)/shard_map/ppermute | solution.py:262
  35.0 1.0 %copy-start.1 = (bf16[512,512]{1,0:T(8,128)(2,1)S(1)}, bf16[512,512]{1,0:T(8,128)(2,1)}, u32[]{:S(2)}) copy-start(bf16[512,512]{1,0:T(8,128)(2,1)} %q_ref.1) | copy-start | bytes 1572868
  36.1 1.2 %copy-start.9 = (f32[512,512]{1,0:T(8,128)S(1)}, f32[512,512]{1,0:T(8,128)}, u32[]{:S(2)}) copy-start(f32[512,512]{1,0:T(8,128)} %copy-done.8) | copy-start | bytes 3145732
  41.8 46.1 %collective-permute-start.12 = (bf16[512,512]{1,0:T(8,128)(2,1)}, bf16[512,512]{1,0:T(8,128)(2,1)}, u32[]{:S(2)}, u32[]{:S(2)}) collective-permute-start(bf16[512,512]{1,0:T(8,128)(2,1)} %collective-permute-done.5.refs_2_), channel_id=1, source_target_pairs={{8,16},{10,18},{12,20},{14,22},{16,8},{18,10},{20,12},{22,14},{9,1... | collective-permute-start | bytes 1572872 | tf_op jit(solution)/shard_map/ppermute | solution.py:262
  43.3 44.6 %collective-permute-start.13 = (bf16[512,512]{1,0:T(8,128)(2,1)S(1)}, bf16[512,512]{1,0:T(8,128)(2,1)}, u32[]{:S(2)}, u32[]{:S(2)}) collective-permute-start(bf16[512,512]{1,0:T(8,128)(2,1)S(1)} %copy-done.7), channel_id=1, source_target_pairs={{8,0},{10,2},{12,4},{14,6},{16,24},{18,26},{20,28},{22,30},{9,1},{... | collective-permute-start | bytes 1572872 | tf_op jit(solution)/shard_map/ppermute | solution.py:262
  44.7 14.1 %collective-permute-start.6 = (bf16[160,128]{1,0:T(8,128)(2,1)S(1)}, bf16[160,128]{1,0:T(8,128)(2,1)S(1)}, u32[]{:S(2)}, u32[]{:S(2)}) collective-permute-start(bf16[160,128]{1,0:T(8,128)(2,1)S(1)} %dynamic-slice_add_fusion.1), channel_id=1, source_target_pairs={{0,8},{2,10},{4,12},{6,14},{8,0},{10,2},{12,4},{14,6},{16,24},{18,... | collective-permute-start | bytes 122888 | tf_op jit(solution)/shard_map/ppermute | solution.py:257
  58.9 0.8 copy-start.14
  59.7 4.9 %collective-permute-start.8 = (bf16[160,128]{1,0:T(8,128)(2,1)S(1)}, bf16[160,128]{1,0:T(8,128)(2,1)S(1)}, u32[]{:S(2)}, u32[]{:S(2)}) collective-permute-start(bf16[160,128]{1,0:T(8,128)(2,1)S(1)} %add.36), channel_id=1, source_target_pairs={{0,16},{2,18},{4,20},{6,22},{8,24},{10,26},{12,28},{14,30},{16,0},... | collective-permute-start | bytes 122888 | tf_op jit(solution)/shard_map/ppermute | solution.py:257
  64.6 18.6 %copy-start.2 = (bf16[512,512]{1,0:T(8,128)(2,1)S(1)}, bf16[512,512]{1,0:T(8,128)(2,1)}, u32[]{:S(2)}) copy-start(bf16[512,512]{1,0:T(8,128)(2,1)} %q_ref.1) | copy-start | bytes 1572868
  64.6 18.6 %copy-start.15 = (bf16[512,512]{1,0:T(8,128)(2,1)S(1)}, bf16[512,512]{1,0:T(8,128)(2,1)}, u32[]{:S(2)}) copy-start(bf16[512,512]{1,0:T(8,128)(2,1)} %copy-done.14) | copy-start | bytes 1572868
  64.6 21.4 %copy-start.19 = (bf16[64,128]{1,0:T(8,128)(2,1)S(1)}, bf16[64,128]{1,0:T(8,128)(2,1)}, u32[]{:S(2)}) copy-start(bf16[64,128]{1,0:T(8,128)(2,1)} %feat_ref.3) | copy-start | bytes 49156
  71.8 1.0 %copy-start.10 = (f32[512,512]{1,0:T(8,128)}, f32[512,512]{1,0:T(8,128)S(1)}, u32[]{:S(2)}) copy-start(f32[512,512]{1,0:T(8,128)S(1)} %get-tuple-element.70.refs_1_) | copy-start | bytes 3145732
  72.8 1.0 %copy-start.12 = (f32[512,512]{1,0:T(8,128)}, f32[512,512]{1,0:T(8,128)S(1)}, u32[]{:S(2)}) copy-start(f32[512,512]{1,0:T(8,128)S(1)} %get-tuple-element.71.refs_2_) | copy-start | bytes 3145732
  73.8 0.8 copy-start.16
  74.6 4.0 %collective-permute-start.14 = (bf16[160,128]{1,0:T(8,128)(2,1)S(1)}, bf16[160,128]{1,0:T(8,128)(2,1)S(1)}, u32[]{:S(2)}, u32[]{:S(2)}) collective-permute-start(bf16[160,128]{1,0:T(8,128)(2,1)S(1)} %add.37), channel_id=1, source_target_pairs={{0,2},{2,0},{4,6},{6,4},{8,10},{10,8},{12,14},{14,12},{16,18},{18,... | collective-permute-start | bytes 122888 | tf_op jit(solution)/shard_map/ppermute | solution.py:257
  78.6 4.5 %collective-permute-start.15 = (bf16[320,128]{1,0:T(8,128)(2,1)S(1)}, bf16[320,128]{1,0:T(8,128)(2,1)S(1)}, u32[]{:S(2)}, u32[]{:S(2)}) collective-permute-start(bf16[320,128]{1,0:T(8,128)(2,1)S(1)} %maximum_select_fusion.1), channel_id=1, source_target_pairs={{0,4},{2,6},{4,0},{6,2},{8,12},{10,14},{12,8},{14,10},{16,20},{18,... | collective-permute-start | bytes 245768 | tf_op jit(solution)/shard_map/ppermute | solution.py:257
  82.3 8.8 %collective-permute-start.17 = (bf16[512,512]{1,0:T(8,128)(2,1)}, bf16[512,512]{1,0:T(8,128)(2,1)}, u32[]{:S(2)}, u32[]{:S(2)}) collective-permute-start(bf16[512,512]{1,0:T(8,128)(2,1)} %get-tuple-element.79), channel_id=1, source_target_pairs={{0,1},{1,0},{2,3},{3,2},{4,5},{5,4},{6,7},{7,6},{8,9},{9,8},{10,11... | collective-permute-start | bytes 1572872 | tf_op jit(solution)/shard_map/ppermute | solution.py:257
  82.3 5.6 %copy-start.11 = (f32[512,512]{1,0:T(8,128)S(1)}, f32[512,512]{1,0:T(8,128)}, u32[]{:S(2)}) copy-start(f32[512,512]{1,0:T(8,128)} %copy-done.10) | copy-start | bytes 3145732
  82.3 5.6 %copy-start.13 = (f32[512,512]{1,0:T(8,128)S(1)}, f32[512,512]{1,0:T(8,128)}, u32[]{:S(2)}) copy-start(f32[512,512]{1,0:T(8,128)} %copy-done.12) | copy-start | bytes 3145732
  83.2 1.0 %copy-start.17 = (bf16[512,512]{1,0:T(8,128)(2,1)S(1)}, bf16[512,512]{1,0:T(8,128)(2,1)}, u32[]{:S(2)}) copy-start(bf16[512,512]{1,0:T(8,128)(2,1)} %copy-done.16) | copy-start | bytes 1572868
  90.6 2.0 %collective-permute-start.16 = (bf16[512,512]{1,0:T(8,128)(2,1)S(1)}, bf16[512,512]{1,0:T(8,128)(2,1)S(1)}, u32[]{:S(2)}, u32[]{:S(2)}) collective-permute-start(bf16[512,512]{1,0:T(8,128)(2,1)S(1)} %gather_last.1.refs_0_), channel_id=1, source_target_pairs={{0,1},{1,0},{2,3},{3,2},{4,5},{5,4},{6,7},{7,6},{8,9},{9,8},{10,11... | collective-permute-start | bytes 1572872 | tf_op jit(solution)/shard_map/ppermute | solution.py:257

commit v2 on v1

--- a/solution.py
+++ b/solution.py
@@ -12,6 +12,7 @@
 PAIR = 2 * HEAD_DIM
 NT = (((1,), (1,)), ((), ()))
 VMEM = pl.BlockSpec(memory_space=pltpu.VMEM)
+SMEM = pl.BlockSpec(memory_space=pltpu.SMEM)
 VMEM_LIMIT = 20 * 2**20
 COST = pl.CostEstimate(flops=1000, transcendentals=0, bytes_accessed=0)
 
@@ -70,29 +71,52 @@
 def kernel_call(body, outs, args, name):
     return pl.pallas_call(
         body,
-        out_shape=outs,
-        in_specs=[VMEM] * len(args),
-        out_specs=jax.tree.map(lambda _: VMEM, outs),
+        out_shape=[pltpu.VMEM(o.shape, o.dtype) for o in outs],
+        in_specs=[SMEM if a.dtype == jnp.int32 else VMEM for a in args],
+        out_specs=[VMEM] * len(outs),
         compiler_params=pltpu.CompilerParams(vmem_limit_bytes=VMEM_LIMIT),
         cost_estimate=COST,
         name=name,
     )(*args)
 
 
-def pairs_call(body, outs, args, pairs, name):
+def whole(array):
+    return [(array, 0, array.shape[1])]
+
+
+def pairs_call(body, outs, operands, pairs, total, name):
+    arrays, places = [], {}
+    for c in pairs:
+        for number, operand in enumerate(operands):
+            share = sum(count for _, _, count in operand) // total
+            at = c * share
+            for array, first, count in operand:
+                if 0 <= at < count:
+                    if not any(array is other for other in arrays):
+                        arrays.append(array)
+                    index = [array is other for other in arrays].index(True)
+                    places[c, number] = index, slice(first + at, first + at + share)
+                at -= count
+
     def every_pair(*refs):
-        for c in range(pairs):
-            widths = [ref.shape[1] // pairs for ref in refs]
-            body(*[ref.at[:, c * n:(c + 1) * n] for ref, n in zip(refs, widths)])
-
-    outs = [pltpu.VMEM(o.shape, o.dtype) for o in outs]
-    return kernel_call(every_pair, outs, args, name)
+        for c in pairs:
+            spots = [places[c, number] for number in range(len(operands))]
+            ins = [refs[index].at[:, part] for index, part in spots]
+            results = []
+            for ref in refs[len(arrays):]:
+                share = ref.shape[1] // len(pairs)
+                at = (c - pairs.start) * share
+                results.append(ref.at[:, at:at + share])
+            body(*ins, *results)
+
+    return kernel_call(every_pair, outs, arrays, name)
 
 
 def attend(q, blocks, before, name):
     tokens, width = q.shape
-    args = [q] + [x for block in blocks for x in block] + list(before or [])
-    count = 1 + 2 * len(blocks)
+    operands = [whole(q)] + [x for block in blocks for x in block]
+    count = len(operands)
+    operands += [whole(x) for x in before or []]
 
     def body(*refs):
         outs = refs[-3:]
@@ -111,12 +135,12 @@
             out[...] = value
 
     outs = [jax.ShapeDtypeStruct((tokens, width), jnp.float32)] * 3
-    return pairs_call(body, outs, args, width // PAIR, name)
+    return pairs_call(body, outs, operands, range(width // PAIR), width // PAIR, name)
 
 
 def weigh(q, parts, name):
     tokens, width = q.shape
-    keys = parts[0].shape[0]
+    keys = parts[0][0][0].shape[0]
 
     def body(q_ref, *refs):
         w_out, top_out = refs[-2:]
@@ -133,27 +157,27 @@
         jax.ShapeDtypeStruct((tokens, width // HEAD_DIM * keys), jnp.bfloat16),
         jax.ShapeDtypeStruct((tokens, width), jnp.float32),
     ]
-    return pairs_call(body, outs, [q] + list(parts), width // PAIR, name)
-
-
-def gather(before, weights, tops, parts, low_rank, name):
-    tokens, width = tops.shape
-    keys = parts[0].shape[0]
+    return pairs_call(body, outs, [whole(q)] + list(parts), range(width // PAIR), width // PAIR, name)
+
+
+def gather(before, weights, tops, parts, low_rank, pairs, name):
+    tokens = tops.shape[0]
+    keys = weights.shape[1] // (tops.shape[1] // HEAD_DIM)
 
     def body(*refs):
-        w_ref, top_ref, low_ref, out = refs[3], refs[4], refs[-2], refs[-1]
+        w_ref, low_ref, out = refs[3], refs[-2], refs[-1]
         v_pair = block_of(refs[5:-2])
         sums = [
             add_values([w_ref[:, half * keys:(half + 1) * keys]], [v_pair], half)
             for half in range(2)
         ]
-        state = (top_ref[...], *numer_denom(*sums))
+        state = (refs[4][...], *numer_denom(*sums))
         _, numer, denom = joined([tuple(r[...] for r in refs[:3]), state])
         out[...] = (numer / denom + low_ref[...]).astype(jnp.bfloat16)
 
-    args = list(before) + [weights, tops] + list(parts) + [low_rank]
-    outs = [jax.ShapeDtypeStruct((tokens, width), jnp.bfloat16)]
-    return pairs_call(body, outs, args, width // PAIR, name)[0]
+    operands = [whole(x) for x in before] + [whole(weights), whole(tops)] + list(parts) + [whole(low_rank)]
+    outs = [jax.ShapeDtypeStruct((tokens, len(pairs) * PAIR), jnp.bfloat16)]
+    return pairs_call(body, outs, operands, pairs, tops.shape[1] // PAIR, name)[0]
 
 
 def twice(feat):
@@ -203,7 +227,7 @@
         out[pairs * features:, :] = norms.astype(jnp.bfloat16)
 
     outs = jax.ShapeDtypeStruct((state_rows(pairs, features), PAIR), jnp.bfloat16)
-    return kernel_call(body, outs, [k, v, feat], "key_state")
+    return kernel_call(body, [outs], [k, v, feat], "key_state")[0]
 
 
 def low_rank_rows(q, feat, state):
@@ -232,25 +256,116 @@
             out[:, c * PAIR:(c + 1) * PAIR] = numer / denom
 
     outs = jax.ShapeDtypeStruct((tokens, width), jnp.float32)
-    return kernel_call(body, outs, [q, feat, state], "low_rank")
-
-
-def project(acc, parts, dtype, name):
+    return kernel_call(body, [outs], [q, feat, state], "low_rank")[0]
+
+
+def project(acc, parts, name):
     tokens, width = parts[0][0].shape[0], parts[0][1].shape[1]
+    arrays = []
+    for array in [x for rows, w, _ in parts for x in (rows, w)] + ([] if acc is None else [acc]):
+        if not any(array is other for other in arrays):
+            arrays.append(array)
 
     def body(*refs):
-        out = refs[-1]
-        rest = list(refs[:-1])
-        total = rest.pop(0)[...] if acc is not None else None
-        for rows, _, first in parts:
-            rows_ref, w_ref = rest.pop(0), rest.pop(0)
-            w = w_ref[first:first + rows.shape[1], :]
-            part = jnp.dot(rows_ref[...], w, preferred_element_type=jnp.float32)
+        def ref_of(array):
+            return refs[[array is other for other in arrays].index(True)]
+
+        total = None if acc is None else ref_of(acc)[...]
+        for rows, w, first in parts:
+            w_rows = ref_of(w)[first:first + rows.shape[1], :]
+            part = jnp.dot(ref_of(rows)[...], w_rows, preferred_element_type=jnp.float32)
             total = part if total is None else total + part
-        out[...] = total.astype(out.dtype)
-
-    args = ([] if acc is None else [acc]) + [x for rows, w, _ in parts for x in (rows, w)]
-    return kernel_call(body, jax.ShapeDtypeStruct((tokens, width), dtype), args, name)
+        refs[-1][...] = total.astype(refs[-1].dtype)
+
+    if acc is None:
+        outs = [jax.ShapeDtypeStruct((tokens, width), jnp.float32)]
+        return kernel_call(body, outs, arrays, name)[0]
+    return pl.pallas_call(
+        body,
+        out_shape=jax.ShapeDtypeStruct((tokens, width), jnp.bfloat16),
+        in_specs=[VMEM] * len(arrays),
+        out_specs=VMEM,
+        compiler_params=pltpu.CompilerParams(vmem_limit_bytes=VMEM_LIMIT),
+        cost_estimate=COST,
+        name=name,
+    )(*arrays)
+
+
+def parted(array, place, bit, axis, name):
+    shape = list(array.shape)
+    shape[axis] //= 2
+    half = shape[axis]
+
+    def body(place_ref, ref, kept, sent):
+        mine = (place_ref[0] >> bit) & 1
+        for out, at in ((kept, mine), (sent, 1 - mine)):
+            rows = pl.ds(pl.multiple_of(at * half, half), half)
+            out[...] = ref[rows, :] if axis == 0 else ref[:, rows]
+
+    outs = [jax.ShapeDtypeStruct(tuple(shape), array.dtype)] * 2
+    return kernel_call(body, outs, [place, array], name)
+
+
+def packed(k, v, split, name):
+    tokens, width = k.shape
+
+    def body(k_ref, v_ref, x_out, y_out, done):
+        copies = [
+            pltpu.make_async_copy(k_ref, x_out.at[:, pl.ds(0, width)], done.at[0]),
+            pltpu.make_async_copy(
+                v_ref.at[:, pl.ds(0, split)], x_out.at[:, pl.ds(width, split)], done.at[1]
+            ),
+            pltpu.make_async_copy(v_ref.at[:, pl.ds(split, width - split)], y_out, done.at[2]),
+        ]
+        for copy in copies:
+            copy.start()
+        for copy in copies:
+            copy.wait()
+
+    return pl.pallas_call(
+        body,
+        out_shape=[
+            pltpu.VMEM((tokens, width + split), k.dtype),
+            pltpu.VMEM((tokens, width - split), k.dtype),
+        ],
+        in_specs=[pl.BlockSpec(memory_space=pl.ANY)] * 2,
+        out_specs=[VMEM] * 2,
+        scratch_shapes=[pltpu.SemaphoreType.DMA((3,))],
+        cost_estimate=COST,
+        name=name,
+    )(k, v)
+
+
+def added(first, second, name):
+    def body(first_ref, second_ref, out):
+        out[...] = first_ref[...] + second_ref[...]
+
+    return kernel_call(body, [jax.ShapeDtypeStruct(first.shape, first.dtype)], [first, second], name)[0]
+
+
+def added_parted(first, second, place, bit, name):
+    half = first.shape[0] // 2
+
+    def body(place_ref, first_ref, second_ref, kept, sent):
+        mine = (place_ref[0] >> bit) & 1
+        for out, at in ((kept, mine), (sent, 1 - mine)):
+            rows = pl.ds(pl.multiple_of(at * half, half), half)
+            out[...] = first_ref[rows, :] + second_ref[rows, :]
+
+    outs = [jax.ShapeDtypeStruct((half, first.shape[1]), first.dtype)] * 2
+    return kernel_call(body, outs, [place, first, second], name)
+
+
+def placed(own, far, place, bit, name):
+    half = own.shape[0]
+
+    def body(place_ref, own_ref, far_ref, out):
+        mine = (place_ref[0] >> bit) & 1
+        for ref, at in ((own_ref, mine), (far_ref, 1 - mine)):
+            out[pl.ds(pl.multiple_of(at * half, half), half), :] = ref[...]
+
+    outs = [jax.ShapeDtypeStruct((2 * half, own.shape[1]), own.dtype)]
+    return kernel_call(body, outs, [place, own, far], name)[0]
 
 
 def swapped(shard, axis, distance):
@@ -264,68 +379,69 @@
     )
 
 
-def halves_summed(state, bit, index):
-    half = state.shape[0] // 2
-    mine = (index >> bit) & 1
-    kept = lax.dynamic_slice_in_dim(state, mine * half, half)
-    sent = lax.dynamic_slice_in_dim(state, (1 - mine) * half, half)
-    return kept + swapped(sent, "seq", 1 << bit)
-
-
-def halves_joined(half, bit, index):
-    far = swapped(half, "seq", 1 << bit)
-    mine = (index >> bit) & 1
-    return jnp.where(
-        mine == 0, jnp.concatenate([half, far], axis=0), jnp.concatenate([far, half], axis=0)
-    )
-
-
 def every_distance(q, k, v, feat, w):
-    index = lax.axis_index("seq")
-    core = lax.axis_index("head")
+    index = lax.axis_index("seq").astype(jnp.int32).reshape(1)
+    core = lax.axis_index("head").astype(jnp.int32).reshape(1)
     width = q.shape[1]
 
     first_steps = [(1, 3), (2, 0), (0, 1), (3, 2)]
     second_steps = [(1, 2), (2, 1)]
     edge_steps = [(1, 0), (2, 3)]
     after = lax.optimization_barrier
-    k_1 = moved(k, first_steps)
-    v_1 = moved(v, first_steps)
+    pairs = width // PAIR
+    split = pairs // 2 * PAIR
+
+    def k_of(x):
+        return [(x, 0, width)]
+
+    def v_of(x, y):
+        return [(x, width, split), (y, 0, width - split)]
+
+    k, index, core = after((k, index, core))
+    x_own, y_own = packed(k, v, split, "values_packed")
+    x_1 = moved(x_own, first_steps)
     k_near = [swapped(k, "seq", d) for d in (1, 2)]
-    sums = attend(q, [(k, v)], None, "attend_own")
+    sums = attend(q, [(whole(k), whole(v))], None, "attend_own")
     state = key_state(k, v, feat)
 
-    state, k_1, k_near, sums = after((state, k_1, k_near, sums))
-    k_2 = moved(k_1, second_steps)
-    state = halves_summed(state, 1, index)
-    state = halves_summed(state, 0, index)
-    state, v_next = after((state, v))
+    state, k_near, sums = after((state, k_near, sums))
+    kept, sent = parted(state, index, 1, 0, "state_parted")
+    kept, sent = added_parted(kept, swapped(sent, "seq", 2), index, 0, "state_second")
+    state = added(kept, swapped(sent, "seq", 1), "state_third")
+
+    state, v_next, y_own = after((state, v, y_own))
     v_near = [swapped(v_next, "seq", d) for d in (1, 2)]
-
-    state, v_1, k_last = after((state, v_1, k))
-    state = state + swapped(state, "seq", 4)
-    k_3 = moved(k_last, edge_steps)
-    sums = attend(q, [(k_1, v_1)], sums, "attend_first")
-
-    v_near, v_1, v_last, sums = after((v_near, v_1, v, sums))
-    v_2 = moved(v_1, second_steps)
-    v_3 = moved(v_last, edge_steps)
-    state, k_2 = after((state, k_2))
-    state = state + swapped(state, "seq", 8)
-    sums = attend(q, list(zip(k_near, v_near)), sums, "attend_near")
-    state, k_3, sums = after((state, k_3, sums))
-    state = halves_joined(state, 0, index)
-    state = halves_joined(state, 1, index)
-
-    w_own = lax.dynamic_slice_in_dim(w, core * width, width, axis=1)
-    w_far = swapped(lax.dynamic_slice_in_dim(w, (1 - core) * width, width, axis=1), "head", 1)
-
-    last = weigh(q, [k_2, k_3], "weigh_last")
+    y_1 = moved(y_own, first_steps)
+    state = added(state, swapped(state, "seq", 4), "state_fourth")
+    state, x_1 = after((state, x_1))
+    far_state = swapped(state, "seq", 8)
+    x_2 = moved(x_1, second_steps)
+
+    y_1, far_state, x_own, y_own = after((y_1, far_state, x_own, y_own))
+    x_3 = moved(x_own, edge_steps)
+    sums = attend(q, [(k_of(x_1), v_of(x_1, y_1))], sums, "attend_first")
+    state = added(state, far_state, "state_summed")
+
+    v_near, y_1, y_own, sums, w, state = after((v_near, y_1, y_own, sums, w, state))
+    w_own, w_sent = parted(w, core, 0, 1, "weights_parted")
+    w_far = swapped(w_sent, "head", 1)
+    y_2 = moved(y_1, second_steps)
+    y_3 = moved(y_own, edge_steps)
+    state = placed(state, swapped(state, "seq", 1), index, 0, "state_joined")
+    near = [(whole(k_far), whole(v_far)) for k_far, v_far in zip(k_near, v_near)]
+    sums = attend(q, near, sums, "attend_near")
+    state, sums, w_far = after((state, sums, w_far))
+    state = placed(state, swapped(state, "seq", 2), index, 1, "state_whole")
+
     low = low_rank_rows(q, feat, state)
-    rows = gather(sums, *last, [v_2, v_3], low, "gather_last")
-    far_rows = swapped(rows, "head", 1)
-    acc = project(None, [(rows, w_own, 0)], jnp.float32, "project_own")
-    return project(acc, [(far_rows, w_far, 0)], jnp.bfloat16, "project_far")
+    last = weigh(q, [k_of(x_2), k_of(x_3)], "weigh_last")
+    v_last = [v_of(x_2, y_2), v_of(x_3, y_3)]
+    rows_a = gather(sums, *last, v_last, low, range(0, pairs // 2), "gather_a")
+    far_a = swapped(rows_a, "head", 1)
+    rows_b = gather(sums, *last, v_last, low, range(pairs // 2, pairs), "gather_b")
+    far_b = swapped(rows_b, "head", 1)
+    acc = project(None, [(rows_a, w_own, 0), (far_a, w_far, 0), (rows_b, w_own, split)], "project_a")
+    return project(acc, [(far_b, w_far, split)], "project_b")
 
 
 def chosen_distances(q, k, v, distances, feat, w):
@@ -340,13 +456,15 @@
 
     paths = [path(bit) for bit in range(bits)]
     low = low_rank_rows(q, feat, state)
-    sums = attend(q, [(k, v)], None, "attend_own")
+    sums = attend(q, [(whole(k), whole(v))], None, "attend_own")
     for partner in range(PARTNERS):
         picked = jnp.sum(jnp.where(distances[partner] == powers, bit_ids, 0))
         k_far, v_far = lax.switch(picked, paths, (k, v))
         if partner < PARTNERS - 1:
-            sums = attend(q, [(k_far, v_far)], sums, "attend_far")
-    rows = gather(sums, *weigh(q, [k_far], "weigh_last"), [v_far], low, "gather_last")
+            sums = attend(q, [(whole(k_far), whole(v_far))], sums, "attend_far")
+    last = weigh(q, [whole(k_far)], "weigh_last")
+    pairs = range(q.shape[1] // PAIR)
+    rows = gather(sums, *last, [whole(v_far)], low, pairs, "gather_last")
     part = jnp.dot(rows, w, preferred_element_type=jnp.float32)
     return lax.psum_scatter(part.astype(jnp.bfloat16), "head", scatter_dimension=1, tiled=True)
 

time: 95.6 us -> 70.8 us (0.74)
  local copies, waits for them, and re-layouts: 16 us -> 2.81 us
  starting transfers between devices: 27.5 us -> 22.1 us
  waiting for transfers between devices: 25.1 us -> 19.9 us
    unnamed x40 -> x12, local copies, waits for them, and re-layouts: 13.9 us -> 2.81 us
    ppermute x6, waiting for transfers between devices: 3.99 us -> 0.02 us  [moved(): lax.ppermute(shard, 'seq', [(a * span + r, b * span + r) for a, b in step...]
    ppermute x12 -> x13, starting transfers between devices: 17 us -> 13.8 us  [swapped(): lax.ppermute(shard, axis, [(i, i ^ distance) for i in range(lax.axis_size...]
    ppermute x6, starting transfers between devices: 10.5 us -> 8.32 us  [moved(): lax.ppermute(shard, 'seq', [(a * span + r, b * span + r) for a, b in step...]
    dynamic_slice x3 -> x0, local copies, waits for them, and re-layouts: 2.1 us -> none  [the longest x1 2.07 us: every_distance(): lax.dynamic_slice_in_dim(w, (1 - core) * width, width, axis=1)]
    ppermute x12 -> x13, waiting for transfers between devices: 21.1 us -> 19.9 us  [swapped(): lax.ppermute(shard, axis, [(i, i ^ distance) for i in range(lax.axis_size...]
    pallas_call x9 -> x19, Pallas kernels: 25.8 us -> 25 us  [the longest x17 22.7 us: kernel_call(): pl.pallas_call(body, out_shape=[pltpu.VMEM(o.shape, o.dtype) for o in out...]
  transfers between devices with their start and end apart: 18 -> 19, of which waited for: 8 -> 8; matrix products, arithmetic and copies ran while one was open for 2% -> 0% of each run, Pallas kernels for 25% -> 34%
where the time goes in v2:
time: 70.8 us; the launch traced here: 70 us
  Pallas kernels  25 us (35%)
  starting transfers between devices  22.1 us (31%)
  waiting for transfers between devices  19.9 us (28%)
  local copies, waits for them, and re-layouts  2.81 us (4%)
    pallas_call x17, Pallas kernels, kernel_call(): pl.pallas_call(body, out_shape=[pltpu.VMEM(o.shape, o.dtype) for o in out...  22.7 us
    ppermute x13, waiting for transfers between devices, swapped(): lax.ppermute(shard, axis, [(i, i ^ distance) for i in range(lax.axis_size...  19.9 us
    ppermute x13, starting transfers between devices, swapped(): lax.ppermute(shard, axis, [(i, i ^ distance) for i in range(lax.axis_size...  13.8 us
    ppermute x6, starting transfers between devices, moved(): lax.ppermute(shard, 'seq', [(a * span + r, b * span + r) for a, b in step...  8.32 us
    unnamed x12, local copies, waits for them, and re-layouts  2.81 us
  transfers between devices with their start and end apart: 19, of which 8 were waited for; matrix products, arithmetic and copies ran while one was open for 0% of the time, Pallas kernels for 34%

profile of v2, /device:TPU:0, one launch (start us, length us, event | category | flops | bytes accessed | tf_op | source)
XLA Modules:
  0.0 70.0 jit_solution(9994053949668149308)
XLA Ops:
  0.0 3.0 %collective-permute-start.1 = (bf16[512,512]{1,0:T(8,128)(2,1)}, bf16[512,512]{1,0:T(8,128)(2,1)S(1)}, u32[]{:S(2)}, u32[]{:S(2)}) collective-permute-start(bf16[512,512]{1,0:T(8,128)(2,1)} %k_ref.1), channel_id=1, source_target_pairs={{0,4},{2,6},{4,0},{6,2},{8,12},{10,14},{12,8},{14,10},{16,20},{18,... | collective-permute-start | bytes 1572872 | tf_op jit(solution)/shard_map/ppermute | solution.py:372
  3.0 1.5 %collective-permute-start = (bf16[512,512]{1,0:T(8,128)(2,1)}, bf16[512,512]{1,0:T(8,128)(2,1)S(1)}, u32[]{:S(2)}, u32[]{:S(2)}) collective-permute-start(bf16[512,512]{1,0:T(8,128)(2,1)} %k_ref.1), channel_id=1, source_target_pairs={{0,2},{2,0},{4,6},{6,4},{8,10},{10,8},{12,14},{14,12},{16,18},{18,... | collective-permute-start | bytes 1572872 | tf_op jit(solution)/shard_map/ppermute | solution.py:372
  4.5 1.2 %values_packed.1 = (bf16[512,768]{1,0:T(8,128)(2,1)S(1)}, bf16[512,256]{1,0:T(8,128)(2,1)S(1)}) custom-call(bf16[512,512]{1,0:T(8,128)(2,1)} %k_ref.1, bf16[512,512]{1,0:T(8,128)(2,1)} %v_ref.3), custom_call_target="tpu_custom_call" | custom-call | flops 1000 | tf_op jit(solution)/shard_map/values_packed/pallas_call | solution.py:325
  5.7 1.6 %collective-permute-start.8 = (bf16[512,768]{1,0:T(8,128)(2,1)S(1)}, bf16[512,768]{1,0:T(8,128)(2,1)S(1)}, u32[]{:S(2)}, u32[]{:S(2)}) collective-permute-start(bf16[512,768]{1,0:T(8,128)(2,1)S(1)} %get-tuple-element.99), channel_id=1, source_target_pairs={{8,24},{10,26},{12,28},{14,30},{16,0},{18,2},{20,4},{22,6},{0,8},{... | collective-permute-start | bytes 2359304 | tf_op jit(solution)/shard_map/ppermute | solution.py:377
  7.3 1.0 %copy-done.2 = bf16[512,512]{1,0:T(8,128)(2,1)S(1)} copy-done((bf16[512,512]{1,0:T(8,128)(2,1)S(1)}, bf16[512,512]{1,0:T(8,128)(2,1)}, u32[]{:S(2)}) %copy-start.2) | copy-done | bytes 524312
  8.4 0.7 %copy-done.4 = bf16[64,128]{1,0:T(8,128)(2,1)S(1)} copy-done((bf16[64,128]{1,0:T(8,128)(2,1)S(1)}, bf16[64,128]{1,0:T(8,128)(2,1)}, u32[]{:S(2)}) %copy-start.4) | copy-done | bytes 16408
  9.1 3.4 %key_state.1.ref = bf16[640,128]{1,0:T(8,128)(2,1)S(1)} custom-call(bf16[512,512]{1,0:T(8,128)(2,1)S(1)} %copy-done.2, bf16[512,512]{1,0:T(8,128)(2,1)} %v_ref.3, bf16[64,128]{1,0:T(8,128)(2,1)S(1)} %copy-done.4), custom_call_target="tpu_custom_call" | custom-call | flops 1000 | tf_op jit(solution)/shard_map/key_state/pallas_call | solution.py:72
  12.5 0.0 copy-start
  12.5 1.0 %copy-done = bf16[512,512]{1,0:T(8,128)(2,1)S(1)} copy-done((bf16[512,512]{1,0:T(8,128)(2,1)S(1)}, bf16[512,512]{1,0:T(8,128)(2,1)}, u32[]{:S(2)}) %copy-start) | copy-done | bytes 524312
  13.6 4.0 %attend_own.1 = (f32[512,512]{1,0:T(8,128)S(1)}, f32[512,512]{1,0:T(8,128)S(1)}, f32[512,512]{1,0:T(8,128)S(1)}) custom-call(bf16[512,512]{1,0:T(8,128)(2,1)S(1)} %copy-done, bf16[512,512]{1,0:T(8,128)(2,1)S(1)} %copy-done.2, bf16[512,512]{1,0:T(8,128)(2,1)} %v_ref.3), custom_call_target="tpu_custom_call" | custom-call | flops 1000 | tf_op jit(solution)/shard_map/attend_own/pallas_call | solution.py:72
  17.5 0.0 collective-permute-done.1.refs_3_
  17.6 0.6 collective-permute-start.2
  18.2 3.9 %collective-permute-done.2.second_ref = bf16[320,128]{1,0:T(8,128)(2,1)S(1)} collective-permute-done((bf16[320,128]{1,0:T(8,128)(2,1)S(1)}, bf16[320,128]{1,0:T(8,128)(2,1)S(1)}, u32[]{:S(2)}, u32[]{:S(2)}) %collective-permute-start.2) | collective-permute-done | bytes 81952 | tf_op jit(solution)/shard_map/ppermute | solution.py:372
  22.1 0.6 collective-permute-start.3
  22.7 3.5 %collective-permute-done.3.second_ref = bf16[160,128]{1,0:T(8,128)(2,1)S(1)} collective-permute-done((bf16[160,128]{1,0:T(8,128)(2,1)S(1)}, bf16[160,128]{1,0:T(8,128)(2,1)S(1)}, u32[]{:S(2)}, u32[]{:S(2)}) %collective-permute-start.3) | collective-permute-done | bytes 40992 | tf_op jit(solution)/shard_map/ppermute | solution.py:372
  26.2 0.6 collective-permute-start.5
  26.8 0.5 collective-permute-start.4
  27.3 2.6 %collective-permute-start.6 = (bf16[512,256]{1,0:T(8,128)(2,1)S(1)}, bf16[512,256]{1,0:T(8,128)(2,1)S(1)}, u32[]{:S(2)}, u32[]{:S(2)}) collective-permute-start(bf16[512,256]{1,0:T(8,128)(2,1)S(1)} %get-tuple-element.103), channel_id=1, source_target_pairs={{8,24},{10,26},{12,28},{14,30},{16,0},{18,2},{20,4},{22,6},{0,8},{... | collective-permute-start | bytes 786440 | tf_op jit(solution)/shard_map/ppermute | solution.py:377
  29.9 1.5 %collective-permute-start.7 = (bf16[160,128]{1,0:T(8,128)(2,1)S(1)}, bf16[160,128]{1,0:T(8,128)(2,1)S(1)}, u32[]{:S(2)}, u32[]{:S(2)}) collective-permute-start(bf16[160,128]{1,0:T(8,128)(2,1)S(1)} %state_third.1.first_ref), channel_id=1, source_target_pairs={{0,8},{2,10},{4,12},{6,14},{8,0},{10,2},{12,4},{14,6},{16,24},{18,... | collective-permute-start | bytes 122888 | tf_op jit(solution)/shard_map/ppermute | solution.py:372
  31.4 4.0 %collective-permute-done.7.second_ref = bf16[160,128]{1,0:T(8,128)(2,1)S(1)} collective-permute-done((bf16[160,128]{1,0:T(8,128)(2,1)S(1)}, bf16[160,128]{1,0:T(8,128)(2,1)S(1)}, u32[]{:S(2)}, u32[]{:S(2)}) %collective-permute-start.7) | collective-permute-done | bytes 40992 | tf_op jit(solution)/shard_map/ppermute | solution.py:372
  35.5 1.7 %collective-permute-start.9 = (bf16[160,128]{1,0:T(8,128)(2,1)S(1)}, bf16[160,128]{1,0:T(8,128)(2,1)S(1)}, u32[]{:S(2)}, u32[]{:S(2)}) collective-permute-start(bf16[160,128]{1,0:T(8,128)(2,1)S(1)} %state_fourth.1.first_ref), channel_id=1, source_target_pairs={{0,16},{2,18},{4,20},{6,22},{8,24},{10,26},{12,28},{14,30},{16,0},... | collective-permute-start | bytes 122888 | tf_op jit(solution)/shard_map/ppermute | solution.py:372
  37.2 0.7 collective-permute-start.12
  37.9 3.1 %collective-permute-done.9.second_ref = bf16[160,128]{1,0:T(8,128)(2,1)S(1)} collective-permute-done((bf16[160,128]{1,0:T(8,128)(2,1)S(1)}, bf16[160,128]{1,0:T(8,128)(2,1)S(1)}, u32[]{:S(2)}, u32[]{:S(2)}) %collective-permute-start.9) | collective-permute-done | bytes 40992 | tf_op jit(solution)/shard_map/ppermute | solution.py:372
  41.0 0.0 collective-permute-done.6.refs_5_
  41.0 1.3 %collective-permute-start.13 = (bf16[512,768]{1,0:T(8,128)(2,1)S(1)}, bf16[512,768]{1,0:T(8,128)(2,1)S(1)}, u32[]{:S(2)}, u32[]{:S(2)}) collective-permute-start(bf16[512,768]{1,0:T(8,128)(2,1)S(1)} %get-tuple-element.99), channel_id=1, source_target_pairs={{8,0},{10,2},{12,4},{14,6},{16,24},{18,26},{20,28},{22,30},{9,1},{... | collective-permute-start | bytes 2359304 | tf_op jit(solution)/shard_map/ppermute | solution.py:377
  42.3 3.3 %attend_first.1 = (f32[512,512]{1,0:T(8,128)S(1)}, f32[512,512]{1,0:T(8,128)S(1)}, f32[512,512]{1,0:T(8,128)S(1)}) custom-call(bf16[512,512]{1,0:T(8,128)(2,1)S(1)} %copy-done.1, bf16[512,768]{1,0:T(8,128)(2,1)S(1)} %collective-permute-done.8.refs_1_, f32[512,512]{1,0:T(8,128)S(1)} %get-tuple-element.75.refs_2_, f32[512,512]{1,0:T(8,128)S(1)} %get-tuple-element.76.refs_3_, ...), custom_call_target="tpu_custom_call" | custom-call | flops 1000 | tf_op jit(solution)/shard_map/attend_first/pallas_call | solution.py:72
  45.6 0.0 collective-permute-done.5.refs_4_
  45.6 0.1 weights_parted.1
  45.7 0.0 copy-start.5
  45.7 0.1 collective-permute-start.11
  45.8 1.6 %collective-permute-start.10 = (bf16[160,128]{1,0:T(8,128)(2,1)S(1)}, bf16[160,128]{1,0:T(8,128)(2,1)S(1)}, u32[]{:S(2)}, u32[]{:S(2)}) collective-permute-start(bf16[160,128]{1,0:T(8,128)(2,1)S(1)} %state_summed.1.own_ref), channel_id=1, source_target_pairs={{0,2},{2,0},{4,6},{6,4},{8,10},{10,8},{12,14},{14,12},{16,18},{18,... | collective-permute-start | bytes 122888 | tf_op jit(solution)/shard_map/ppermute | solution.py:372
  47.3 0.7 collective-permute-start.14
  48.0 1.8 %collective-permute-done.10.far_ref = bf16[160,128]{1,0:T(8,128)(2,1)S(1)} collective-permute-done((bf16[160,128]{1,0:T(8,128)(2,1)S(1)}, bf16[160,128]{1,0:T(8,128)(2,1)S(1)}, u32[]{:S(2)}, u32[]{:S(2)}) %collective-permute-start.10) | collective-permute-done | bytes 40992 | tf_op jit(solution)/shard_map/ppermute | solution.py:372
  49.8 1.5 %collective-permute-start.15 = (bf16[512,256]{1,0:T(8,128)(2,1)S(1)}, bf16[512,256]{1,0:T(8,128)(2,1)S(1)}, u32[]{:S(2)}, u32[]{:S(2)}) collective-permute-start(bf16[512,256]{1,0:T(8,128)(2,1)S(1)} %get-tuple-element.103), channel_id=1, source_target_pairs={{8,0},{10,2},{12,4},{14,6},{16,24},{18,26},{20,28},{22,30},{9,1},{... | collective-permute-start | bytes 786440 | tf_op jit(solution)/shard_map/ppermute | solution.py:377
  51.3 5.9 %attend_near.1 = (f32[512,512]{1,0:T(8,128)S(1)}, f32[512,512]{1,0:T(8,128)S(1)}, f32[512,512]{1,0:T(8,128)S(1)}) custom-call(bf16[512,512]{1,0:T(8,128)(2,1)S(1)} %copy-done.1, bf16[512,512]{1,0:T(8,128)(2,1)S(1)} %collective-permute-done.refs_1_, bf16[512,512]{1,0:T(8,128)(2,1)S(1)} %collective-permute-done.4.refs_2_, ...), custom_call_target="tpu_custom_call" | custom-call | flops 1000 | tf_op jit(solution)/shard_map/attend_near/pallas_call | solution.py:72
  57.2 1.6 %collective-permute-start.16 = (bf16[320,128]{1,0:T(8,128)(2,1)S(1)}, bf16[320,128]{1,0:T(8,128)(2,1)S(1)}, u32[]{:S(2)}, u32[]{:S(2)}) collective-permute-start(bf16[320,128]{1,0:T(8,128)(2,1)S(1)} %state_joined.1.own_ref), channel_id=1, source_target_pairs={{0,4},{2,6},{4,0},{6,2},{8,12},{10,14},{12,8},{14,10},{16,20},{18,... | collective-permute-start | bytes 245768 | tf_op jit(solution)/shard_map/ppermute | solution.py:372
  58.8 2.9 %collective-permute-done.16.far_ref = bf16[320,128]{1,0:T(8,128)(2,1)S(1)} collective-permute-done((bf16[320,128]{1,0:T(8,128)(2,1)S(1)}, bf16[320,128]{1,0:T(8,128)(2,1)S(1)}, u32[]{:S(2)}, u32[]{:S(2)}) %collective-permute-start.16) | collective-permute-done | bytes 81952 | tf_op jit(solution)/shard_map/ppermute | solution.py:372
  61.8 0.0 collective-permute-done.12.refs_1_.refs_5_
  61.8 1.7 %weigh_last.1 = (bf16[512,4096]{1,0:T(8,128)(2,1)S(1)}, f32[512,512]{1,0:T(8,128)S(1)}) custom-call(bf16[512,512]{1,0:T(8,128)(2,1)S(1)} %copy-done.1, bf16[512,768]{1,0:T(8,128)(2,1)S(1)} %collective-permute-done.12.refs_1_.refs_5_, bf16[512,768]{1,0:T(8,128)(2,1)S(1)} %collective-permute-done.13.refs_2_.refs_6_), custom_call_target="tpu_custom_call" | custom-call | flops 1000 | tf_op jit(solution)/shard_map/weigh_last/pallas_call | solution.py:72
  63.5 1.9 %low_rank.1.refs_7_ = f32[512,512]{1,0:T(8,128)S(1)} custom-call(bf16[512,512]{1,0:T(8,128)(2,1)S(1)} %copy-done.1, bf16[64,128]{1,0:T(8,128)(2,1)S(1)} %copy-done.5, bf16[640,128]{1,0:T(8,128)(2,1)S(1)} %state_whole.1.state_ref), custom_call_target="tpu_custom_call" | custom-call | flops 1000 | tf_op jit(solution)/shard_map/low_rank/pallas_call | solution.py:72
  65.4 0.8 %gather_a.1.refs_0_ = bf16[512,256]{1,0:T(8,128)(2,1)S(1)} custom-call(f32[512,512]{1,0:T(8,128)S(1)} %get-tuple-element.96.refs_0_, f32[512,512]{1,0:T(8,128)S(1)} %get-tuple-element.97.refs_1_, f32[512,512]{1,0:T(8,128)S(1)} %get-tuple-element.98.refs_2_, bf16[512,4096]{1,0:T(8,128)(2,1)S(1)} %get-tuple-element.100.refs_3_, ...), custom_call_target="tpu_custom_call" | custom-call | flops 1000 | tf_op jit(solution)/shard_map/gather_a/pallas_call | solution.py:72
  66.3 0.1 collective-permute-start.18
  66.4 0.8 %gather_b.1.refs_4_ = bf16[512,256]{1,0:T(8,128)(2,1)S(1)} custom-call(f32[512,512]{1,0:T(8,128)S(1)} %get-tuple-element.96.refs_0_, f32[512,512]{1,0:T(8,128)S(1)} %get-tuple-element.97.refs_1_, f32[512,512]{1,0:T(8,128)S(1)} %get-tuple-element.98.refs_2_, bf16[512,4096]{1,0:T(8,128)(2,1)S(1)} %get-tuple-element.100.refs_3_, ...), custom_call_target="tpu_custom_call" | custom-call | flops 1000 | tf_op jit(solution)/shard_map/gather_b/pallas_call | solution.py:72
  67.2 0.5 collective-permute-start.17
  67.8 0.1 collective-permute-done.18.refs_2_
  67.9 0.6 project_a.1.refs_2_
  68.5 0.5 collective-permute-done.17.refs_0_
  68.9 1.1 %project_b.1 = bf16[512,512]{1,0:T(8,128)(2,1)} custom-call(bf16[512,256]{1,0:T(8,128)(2,1)S(1)} %collective-permute-done.17.refs_0_, bf16[512,512]{1,0:T(8,128)(2,1)S(1)} %collective-permute-done.11.refs_3_.refs_1_, f32[512,512]{1,0:T(8,128)S(1)} %project_a.1.refs_2_), custom_call_target="tpu_custom_call" | custom-call | flops 1000 | tf_op jit(solution)/shard_map/project_b/pallas_call | solution.py:283
  (21 shorter events, 0.1 us)
Async XLA Ops:
  0.0 42.3 %copy-start.1 = (bf16[512,512]{1,0:T(8,128)(2,1)S(1)}, bf16[512,512]{1,0:T(8,128)(2,1)}, u32[]{:S(2)}) copy-start(bf16[512,512]{1,0:T(8,128)(2,1)} %q_ref.1) | copy-start | bytes 1572868
  0.0 17.5 %collective-permute-start.1 = (bf16[512,512]{1,0:T(8,128)(2,1)}, bf16[512,512]{1,0:T(8,128)(2,1)S(1)}, u32[]{:S(2)}, u32[]{:S(2)}) collective-permute-start(bf16[512,512]{1,0:T(8,128)(2,1)} %k_ref.1), channel_id=1, source_target_pairs={{0,4},{2,6},{4,0},{6,2},{8,12},{10,14},{12,8},{14,10},{16,20},{18,... | collective-permute-start | bytes 1572872 | tf_op jit(solution)/shard_map/ppermute | solution.py:372
  3.0 14.6 %collective-permute-start = (bf16[512,512]{1,0:T(8,128)(2,1)}, bf16[512,512]{1,0:T(8,128)(2,1)S(1)}, u32[]{:S(2)}, u32[]{:S(2)}) collective-permute-start(bf16[512,512]{1,0:T(8,128)(2,1)} %k_ref.1), channel_id=1, source_target_pairs={{0,2},{2,0},{4,6},{6,4},{8,10},{10,8},{12,14},{14,12},{16,18},{18,... | collective-permute-start | bytes 1572872 | tf_op jit(solution)/shard_map/ppermute | solution.py:372
  5.7 29.8 %collective-permute-start.8 = (bf16[512,768]{1,0:T(8,128)(2,1)S(1)}, bf16[512,768]{1,0:T(8,128)(2,1)S(1)}, u32[]{:S(2)}, u32[]{:S(2)}) collective-permute-start(bf16[512,768]{1,0:T(8,128)(2,1)S(1)} %get-tuple-element.99), channel_id=1, source_target_pairs={{8,24},{10,26},{12,28},{14,30},{16,0},{18,2},{20,4},{22,6},{0,8},{... | collective-permute-start | bytes 2359304 | tf_op jit(solution)/shard_map/ppermute | solution.py:377
  7.3 1.0 %copy-start.2 = (bf16[512,512]{1,0:T(8,128)(2,1)S(1)}, bf16[512,512]{1,0:T(8,128)(2,1)}, u32[]{:S(2)}) copy-start(bf16[512,512]{1,0:T(8,128)(2,1)} %k_ref.1) | copy-start | bytes 1572868
  8.4 0.7 %copy-start.4 = (bf16[64,128]{1,0:T(8,128)(2,1)S(1)}, bf16[64,128]{1,0:T(8,128)(2,1)}, u32[]{:S(2)}) copy-start(bf16[64,128]{1,0:T(8,128)(2,1)} %feat_ref.3) | copy-start | bytes 49156
  9.1 36.5 %copy-start.3 = (bf16[512,1024]{1,0:T(8,128)(2,1)S(1)}, bf16[512,1024]{1,0:T(8,128)(2,1)}, u32[]{:S(2)}) copy-start(bf16[512,1024]{1,0:T(8,128)(2,1)} %ref) | copy-start | bytes 3145732
  12.5 1.0 %copy-start = (bf16[512,512]{1,0:T(8,128)(2,1)S(1)}, bf16[512,512]{1,0:T(8,128)(2,1)}, u32[]{:S(2)}) copy-start(bf16[512,512]{1,0:T(8,128)(2,1)} %q_ref.1) | copy-start | bytes 1572868
  17.6 4.5 %collective-permute-start.2 = (bf16[320,128]{1,0:T(8,128)(2,1)S(1)}, bf16[320,128]{1,0:T(8,128)(2,1)S(1)}, u32[]{:S(2)}, u32[]{:S(2)}) collective-permute-start(bf16[320,128]{1,0:T(8,128)(2,1)S(1)} %get-tuple-element.63), channel_id=1, source_target_pairs={{0,4},{2,6},{4,0},{6,2},{8,12},{10,14},{12,8},{14,10},{16,20},{18,... | collective-permute-start | bytes 245768 | tf_op jit(solution)/shard_map/ppermute | solution.py:372
  22.1 4.1 %collective-permute-start.3 = (bf16[160,128]{1,0:T(8,128)(2,1)S(1)}, bf16[160,128]{1,0:T(8,128)(2,1)S(1)}, u32[]{:S(2)}, u32[]{:S(2)}) collective-permute-start(bf16[160,128]{1,0:T(8,128)(2,1)S(1)} %get-tuple-element.65), channel_id=1, source_target_pairs={{0,2},{2,0},{4,6},{6,4},{8,10},{10,8},{12,14},{14,12},{16,18},{18,... | collective-permute-start | bytes 122888 | tf_op jit(solution)/shard_map/ppermute | solution.py:372
  26.2 19.4 %collective-permute-start.5 = (bf16[512,512]{1,0:T(8,128)(2,1)}, bf16[512,512]{1,0:T(8,128)(2,1)S(1)}, u32[]{:S(2)}, u32[]{:S(2)}) collective-permute-start(bf16[512,512]{1,0:T(8,128)(2,1)} %v_ref.3), channel_id=1, source_target_pairs={{0,4},{2,6},{4,0},{6,2},{8,12},{10,14},{12,8},{14,10},{16,20},{18,... | collective-permute-start | bytes 1572872 | tf_op jit(solution)/shard_map/ppermute | solution.py:372
  26.8 18.8 %collective-permute-start.4 = (bf16[512,512]{1,0:T(8,128)(2,1)}, bf16[512,512]{1,0:T(8,128)(2,1)S(1)}, u32[]{:S(2)}, u32[]{:S(2)}) collective-permute-start(bf16[512,512]{1,0:T(8,128)(2,1)} %v_ref.3), channel_id=1, source_target_pairs={{0,2},{2,0},{4,6},{6,4},{8,10},{10,8},{12,14},{14,12},{16,18},{18,... | collective-permute-start | bytes 1572872 | tf_op jit(solution)/shard_map/ppermute | solution.py:372
  27.3 13.6 %collective-permute-start.6 = (bf16[512,256]{1,0:T(8,128)(2,1)S(1)}, bf16[512,256]{1,0:T(8,128)(2,1)S(1)}, u32[]{:S(2)}, u32[]{:S(2)}) collective-permute-start(bf16[512,256]{1,0:T(8,128)(2,1)S(1)} %get-tuple-element.103), channel_id=1, source_target_pairs={{8,24},{10,26},{12,28},{14,30},{16,0},{18,2},{20,4},{22,6},{0,8},{... | collective-permute-start | bytes 786440 | tf_op jit(solution)/shard_map/ppermute | solution.py:377
  29.9 5.6 %collective-permute-start.7 = (bf16[160,128]{1,0:T(8,128)(2,1)S(1)}, bf16[160,128]{1,0:T(8,128)(2,1)S(1)}, u32[]{:S(2)}, u32[]{:S(2)}) collective-permute-start(bf16[160,128]{1,0:T(8,128)(2,1)S(1)} %state_third.1.first_ref), channel_id=1, source_target_pairs={{0,8},{2,10},{4,12},{6,14},{8,0},{10,2},{12,4},{14,6},{16,24},{18,... | collective-permute-start | bytes 122888 | tf_op jit(solution)/shard_map/ppermute | solution.py:372
  35.5 5.5 %collective-permute-start.9 = (bf16[160,128]{1,0:T(8,128)(2,1)S(1)}, bf16[160,128]{1,0:T(8,128)(2,1)S(1)}, u32[]{:S(2)}, u32[]{:S(2)}) collective-permute-start(bf16[160,128]{1,0:T(8,128)(2,1)S(1)} %state_fourth.1.first_ref), channel_id=1, source_target_pairs={{0,16},{2,18},{4,20},{6,22},{8,24},{10,26},{12,28},{14,30},{16,0},... | collective-permute-start | bytes 122888 | tf_op jit(solution)/shard_map/ppermute | solution.py:372
  37.2 24.6 %collective-permute-start.12 = (bf16[512,768]{1,0:T(8,128)(2,1)S(1)}, bf16[512,768]{1,0:T(8,128)(2,1)S(1)}, u32[]{:S(2)}, u32[]{:S(2)}) collective-permute-start(bf16[512,768]{1,0:T(8,128)(2,1)S(1)} %collective-permute-done.8.refs_1_), channel_id=1, source_target_pairs={{8,16},{10,18},{12,20},{14,22},{16,8},{18,10},{20,12},{22,14},{9,1... | collective-permute-start | bytes 2359304 | tf_op jit(solution)/shard_map/ppermute | solution.py:377
  41.0 20.8 %collective-permute-start.13 = (bf16[512,768]{1,0:T(8,128)(2,1)S(1)}, bf16[512,768]{1,0:T(8,128)(2,1)S(1)}, u32[]{:S(2)}, u32[]{:S(2)}) collective-permute-start(bf16[512,768]{1,0:T(8,128)(2,1)S(1)} %get-tuple-element.99), channel_id=1, source_target_pairs={{8,0},{10,2},{12,4},{14,6},{16,24},{18,26},{20,28},{22,30},{9,1},{... | collective-permute-start | bytes 2359304 | tf_op jit(solution)/shard_map/ppermute | solution.py:377
  45.7 17.9 %copy-start.5 = (bf16[64,128]{1,0:T(8,128)(2,1)S(1)}, bf16[64,128]{1,0:T(8,128)(2,1)}, u32[]{:S(2)}) copy-start(bf16[64,128]{1,0:T(8,128)(2,1)} %feat_ref.3) | copy-start | bytes 49156
  45.7 11.6 %collective-permute-start.11 = (bf16[512,512]{1,0:T(8,128)(2,1)S(1)}, bf16[512,512]{1,0:T(8,128)(2,1)S(1)}, u32[]{:S(2)}, u32[]{:S(2)}) collective-permute-start(bf16[512,512]{1,0:T(8,128)(2,1)S(1)} %get-tuple-element.95), channel_id=1, source_target_pairs={{0,1},{1,0},{2,3},{3,2},{4,5},{5,4},{6,7},{7,6},{8,9},{9,8},{10,11... | collective-permute-start | bytes 1572872 | tf_op jit(solution)/shard_map/ppermute | solution.py:372
  45.8 4.1 %collective-permute-start.10 = (bf16[160,128]{1,0:T(8,128)(2,1)S(1)}, bf16[160,128]{1,0:T(8,128)(2,1)S(1)}, u32[]{:S(2)}, u32[]{:S(2)}) collective-permute-start(bf16[160,128]{1,0:T(8,128)(2,1)S(1)} %state_summed.1.own_ref), channel_id=1, source_target_pairs={{0,2},{2,0},{4,6},{6,4},{8,10},{10,8},{12,14},{14,12},{16,18},{18,... | collective-permute-start | bytes 122888 | tf_op jit(solution)/shard_map/ppermute | solution.py:372
  47.3 19.0 %collective-permute-start.14 = (bf16[512,256]{1,0:T(8,128)(2,1)S(1)}, bf16[512,256]{1,0:T(8,128)(2,1)S(1)}, u32[]{:S(2)}, u32[]{:S(2)}) collective-permute-start(bf16[512,256]{1,0:T(8,128)(2,1)S(1)} %collective-permute-done.6.refs_5_), channel_id=1, source_target_pairs={{8,16},{10,18},{12,20},{14,22},{16,8},{18,10},{20,12},{22,14},{9,1... | collective-permute-start | bytes 786440 | tf_op jit(solution)/shard_map/ppermute | solution.py:377
  49.8 16.5 %collective-permute-start.15 = (bf16[512,256]{1,0:T(8,128)(2,1)S(1)}, bf16[512,256]{1,0:T(8,128)(2,1)S(1)}, u32[]{:S(2)}, u32[]{:S(2)}) collective-permute-start(bf16[512,256]{1,0:T(8,128)(2,1)S(1)} %get-tuple-element.103), channel_id=1, source_target_pairs={{8,0},{10,2},{12,4},{14,6},{16,24},{18,26},{20,28},{22,30},{9,1},{... | collective-permute-start | bytes 786440 | tf_op jit(solution)/shard_map/ppermute | solution.py:377
  57.2 4.5 %collective-permute-start.16 = (bf16[320,128]{1,0:T(8,128)(2,1)S(1)}, bf16[320,128]{1,0:T(8,128)(2,1)S(1)}, u32[]{:S(2)}, u32[]{:S(2)}) collective-permute-start(bf16[320,128]{1,0:T(8,128)(2,1)S(1)} %state_joined.1.own_ref), channel_id=1, source_target_pairs={{0,4},{2,6},{4,0},{6,2},{8,12},{10,14},{12,8},{14,10},{16,20},{18,... | collective-permute-start | bytes 245768 | tf_op jit(solution)/shard_map/ppermute | solution.py:372
  66.3 1.6 %collective-permute-start.18 = (bf16[512,256]{1,0:T(8,128)(2,1)S(1)}, bf16[512,256]{1,0:T(8,128)(2,1)S(1)}, u32[]{:S(2)}, u32[]{:S(2)}) collective-permute-start(bf16[512,256]{1,0:T(8,128)(2,1)S(1)} %gather_a.1.refs_0_), channel_id=1, source_target_pairs={{0,1},{1,0},{2,3},{3,2},{4,5},{5,4},{6,7},{7,6},{8,9},{9,8},{10,11... | collective-permute-start | bytes 786440 | tf_op jit(solution)/shard_map/ppermute | solution.py:372
  67.2 1.7 %collective-permute-start.17 = (bf16[512,256]{1,0:T(8,128)(2,1)S(1)}, bf16[512,256]{1,0:T(8,128)(2,1)S(1)}, u32[]{:S(2)}, u32[]{:S(2)}) collective-permute-start(bf16[512,256]{1,0:T(8,128)(2,1)S(1)} %gather_b.1.refs_4_), channel_id=1, source_target_pairs={{0,1},{1,0},{2,3},{3,2},{4,5},{5,4},{6,7},{7,6},{8,9},{9,8},{10,11... | collective-permute-start | bytes 786440 | tf_op jit(solution)/shard_map/ppermute | solution.py:372

commit v3 on v2

--- a/solution.py
+++ b/solution.py
@@ -138,46 +138,83 @@
     return pairs_call(body, outs, operands, range(width // PAIR), width // PAIR, name)
 
 
-def weigh(q, parts, name):
+def weigh(q, blocks, name):
     tokens, width = q.shape
-    keys = parts[0][0][0].shape[0]
+    keys = blocks[0][0][0][0].shape[0]
+    count = len(blocks)
 
     def body(q_ref, *refs):
         w_out, top_out = refs[-2:]
         q_pair = scaled(q_ref[...])
-        k_pair = block_of(refs[:-2])
+        rest = list(refs[:-2])
+        k_pairs = [block_of([rest.pop(0) for _ in block]) for block in blocks]
         tops = []
+        for half in range(2):
+            top, weights = weigh_head(q_pair, k_pairs, half)
+            tops.append(top)
+            for i, w in enumerate(weights):
+                at = (half * count + i) * keys
+                w_out[:, at:at + keys] = w
+        top_out[...] = jnp.where(low_lanes(tokens), *tops)
+
+    outs = [
+        jax.ShapeDtypeStruct((tokens, width // HEAD_DIM * count * keys), jnp.bfloat16),
+        jax.ShapeDtypeStruct((tokens, width), jnp.float32),
+    ]
+    operands = [whole(q)] + [part for block in blocks for part in block]
+    return pairs_call(body, outs, operands, range(width // PAIR), width // PAIR, name)
+
+
+def gather(before, weighed, blocks, low_rank, pairs, name):
+    weights, tops = weighed
+    tokens, width = tops.shape
+    count = len(blocks)
+    keys = weights.shape[1] // (width // HEAD_DIM) // count
+    operands = [whole(x) for x in (*before, weights, tops)]
+    operands += [part for block in blocks for part in block]
+    if low_rank is not None:
+        operands.append(whole(low_rank))
+
+    def body(*refs):
+        rest = list(refs[5:len(operands)])
+        v_pairs = [block_of([rest.pop(0) for _ in block]) for block in blocks]
+        sums = []
+        for half in range(2):
+            ats = [(half * count + i) * keys for i in range(count)]
+            sums.append(add_values([refs[3][:, at:at + keys] for at in ats], v_pairs, half))
+        state = joined([tuple(r[...] for r in refs[:3]), (refs[4][...], *numer_denom(*sums))])
+        if low_rank is not None:
+            state = [(state[1] / state[2] + rest[0][...]).astype(jnp.bfloat16)]
+        for out, value in zip(refs[len(operands):], state):
+            out[...] = value
+
+    if low_rank is not None:
+        outs = [jax.ShapeDtypeStruct((tokens, len(pairs) * PAIR), jnp.bfloat16)]
+        return pairs_call(body, outs, operands, pairs, width // PAIR, name)[0]
+    outs = [jax.ShapeDtypeStruct((tokens, width), jnp.float32)] * 3
+    return pairs_call(body, outs, operands, pairs, width // PAIR, name)
+
+
+def finish(q, parts, before, low_rank, pairs, name):
+    tokens, width = q.shape
+    count = len(parts)
+    operands = [whole(q)] + [k for k, _ in parts] + [v for _, v in parts]
+    operands += [whole(x) for x in (*before, low_rank)]
+
+    def body(*refs):
+        q_pair = scaled(refs[0][...])
+        k_pair, v_pair = block_of(refs[1:1 + count]), block_of(refs[1 + count:1 + 2 * count])
+        tops, sums = [], []
         for half in range(2):
             top, weights = weigh_head(q_pair, [k_pair], half)
             tops.append(top)
-            w_out[:, half * keys:(half + 1) * keys] = weights[0]
-        top_out[...] = jnp.where(low_lanes(tokens), *tops)
-
-    outs = [
-        jax.ShapeDtypeStruct((tokens, width // HEAD_DIM * keys), jnp.bfloat16),
-        jax.ShapeDtypeStruct((tokens, width), jnp.float32),
-    ]
-    return pairs_call(body, outs, [whole(q)] + list(parts), range(width // PAIR), width // PAIR, name)
-
-
-def gather(before, weights, tops, parts, low_rank, pairs, name):
-    tokens = tops.shape[0]
-    keys = weights.shape[1] // (tops.shape[1] // HEAD_DIM)
-
-    def body(*refs):
-        w_ref, low_ref, out = refs[3], refs[-2], refs[-1]
-        v_pair = block_of(refs[5:-2])
-        sums = [
-            add_values([w_ref[:, half * keys:(half + 1) * keys]], [v_pair], half)
-            for half in range(2)
-        ]
-        state = (refs[4][...], *numer_denom(*sums))
-        _, numer, denom = joined([tuple(r[...] for r in refs[:3]), state])
-        out[...] = (numer / denom + low_ref[...]).astype(jnp.bfloat16)
-
-    operands = [whole(x) for x in before] + [whole(weights), whole(tops)] + list(parts) + [whole(low_rank)]
+            sums.append(add_values(weights, [v_pair], half))
+        state = (jnp.where(low_lanes(tokens), *tops), *numer_denom(*sums))
+        _, numer, denom = joined([state, tuple(r[...] for r in refs[1 + 2 * count:-2])])
+        refs[-1][...] = (numer / denom + refs[-2][...]).astype(jnp.bfloat16)
+
     outs = [jax.ShapeDtypeStruct((tokens, len(pairs) * PAIR), jnp.bfloat16)]
-    return pairs_call(body, outs, operands, pairs, tops.shape[1] // PAIR, name)[0]
+    return pairs_call(body, outs, operands, pairs, width // PAIR, name)[0]
 
 
 def twice(feat):
@@ -188,17 +225,29 @@
     return pairs * features + features
 
 
-def key_state(k, v, feat):
-    tokens, width = k.shape
-    pairs, features = width // PAIR, feat.shape[1]
+def key_state(k, v, feat, pairs):
+    features = feat.shape[1]
     spread = PAIR // (2 * pairs)
-
-    def body(k_ref, v_ref, feat_ref, out):
+    arrays = []
+    for array, _, _ in k + v:
+        if not any(array is other for other in arrays):
+            arrays.append(array)
+
+    def pair_of(refs, operand, c):
+        at = c * PAIR
+        for array, first, count in operand:
+            if 0 <= at < count:
+                index = [array is other for other in arrays].index(True)
+                return refs[index][:, first + at:first + at + PAIR]
+            at -= count
+
+    def body(*refs):
+        feat_ref, out = refs[-2:]
         feat_t = twice(feat_ref[...].astype(jnp.float32)).T.astype(jnp.bfloat16)
         lane = lax.broadcasted_iota(jnp.int32, (features, PAIR), 1)
         norms = jnp.zeros((features, PAIR), jnp.float32)
         for c in range(pairs):
-            k_pair, v_pair = cols(k_ref, c), cols(v_ref, c)
+            k_pair, v_pair = pair_of(refs, k, c), pair_of(refs, v, c)
             k_float = k_pair.astype(jnp.float32)
             square = k_float * k_float
             square_hi = square.astype(jnp.bfloat16)
@@ -227,7 +276,7 @@
         out[pairs * features:, :] = norms.astype(jnp.bfloat16)
 
     outs = jax.ShapeDtypeStruct((state_rows(pairs, features), PAIR), jnp.bfloat16)
-    return kernel_call(body, [outs], [k, v, feat], "key_state")[0]
+    return kernel_call(body, [outs], arrays + [feat], "key_state")[0]
 
 
 def low_rank_rows(q, feat, state):
@@ -306,16 +355,13 @@
     return kernel_call(body, outs, [place, array], name)
 
 
-def packed(k, v, split, name):
+def packed(k, v, name):
     tokens, width = k.shape
 
-    def body(k_ref, v_ref, x_out, y_out, done):
+    def body(k_ref, v_ref, out, done):
         copies = [
-            pltpu.make_async_copy(k_ref, x_out.at[:, pl.ds(0, width)], done.at[0]),
-            pltpu.make_async_copy(
-                v_ref.at[:, pl.ds(0, split)], x_out.at[:, pl.ds(width, split)], done.at[1]
-            ),
-            pltpu.make_async_copy(v_ref.at[:, pl.ds(split, width - split)], y_out, done.at[2]),
+            pltpu.make_async_copy(ref, out.at[:, pl.ds(at, width)], done.at[i])
+            for i, (ref, at) in enumerate(((k_ref, 0), (v_ref, width)))
         ]
         for copy in copies:
             copy.start()
@@ -324,48 +370,48 @@
 
     return pl.pallas_call(
         body,
-        out_shape=[
-            pltpu.VMEM((tokens, width + split), k.dtype),
-            pltpu.VMEM((tokens, width - split), k.dtype),
-        ],
+        out_shape=pltpu.VMEM((tokens, 2 * width), k.dtype),
         in_specs=[pl.BlockSpec(memory_space=pl.ANY)] * 2,
-        out_specs=[VMEM] * 2,
-        scratch_shapes=[pltpu.SemaphoreType.DMA((3,))],
+        out_specs=VMEM,
+        scratch_shapes=[pltpu.SemaphoreType.DMA((2,))],
         cost_estimate=COST,
         name=name,
     )(k, v)
 
 
-def added(first, second, name):
-    def body(first_ref, second_ref, out):
-        out[...] = first_ref[...] + second_ref[...]
-
-    return kernel_call(body, [jax.ShapeDtypeStruct(first.shape, first.dtype)], [first, second], name)[0]
-
-
-def added_parted(first, second, place, bit, name):
-    half = first.shape[0] // 2
-
-    def body(place_ref, first_ref, second_ref, kept, sent):
-        mine = (place_ref[0] >> bit) & 1
-        for out, at in ((kept, mine), (sent, 1 - mine)):
-            rows = pl.ds(pl.multiple_of(at * half, half), half)
-            out[...] = first_ref[rows, :] + second_ref[rows, :]
-
-    outs = [jax.ShapeDtypeStruct((half, first.shape[1]), first.dtype)] * 2
-    return kernel_call(body, outs, [place, first, second], name)
-
-
-def placed(own, far, place, bit, name):
-    half = own.shape[0]
-
-    def body(place_ref, own_ref, far_ref, out):
-        mine = (place_ref[0] >> bit) & 1
-        for ref, at in ((own_ref, mine), (far_ref, 1 - mine)):
-            out[pl.ds(pl.multiple_of(at * half, half), half), :] = ref[...]
-
-    outs = [jax.ShapeDtypeStruct((2 * half, own.shape[1]), own.dtype)]
-    return kernel_call(body, outs, [place, own, far], name)[0]
+def quarters(state, place, name):
+    rows = state.shape[0] // 4
+
+    def body(place_ref, ref, *outs):
+        mine = place_ref[0] & 3
+        for step, out in enumerate(outs):
+            at = pl.multiple_of((mine ^ step) * rows, rows)
+            out[...] = ref[pl.ds(at, rows), :]
+
+    outs = [jax.ShapeDtypeStruct((rows, state.shape[1]), state.dtype)] * 4
+    return kernel_call(body, outs, [place, state], name)
+
+
+def added(arrays, name):
+    def body(*refs):
+        total = functools.reduce(jnp.add, [ref[...].astype(jnp.float32) for ref in refs[:-1]])
+        refs[-1][...] = total.astype(refs[-1].dtype)
+
+    outs = [jax.ShapeDtypeStruct(arrays[0].shape, arrays[0].dtype)]
+    return kernel_call(body, outs, list(arrays), name)[0]
+
+
+def whole_state(parts, place, name):
+    rows = parts[0].shape[0]
+
+    def body(place_ref, *refs):
+        mine = place_ref[0] & 3
+        for step, ref in enumerate(refs[:-1]):
+            at = pl.multiple_of((mine ^ step) * rows, rows)
+            refs[-1][pl.ds(at, rows), :] = ref[...]
+
+    outs = [jax.ShapeDtypeStruct((4 * rows, parts[0].shape[1]), parts[0].dtype)]
+    return kernel_call(body, outs, [place] + list(parts), name)[0]
 
 
 def swapped(shard, axis, distance):
@@ -391,61 +437,58 @@
     pairs = width // PAIR
     split = pairs // 2 * PAIR
 
-    def k_of(x):
-        return [(x, 0, width)]
-
-    def v_of(x, y):
-        return [(x, width, split), (y, 0, width - split)]
-
     k, index, core = after((k, index, core))
-    x_own, y_own = packed(k, v, split, "values_packed")
-    x_1 = moved(x_own, first_steps)
-    k_near = [swapped(k, "seq", d) for d in (1, 2)]
+    k_1 = moved(k, first_steps)
+    state = key_state(whole(k), whole(v), feat, pairs)
+    kept, *sent = quarters(state, index, "state_quarters")
+    got = [swapped(part, "seq", d) for part, d in zip(sent, (1, 2, 3))]
+    got, k_next, v_next = after((got, k, v))
+    v_1 = moved(v_next, first_steps)
+    k_near = [swapped(k_next, "seq", d) for d in (1, 2)]
+    state = added([kept] + got, "state_plane")
+    state, k_1 = after((state, k_1))
+    got = swapped(state, "seq", 4)
     sums = attend(q, [(whole(k), whole(v))], None, "attend_own")
-    state = key_state(k, v, feat)
-
-    state, k_near, sums = after((state, k_near, sums))
-    kept, sent = parted(state, index, 1, 0, "state_parted")
-    kept, sent = added_parted(kept, swapped(sent, "seq", 2), index, 0, "state_second")
-    state = added(kept, swapped(sent, "seq", 1), "state_third")
-
-    state, v_next, y_own = after((state, v, y_own))
-    v_near = [swapped(v_next, "seq", d) for d in (1, 2)]
-    y_1 = moved(y_own, first_steps)
-    state = added(state, swapped(state, "seq", 4), "state_fourth")
-    state, x_1 = after((state, x_1))
-    far_state = swapped(state, "seq", 8)
-    x_2 = moved(x_1, second_steps)
-
-    y_1, far_state, x_own, y_own = after((y_1, far_state, x_own, y_own))
-    x_3 = moved(x_own, edge_steps)
-    sums = attend(q, [(k_of(x_1), v_of(x_1, y_1))], sums, "attend_first")
-    state = added(state, far_state, "state_summed")
-
-    v_near, y_1, y_own, sums, w, state = after((v_near, y_1, y_own, sums, w, state))
+    first = weigh(q, [[whole(k_1)]], "weigh_first")
+    first, w = after((first, w))
     w_own, w_sent = parted(w, core, 0, 1, "weights_parted")
     w_far = swapped(w_sent, "head", 1)
-    y_2 = moved(y_1, second_steps)
-    y_3 = moved(y_own, edge_steps)
-    state = placed(state, swapped(state, "seq", 1), index, 0, "state_joined")
-    near = [(whole(k_far), whole(v_far)) for k_far, v_far in zip(k_near, v_near)]
-    sums = attend(q, near, sums, "attend_near")
-    state, sums, w_far = after((state, sums, w_far))
-    state = placed(state, swapped(state, "seq", 2), index, 1, "state_whole")
-
+
+    got, k_1, k_near, v_1, w_far, sums, k_next, v_next = after(
+        (got, k_1, k_near, v_1, w_far, sums, k, v)
+    )
+    state = added([state, got], "state_line")
+    got = swapped(state, "seq", 8)
+    k_2 = moved(k_1, second_steps)
+    k_3 = moved(k_next, edge_steps)
+    v_near = [swapped(v_next, "seq", d) for d in (1, 2)]
+    everyone = range(pairs)
+    sums = gather(sums, first, [[whole(v_1)]], None, everyone, "gather_first")
+    near = weigh(q, [[whole(far)] for far in k_near], "weigh_near")
+
+    got, v_1, v_last, near, sums = after((got, v_1, v, near, sums))
+    v_2 = moved(v_1, second_steps)
+    v_3 = moved(v_last, edge_steps)
+    v_near, got, sums, near, k_2, k_3 = after((v_near, got, sums, near, k_2, k_3))
+    last = weigh(q, [[whole(k_2), whole(k_3)]], "weigh_last")
+    state = added([state, got], "state_summed")
+    got = [swapped(state, "seq", d) for d in (1, 2, 3)]
+    sums = gather(sums, near, [[whole(far)] for far in v_near], None, everyone, "gather_near")
+    got, sums, last = after((got, sums, last))
+    state = whole_state([state] + got, index, "state_whole")
     low = low_rank_rows(q, feat, state)
-    last = weigh(q, [k_of(x_2), k_of(x_3)], "weigh_last")
-    v_last = [v_of(x_2, y_2), v_of(x_3, y_3)]
-    rows_a = gather(sums, *last, v_last, low, range(0, pairs // 2), "gather_a")
+
+    v_last = [[whole(v_2), whole(v_3)]]
+    rows_a = gather(sums, last, v_last, low, range(0, pairs // 2), "gather_a")
     far_a = swapped(rows_a, "head", 1)
-    rows_b = gather(sums, *last, v_last, low, range(pairs // 2, pairs), "gather_b")
+    rows_b = gather(sums, last, v_last, low, range(pairs // 2, pairs), "gather_b")
     far_b = swapped(rows_b, "head", 1)
     acc = project(None, [(rows_a, w_own, 0), (far_a, w_far, 0), (rows_b, w_own, split)], "project_a")
     return project(acc, [(far_b, w_far, split)], "project_b")
 
 
 def chosen_distances(q, k, v, distances, feat, w):
-    state = key_state(k, v, feat).astype(jnp.float32)
+    state = key_state(whole(k), whole(v), feat, q.shape[1] // PAIR).astype(jnp.float32)
     state = lax.psum(state, "seq").astype(jnp.bfloat16)
     bits = lax.axis_size("seq").bit_length() - 1
     bit_ids = jnp.arange(bits, dtype=jnp.int32)
@@ -459,12 +502,10 @@
     sums = attend(q, [(whole(k), whole(v))], None, "attend_own")
     for partner in range(PARTNERS):
         picked = jnp.sum(jnp.where(distances[partner] == powers, bit_ids, 0))
-        k_far, v_far = lax.switch(picked, paths, (k, v))
+        far = [whole(x) for x in lax.switch(picked, paths, (k, v))]
         if partner < PARTNERS - 1:
-            sums = attend(q, [(whole(k_far), whole(v_far))], sums, "attend_far")
-    last = weigh(q, [whole(k_far)], "weigh_last")
-    pairs = range(q.shape[1] // PAIR)
-    rows = gather(sums, *last, [whole(v_far)], low, pairs, "gather_last")
+            sums = attend(q, [far], sums, "attend_far")
+    rows = finish(q, [far], sums, low, range(q.shape[1] // PAIR), "finish")
     part = jnp.dot(rows, w, preferred_element_type=jnp.float32)
     return lax.psum_scatter(part.astype(jnp.bfloat16), "head", scatter_dimension=1, tiled=True)
 

time: 70.8 us -> 66.8 us (0.944)
  waiting for transfers between devices: 19.9 us -> 11.8 us
  starting transfers between devices: 22.1 us -> 26.2 us
  local copies, waits for them, and re-layouts: 2.81 us -> 4.02 us
  Pallas kernels: 25 us -> 24.1 us
    ppermute x13 -> x15, waiting for transfers between devices: 19.9 us -> 9.11 us  [swapped(): lax.ppermute(shard, axis, [(i, i ^ distance) for i in range(lax.axis_size...]
    ppermute x6, waiting for transfers between devices: 0.02 us -> 2.72 us  [moved(): lax.ppermute(shard, 'seq', [(a * span + r, b * span + r) for a, b in step...]
    ppermute x13 -> x15, starting transfers between devices: 13.8 us -> 16.2 us  [swapped(): lax.ppermute(shard, axis, [(i, i ^ distance) for i in range(lax.axis_size...]
    ppermute x6, starting transfers between devices: 8.32 us -> 9.96 us  [moved(): lax.ppermute(shard, 'seq', [(a * span + r, b * span + r) for a, b in step...]
    unnamed x12, local copies, waits for them, and re-layouts: 2.81 us -> 4.02 us
    pallas_call x1 -> x0, Pallas kernels: 1.21 us -> none  [packed(): pl.pallas_call(body, out_shape=[pltpu.VMEM((tokens, width + split), k.dty...]
  transfers between devices with their start and end apart: 19 -> 21, of which waited for: 8 -> 9; matrix products, arithmetic and copies ran while one was open for 0% -> 0% of each run, Pallas kernels for 34% -> 33%
where the time goes in v3:
time: 66.8 us; the launch traced here: 66.4 us
  starting transfers between devices  26.2 us (39%)
  Pallas kernels  24.1 us (36%)
  waiting for transfers between devices  11.8 us (18%)
  local copies, waits for them, and re-layouts  4.02 us (6%)
    pallas_call x17, Pallas kernels, kernel_call(): pl.pallas_call(body, out_shape=[pltpu.VMEM(o.shape, o.dtype) for o in out...  23 us
    ppermute x15, starting transfers between devices, swapped(): lax.ppermute(shard, axis, [(i, i ^ distance) for i in range(lax.axis_size...  16.2 us
    ppermute x6, starting transfers between devices, moved(): lax.ppermute(shard, 'seq', [(a * span + r, b * span + r) for a, b in step...  9.96 us
    ppermute x15, waiting for transfers between devices, swapped(): lax.ppermute(shard, axis, [(i, i ^ distance) for i in range(lax.axis_size...  9.11 us
    unnamed x12, local copies, waits for them, and re-layouts  4.02 us
    ppermute x6, waiting for transfers between devices, moved(): lax.ppermute(shard, 'seq', [(a * span + r, b * span + r) for a, b in step...  2.72 us
  transfers between devices with their start and end apart: 21, of which 9 were waited for; matrix products, arithmetic and copies ran while one was open for 0% of the time, Pallas kernels for 33%

profile of v3, /device:TPU:0, one launch (start us, length us, event | category | flops | bytes accessed | tf_op | source)
XLA Modules:
  0.0 66.4 jit_solution(13969579391598332580)
XLA Ops:
  0.0 3.0 %collective-permute-start.3 = (bf16[512,512]{1,0:T(8,128)(2,1)}, bf16[512,512]{1,0:T(8,128)(2,1)S(1)}, u32[]{:S(2)}, u32[]{:S(2)}) collective-permute-start(bf16[512,512]{1,0:T(8,128)(2,1)} %refs_1_.2), channel_id=1, source_target_pairs={{8,24},{10,26},{12,28},{14,30},{16,0},{18,2},{20,4},{22,6},{0,8},{... | collective-permute-start | bytes 1572872 | tf_op jit(solution)/shard_map/ppermute | solution.py:423
  3.0 0.7 %copy-done.4 = bf16[64,128]{1,0:T(8,128)(2,1)S(1)} copy-done((bf16[64,128]{1,0:T(8,128)(2,1)S(1)}, bf16[64,128]{1,0:T(8,128)(2,1)}, u32[]{:S(2)}) %copy-start.4) | copy-done | bytes 16408
  3.7 3.5 %key_state.1.ref = bf16[640,128]{1,0:T(8,128)(2,1)S(1)} custom-call(bf16[512,512]{1,0:T(8,128)(2,1)} %refs_1_.2, bf16[512,512]{1,0:T(8,128)(2,1)} %refs_2_.3, bf16[64,128]{1,0:T(8,128)(2,1)S(1)} %copy-done.4), custom_call_target="tpu_custom_call" | custom-call | flops 1000 | tf_op jit(solution)/shard_map/key_state/pallas_call | solution.py:72
  7.3 1.6 %collective-permute-start = (bf16[160,128]{1,0:T(8,128)(2,1)S(1)}, bf16[160,128]{1,0:T(8,128)(2,1)S(1)}, u32[]{:S(2)}, u32[]{:S(2)}) collective-permute-start(bf16[160,128]{1,0:T(8,128)(2,1)S(1)} %get-tuple-element.79), channel_id=1, source_target_pairs={{0,2},{2,0},{4,6},{6,4},{8,10},{10,8},{12,14},{14,12},{16,18},{18,... | collective-permute-start | bytes 122888 | tf_op jit(solution)/shard_map/ppermute | solution.py:418
  8.8 1.5 %collective-permute-start.1 = (bf16[160,128]{1,0:T(8,128)(2,1)S(1)}, bf16[160,128]{1,0:T(8,128)(2,1)S(1)}, u32[]{:S(2)}, u32[]{:S(2)}) collective-permute-start(bf16[160,128]{1,0:T(8,128)(2,1)S(1)} %get-tuple-element.80), channel_id=1, source_target_pairs={{0,4},{2,6},{4,0},{6,2},{8,12},{10,14},{12,8},{14,10},{16,20},{18,... | collective-permute-start | bytes 122888 | tf_op jit(solution)/shard_map/ppermute | solution.py:418
  10.4 0.5 collective-permute-start.2
  10.8 0.5 collective-permute-done.refs_1_
  11.4 1.5 %collective-permute-done.1.refs_2_ = bf16[160,128]{1,0:T(8,128)(2,1)S(1)} collective-permute-done((bf16[160,128]{1,0:T(8,128)(2,1)S(1)}, bf16[160,128]{1,0:T(8,128)(2,1)S(1)}, u32[]{:S(2)}, u32[]{:S(2)}) %collective-permute-start.1) | collective-permute-done | bytes 40992 | tf_op jit(solution)/shard_map/ppermute | solution.py:418
  12.9 2.4 %collective-permute-done.2.refs_3_ = bf16[160,128]{1,0:T(8,128)(2,1)S(1)} collective-permute-done((bf16[160,128]{1,0:T(8,128)(2,1)S(1)}, bf16[160,128]{1,0:T(8,128)(2,1)S(1)}, u32[]{:S(2)}, u32[]{:S(2)}) %collective-permute-start.2) | collective-permute-done | bytes 40992 | tf_op jit(solution)/shard_map/ppermute | solution.py:418
  15.3 0.5 collective-permute-start.6
  15.8 0.5 collective-permute-start.5
  16.3 2.6 %collective-permute-start.7 = (bf16[512,512]{1,0:T(8,128)(2,1)}, bf16[512,512]{1,0:T(8,128)(2,1)S(1)}, u32[]{:S(2)}, u32[]{:S(2)}) collective-permute-start(bf16[512,512]{1,0:T(8,128)(2,1)} %refs_2_.3), channel_id=1, source_target_pairs={{8,24},{10,26},{12,28},{14,30},{16,0},{18,2},{20,4},{22,6},{0,8},{... | collective-permute-start | bytes 1572872 | tf_op jit(solution)/shard_map/ppermute | solution.py:423
  18.9 1.0 %copy-done = bf16[512,512]{1,0:T(8,128)(2,1)S(1)} copy-done((bf16[512,512]{1,0:T(8,128)(2,1)S(1)}, bf16[512,512]{1,0:T(8,128)(2,1)}, u32[]{:S(2)}) %copy-start) | copy-done | bytes 524312
  20.0 1.7 %weigh_first.1 = (bf16[512,4096]{1,0:T(8,128)(2,1)S(1)}, f32[512,512]{1,0:T(8,128)S(1)}) custom-call(bf16[512,512]{1,0:T(8,128)(2,1)S(1)} %copy-done, bf16[512,512]{1,0:T(8,128)(2,1)S(1)} %collective-permute-done.3.refs_1_), custom_call_target="tpu_custom_call" | custom-call | flops 1000 | tf_op jit(solution)/shard_map/weigh_first/pallas_call | solution.py:72
  21.7 0.0 copy-start.3
  21.7 1.2 %copy-done.3 = bf16[512,1024]{1,0:T(8,128)(2,1)S(1)} copy-done((bf16[512,1024]{1,0:T(8,128)(2,1)S(1)}, bf16[512,1024]{1,0:T(8,128)(2,1)}, u32[]{:S(2)}) %copy-start.3) | copy-done | bytes 1048600
  22.9 0.1 weights_parted.1
  23.0 0.1 collective-permute-start.8
  23.0 0.5 collective-permute-start.4
  23.6 1.0 %copy-done.1 = bf16[512,512]{1,0:T(8,128)(2,1)S(1)} copy-done((bf16[512,512]{1,0:T(8,128)(2,1)S(1)}, bf16[512,512]{1,0:T(8,128)(2,1)}, u32[]{:S(2)}) %copy-start.1) | copy-done | bytes 524312
  24.6 4.1 %attend_own.1 = (f32[512,512]{1,0:T(8,128)S(1)}, f32[512,512]{1,0:T(8,128)S(1)}, f32[512,512]{1,0:T(8,128)S(1)}) custom-call(bf16[512,512]{1,0:T(8,128)(2,1)S(1)} %copy-done.1, bf16[512,512]{1,0:T(8,128)(2,1)} %refs_1_.2, bf16[512,512]{1,0:T(8,128)(2,1)} %refs_2_.3), custom_call_target="tpu_custom_call" | custom-call | flops 1000 | tf_op jit(solution)/shard_map/attend_own/pallas_call | solution.py:72
  28.8 0.6 collective-permute-done.7.refs_5_
  29.4 0.8 %collective-permute-done.4.refs_1_ = bf16[160,128]{1,0:T(8,128)(2,1)S(1)} collective-permute-done((bf16[160,128]{1,0:T(8,128)(2,1)S(1)}, bf16[160,128]{1,0:T(8,128)(2,1)S(1)}, u32[]{:S(2)}, u32[]{:S(2)}) %collective-permute-start.4) | collective-permute-done | bytes 40992 | tf_op jit(solution)/shard_map/ppermute | solution.py:418
  30.1 0.7 %collective-permute-start.12 = (bf16[512,512]{1,0:T(8,128)(2,1)S(1)}, bf16[512,512]{1,0:T(8,128)(2,1)S(1)}, u32[]{:S(2)}, u32[]{:S(2)}) collective-permute-start(bf16[512,512]{1,0:T(8,128)(2,1)S(1)} %collective-permute-done.3.refs_1_), channel_id=1, source_target_pairs={{8,16},{10,18},{12,20},{14,22},{16,8},{18,10},{20,12},{22,14},{9,1... | collective-permute-start | bytes 1572872 | tf_op jit(solution)/shard_map/ppermute | solution.py:423
  30.8 1.5 %collective-permute-start.13 = (bf16[512,512]{1,0:T(8,128)(2,1)}, bf16[512,512]{1,0:T(8,128)(2,1)S(1)}, u32[]{:S(2)}, u32[]{:S(2)}) collective-permute-start(bf16[512,512]{1,0:T(8,128)(2,1)} %refs_1_.2), channel_id=1, source_target_pairs={{8,0},{10,2},{12,4},{14,6},{16,24},{18,26},{20,28},{22,30},{9,1},{... | collective-permute-start | bytes 1572872 | tf_op jit(solution)/shard_map/ppermute | solution.py:423
  32.3 1.6 %collective-permute-start.10 = (bf16[512,512]{1,0:T(8,128)(2,1)}, bf16[512,512]{1,0:T(8,128)(2,1)S(1)}, u32[]{:S(2)}, u32[]{:S(2)}) collective-permute-start(bf16[512,512]{1,0:T(8,128)(2,1)} %refs_2_.3), channel_id=1, source_target_pairs={{0,4},{2,6},{4,0},{6,2},{8,12},{10,14},{12,8},{14,10},{16,20},{18,... | collective-permute-start | bytes 1572872 | tf_op jit(solution)/shard_map/ppermute | solution.py:418
  33.9 1.1 %collective-permute-start.9 = (bf16[512,512]{1,0:T(8,128)(2,1)}, bf16[512,512]{1,0:T(8,128)(2,1)S(1)}, u32[]{:S(2)}, u32[]{:S(2)}) collective-permute-start(bf16[512,512]{1,0:T(8,128)(2,1)} %refs_2_.3), channel_id=1, source_target_pairs={{0,2},{2,0},{4,6},{6,4},{8,10},{10,8},{12,14},{14,12},{16,18},{18,... | collective-permute-start | bytes 1572872 | tf_op jit(solution)/shard_map/ppermute | solution.py:418
  35.0 4.2 %collective-permute-start.11 = (bf16[160,128]{1,0:T(8,128)(2,1)S(1)}, bf16[160,128]{1,0:T(8,128)(2,1)S(1)}, u32[]{:S(2)}, u32[]{:S(2)}) collective-permute-start(bf16[160,128]{1,0:T(8,128)(2,1)S(1)} %state_line.1.refs_0_), channel_id=1, source_target_pairs={{0,16},{2,18},{4,20},{6,22},{8,24},{10,26},{12,28},{14,30},{16,0},... | collective-permute-start | bytes 122888 | tf_op jit(solution)/shard_map/ppermute | solution.py:418
  39.2 3.7 %weigh_near.1 = (bf16[512,8192]{1,0:T(8,128)(2,1)S(1)}, f32[512,512]{1,0:T(8,128)S(1)}) custom-call(bf16[512,512]{1,0:T(8,128)(2,1)S(1)} %copy-done.2, bf16[512,512]{1,0:T(8,128)(2,1)S(1)} %collective-permute-done.5.refs_1_, bf16[512,512]{1,0:T(8,128)(2,1)S(1)} %collective-permute-done.6.refs_2_), custom_call_target="tpu_custom_call" | custom-call | flops 1000 | tf_op jit(solution)/shard_map/weigh_near/pallas_call | solution.py:72
  42.8 1.4 %gather_first.1 = (f32[512,512]{1,0:T(8,128)S(1)}, f32[512,512]{1,0:T(8,128)S(1)}, f32[512,512]{1,0:T(8,128)S(1)}) custom-call(f32[512,512]{1,0:T(8,128)S(1)} %get-tuple-element.104.refs_0_, f32[512,512]{1,0:T(8,128)S(1)} %get-tuple-element.105.refs_1_, f32[512,512]{1,0:T(8,128)S(1)} %get-tuple-element.106.refs_2_, ...), custom_call_target="tpu_custom_call" | custom-call | flops 1000 | tf_op jit(solution)/shard_map/gather_first/pallas_call | solution.py:72
  44.2 3.3 %collective-permute-done.11.refs_1_ = bf16[160,128]{1,0:T(8,128)(2,1)S(1)} collective-permute-done((bf16[160,128]{1,0:T(8,128)(2,1)S(1)}, bf16[160,128]{1,0:T(8,128)(2,1)S(1)}, u32[]{:S(2)}, u32[]{:S(2)}) %collective-permute-start.11) | collective-permute-done | bytes 40992 | tf_op jit(solution)/shard_map/ppermute | solution.py:418
  47.6 0.7 %collective-permute-start.17 = (bf16[512,512]{1,0:T(8,128)(2,1)S(1)}, bf16[512,512]{1,0:T(8,128)(2,1)S(1)}, u32[]{:S(2)}, u32[]{:S(2)}) collective-permute-start(bf16[512,512]{1,0:T(8,128)(2,1)S(1)} %collective-permute-done.7.refs_5_), channel_id=1, source_target_pairs={{8,16},{10,18},{12,20},{14,22},{16,8},{18,10},{20,12},{22,14},{9,1... | collective-permute-start | bytes 1572872 | tf_op jit(solution)/shard_map/ppermute | solution.py:423
  48.3 1.5 %collective-permute-start.18 = (bf16[512,512]{1,0:T(8,128)(2,1)}, bf16[512,512]{1,0:T(8,128)(2,1)S(1)}, u32[]{:S(2)}, u32[]{:S(2)}) collective-permute-start(bf16[512,512]{1,0:T(8,128)(2,1)} %refs_2_.3), channel_id=1, source_target_pairs={{8,0},{10,2},{12,4},{14,6},{16,24},{18,26},{20,28},{22,30},{9,1},{... | collective-permute-start | bytes 1572872 | tf_op jit(solution)/shard_map/ppermute | solution.py:423
  49.8 2.4 %collective-permute-start.16 = (bf16[160,128]{1,0:T(8,128)(2,1)S(1)}, bf16[160,128]{1,0:T(8,128)(2,1)S(1)}, u32[]{:S(2)}, u32[]{:S(2)}) collective-permute-start(bf16[160,128]{1,0:T(8,128)(2,1)S(1)} %state_summed.1.refs_0_), channel_id=1, source_target_pairs={{0,6},{2,4},{4,2},{6,0},{8,14},{10,12},{12,10},{14,8},{16,22},{18,... | collective-permute-start | bytes 122888 | tf_op jit(solution)/shard_map/ppermute | solution.py:418
  52.2 0.5 collective-permute-start.15
  52.8 0.6 collective-permute-start.14
  53.4 1.8 %weigh_last.1 = (bf16[512,4096]{1,0:T(8,128)(2,1)S(1)}, f32[512,512]{1,0:T(8,128)S(1)}) custom-call(bf16[512,512]{1,0:T(8,128)(2,1)S(1)} %copy-done.2, bf16[512,512]{1,0:T(8,128)(2,1)S(1)} %collective-permute-done.12.refs_1_, bf16[512,512]{1,0:T(8,128)(2,1)S(1)} %collective-permute-done.13.refs_2_), custom_call_target="tpu_custom_call" | custom-call | flops 1000 | tf_op jit(solution)/shard_map/weigh_last/pallas_call | solution.py:72
  55.2 2.5 %gather_near.1 = (f32[512,512]{1,0:T(8,128)S(1)}, f32[512,512]{1,0:T(8,128)S(1)}, f32[512,512]{1,0:T(8,128)S(1)}) custom-call(f32[512,512]{1,0:T(8,128)S(1)} %get-tuple-element.121.refs_0_, f32[512,512]{1,0:T(8,128)S(1)} %get-tuple-element.122.refs_1_, f32[512,512]{1,0:T(8,128)S(1)} %get-tuple-element.123.refs_2_, ...), custom_call_target="tpu_custom_call" | custom-call | flops 1000 | tf_op jit(solution)/shard_map/gather_near/pallas_call | solution.py:72
  57.8 1.9 %low_rank.1.refs_7_ = f32[512,512]{1,0:T(8,128)S(1)} custom-call(bf16[512,512]{1,0:T(8,128)(2,1)S(1)} %copy-done.2, bf16[64,128]{1,0:T(8,128)(2,1)S(1)} %copy-done.5, bf16[640,128]{1,0:T(8,128)(2,1)S(1)} %state_whole.1.state_ref), custom_call_target="tpu_custom_call" | custom-call | flops 1000 | tf_op jit(solution)/shard_map/low_rank/pallas_call | solution.py:72
  59.7 2.1 %collective-permute-done.18.refs_6_ = bf16[512,512]{1,0:T(8,128)(2,1)S(1)} collective-permute-done((bf16[512,512]{1,0:T(8,128)(2,1)}, bf16[512,512]{1,0:T(8,128)(2,1)S(1)}, u32[]{:S(2)}, u32[]{:S(2)}) %collective-permute-start.18) | collective-permute-done | bytes 524320 | tf_op jit(solution)/shard_map/ppermute | solution.py:423
  61.8 0.8 %gather_a.1.refs_0_ = bf16[512,256]{1,0:T(8,128)(2,1)S(1)} custom-call(f32[512,512]{1,0:T(8,128)S(1)} %get-tuple-element.135.refs_0_, f32[512,512]{1,0:T(8,128)S(1)} %get-tuple-element.136.refs_1_, f32[512,512]{1,0:T(8,128)S(1)} %get-tuple-element.137.refs_2_, bf16[512,4096]{1,0:T(8,128)(2,1)S(1)} %get-tuple-element.138.refs_3_, ...), custom_call_target="tpu_custom_call" | custom-call | flops 1000 | tf_op jit(solution)/shard_map/gather_a/pallas_call | solution.py:72
  62.6 0.1 collective-permute-start.20
  62.7 0.8 %gather_b.1.refs_4_ = bf16[512,256]{1,0:T(8,128)(2,1)S(1)} custom-call(f32[512,512]{1,0:T(8,128)S(1)} %get-tuple-element.135.refs_0_, f32[512,512]{1,0:T(8,128)S(1)} %get-tuple-element.136.refs_1_, f32[512,512]{1,0:T(8,128)S(1)} %get-tuple-element.137.refs_2_, bf16[512,4096]{1,0:T(8,128)(2,1)S(1)} %get-tuple-element.138.refs_3_, ...), custom_call_target="tpu_custom_call" | custom-call | flops 1000 | tf_op jit(solution)/shard_map/gather_b/pallas_call | solution.py:72
  63.5 0.6 collective-permute-start.19
  64.1 0.1 collective-permute-done.20.refs_2_
  64.2 0.6 project_a.1.refs_2_
  64.8 0.5 collective-permute-done.19.refs_0_
  65.3 1.1 %project_b.1 = bf16[512,512]{1,0:T(8,128)(2,1)} custom-call(bf16[512,256]{1,0:T(8,128)(2,1)S(1)} %collective-permute-done.19.refs_0_, bf16[512,512]{1,0:T(8,128)(2,1)S(1)} %collective-permute-done.8.refs_3_.refs_1_, f32[512,512]{1,0:T(8,128)S(1)} %project_a.1.refs_2_), custom_call_target="tpu_custom_call" | custom-call | flops 1000 | tf_op jit(solution)/shard_map/project_b/pallas_call | solution.py:332
  (24 shorter events, 0.1 us)
Async XLA Ops:
  0.0 39.1 %copy-start.2 = (bf16[512,512]{1,0:T(8,128)(2,1)S(1)}, bf16[512,512]{1,0:T(8,128)(2,1)}, u32[]{:S(2)}) copy-start(bf16[512,512]{1,0:T(8,128)(2,1)} %q_ref.1) | copy-start | bytes 1572868
  0.0 18.9 %collective-permute-start.3 = (bf16[512,512]{1,0:T(8,128)(2,1)}, bf16[512,512]{1,0:T(8,128)(2,1)S(1)}, u32[]{:S(2)}, u32[]{:S(2)}) collective-permute-start(bf16[512,512]{1,0:T(8,128)(2,1)} %refs_1_.2), channel_id=1, source_target_pairs={{8,24},{10,26},{12,28},{14,30},{16,0},{18,2},{20,4},{22,6},{0,8},{... | collective-permute-start | bytes 1572872 | tf_op jit(solution)/shard_map/ppermute | solution.py:423
  3.0 0.7 %copy-start.4 = (bf16[64,128]{1,0:T(8,128)(2,1)S(1)}, bf16[64,128]{1,0:T(8,128)(2,1)}, u32[]{:S(2)}) copy-start(bf16[64,128]{1,0:T(8,128)(2,1)} %feat_ref.1) | copy-start | bytes 49156
  7.3 4.1 %collective-permute-start = (bf16[160,128]{1,0:T(8,128)(2,1)S(1)}, bf16[160,128]{1,0:T(8,128)(2,1)S(1)}, u32[]{:S(2)}, u32[]{:S(2)}) collective-permute-start(bf16[160,128]{1,0:T(8,128)(2,1)S(1)} %get-tuple-element.79), channel_id=1, source_target_pairs={{0,2},{2,0},{4,6},{6,4},{8,10},{10,8},{12,14},{14,12},{16,18},{18,... | collective-permute-start | bytes 122888 | tf_op jit(solution)/shard_map/ppermute | solution.py:418
  8.8 4.0 %collective-permute-start.1 = (bf16[160,128]{1,0:T(8,128)(2,1)S(1)}, bf16[160,128]{1,0:T(8,128)(2,1)S(1)}, u32[]{:S(2)}, u32[]{:S(2)}) collective-permute-start(bf16[160,128]{1,0:T(8,128)(2,1)S(1)} %get-tuple-element.80), channel_id=1, source_target_pairs={{0,4},{2,6},{4,0},{6,2},{8,12},{10,14},{12,8},{14,10},{16,20},{18,... | collective-permute-start | bytes 122888 | tf_op jit(solution)/shard_map/ppermute | solution.py:418
  10.4 4.9 %collective-permute-start.2 = (bf16[160,128]{1,0:T(8,128)(2,1)S(1)}, bf16[160,128]{1,0:T(8,128)(2,1)S(1)}, u32[]{:S(2)}, u32[]{:S(2)}) collective-permute-start(bf16[160,128]{1,0:T(8,128)(2,1)S(1)} %get-tuple-element.81), channel_id=1, source_target_pairs={{0,6},{2,4},{4,2},{6,0},{8,14},{10,12},{12,10},{14,8},{16,22},{18,... | collective-permute-start | bytes 122888 | tf_op jit(solution)/shard_map/ppermute | solution.py:418
  15.3 14.1 %collective-permute-start.6 = (bf16[512,512]{1,0:T(8,128)(2,1)}, bf16[512,512]{1,0:T(8,128)(2,1)S(1)}, u32[]{:S(2)}, u32[]{:S(2)}) collective-permute-start(bf16[512,512]{1,0:T(8,128)(2,1)} %refs_1_.2), channel_id=1, source_target_pairs={{0,4},{2,6},{4,0},{6,2},{8,12},{10,14},{12,8},{14,10},{16,20},{18,... | collective-permute-start | bytes 1572872 | tf_op jit(solution)/shard_map/ppermute | solution.py:418
  15.8 13.6 %collective-permute-start.5 = (bf16[512,512]{1,0:T(8,128)(2,1)}, bf16[512,512]{1,0:T(8,128)(2,1)S(1)}, u32[]{:S(2)}, u32[]{:S(2)}) collective-permute-start(bf16[512,512]{1,0:T(8,128)(2,1)} %refs_1_.2), channel_id=1, source_target_pairs={{0,2},{2,0},{4,6},{6,4},{8,10},{10,8},{12,14},{14,12},{16,18},{18,... | collective-permute-start | bytes 1572872 | tf_op jit(solution)/shard_map/ppermute | solution.py:418
  16.3 13.0 %collective-permute-start.7 = (bf16[512,512]{1,0:T(8,128)(2,1)}, bf16[512,512]{1,0:T(8,128)(2,1)S(1)}, u32[]{:S(2)}, u32[]{:S(2)}) collective-permute-start(bf16[512,512]{1,0:T(8,128)(2,1)} %refs_2_.3), channel_id=1, source_target_pairs={{8,24},{10,26},{12,28},{14,30},{16,0},{18,2},{20,4},{22,6},{0,8},{... | collective-permute-start | bytes 1572872 | tf_op jit(solution)/shard_map/ppermute | solution.py:423
  18.9 1.0 %copy-start = (bf16[512,512]{1,0:T(8,128)(2,1)S(1)}, bf16[512,512]{1,0:T(8,128)(2,1)}, u32[]{:S(2)}) copy-start(bf16[512,512]{1,0:T(8,128)(2,1)} %q_ref.1) | copy-start | bytes 1572868
  21.7 1.2 %copy-start.3 = (bf16[512,1024]{1,0:T(8,128)(2,1)S(1)}, bf16[512,1024]{1,0:T(8,128)(2,1)}, u32[]{:S(2)}) copy-start(bf16[512,1024]{1,0:T(8,128)(2,1)} %ref) | copy-start | bytes 3145732
  23.0 7.2 %collective-permute-start.8 = (bf16[512,512]{1,0:T(8,128)(2,1)S(1)}, bf16[512,512]{1,0:T(8,128)(2,1)S(1)}, u32[]{:S(2)}, u32[]{:S(2)}) collective-permute-start(bf16[512,512]{1,0:T(8,128)(2,1)S(1)} %get-tuple-element.93), channel_id=1, source_target_pairs={{0,1},{1,0},{2,3},{3,2},{4,5},{5,4},{6,7},{7,6},{8,9},{9,8},{10,11... | collective-permute-start | bytes 1572872 | tf_op jit(solution)/shard_map/ppermute | solution.py:418
  23.0 7.1 %collective-permute-start.4 = (bf16[160,128]{1,0:T(8,128)(2,1)S(1)}, bf16[160,128]{1,0:T(8,128)(2,1)S(1)}, u32[]{:S(2)}, u32[]{:S(2)}) collective-permute-start(bf16[160,128]{1,0:T(8,128)(2,1)S(1)} %state_plane.1.refs_0_), channel_id=1, source_target_pairs={{0,8},{2,10},{4,12},{6,14},{8,0},{10,2},{12,4},{14,6},{16,24},{18,... | collective-permute-start | bytes 122888 | tf_op jit(solution)/shard_map/ppermute | solution.py:418
  23.6 1.0 %copy-start.1 = (bf16[512,512]{1,0:T(8,128)(2,1)S(1)}, bf16[512,512]{1,0:T(8,128)(2,1)}, u32[]{:S(2)}) copy-start(bf16[512,512]{1,0:T(8,128)(2,1)} %q_ref.1) | copy-start | bytes 1572868
  30.1 18.1 %collective-permute-start.12 = (bf16[512,512]{1,0:T(8,128)(2,1)S(1)}, bf16[512,512]{1,0:T(8,128)(2,1)S(1)}, u32[]{:S(2)}, u32[]{:S(2)}) collective-permute-start(bf16[512,512]{1,0:T(8,128)(2,1)S(1)} %collective-permute-done.3.refs_1_), channel_id=1, source_target_pairs={{8,16},{10,18},{12,20},{14,22},{16,8},{18,10},{20,12},{22,14},{9,1... | collective-permute-start | bytes 1572872 | tf_op jit(solution)/shard_map/ppermute | solution.py:423
  30.8 19.0 %collective-permute-start.13 = (bf16[512,512]{1,0:T(8,128)(2,1)}, bf16[512,512]{1,0:T(8,128)(2,1)S(1)}, u32[]{:S(2)}, u32[]{:S(2)}) collective-permute-start(bf16[512,512]{1,0:T(8,128)(2,1)} %refs_1_.2), channel_id=1, source_target_pairs={{8,0},{10,2},{12,4},{14,6},{16,24},{18,26},{20,28},{22,30},{9,1},{... | collective-permute-start | bytes 1572872 | tf_op jit(solution)/shard_map/ppermute | solution.py:423
  32.3 17.5 %collective-permute-start.10 = (bf16[512,512]{1,0:T(8,128)(2,1)}, bf16[512,512]{1,0:T(8,128)(2,1)S(1)}, u32[]{:S(2)}, u32[]{:S(2)}) collective-permute-start(bf16[512,512]{1,0:T(8,128)(2,1)} %refs_2_.3), channel_id=1, source_target_pairs={{0,4},{2,6},{4,0},{6,2},{8,12},{10,14},{12,8},{14,10},{16,20},{18,... | collective-permute-start | bytes 1572872 | tf_op jit(solution)/shard_map/ppermute | solution.py:418
  33.9 15.9 %collective-permute-start.9 = (bf16[512,512]{1,0:T(8,128)(2,1)}, bf16[512,512]{1,0:T(8,128)(2,1)S(1)}, u32[]{:S(2)}, u32[]{:S(2)}) collective-permute-start(bf16[512,512]{1,0:T(8,128)(2,1)} %refs_2_.3), channel_id=1, source_target_pairs={{0,2},{2,0},{4,6},{6,4},{8,10},{10,8},{12,14},{14,12},{16,18},{18,... | collective-permute-start | bytes 1572872 | tf_op jit(solution)/shard_map/ppermute | solution.py:418
  35.0 12.6 %collective-permute-start.11 = (bf16[160,128]{1,0:T(8,128)(2,1)S(1)}, bf16[160,128]{1,0:T(8,128)(2,1)S(1)}, u32[]{:S(2)}, u32[]{:S(2)}) collective-permute-start(bf16[160,128]{1,0:T(8,128)(2,1)S(1)} %state_line.1.refs_0_), channel_id=1, source_target_pairs={{0,16},{2,18},{4,20},{6,22},{8,24},{10,26},{12,28},{14,30},{16,0},... | collective-permute-start | bytes 122888 | tf_op jit(solution)/shard_map/ppermute | solution.py:418
  47.6 12.1 %collective-permute-start.17 = (bf16[512,512]{1,0:T(8,128)(2,1)S(1)}, bf16[512,512]{1,0:T(8,128)(2,1)S(1)}, u32[]{:S(2)}, u32[]{:S(2)}) collective-permute-start(bf16[512,512]{1,0:T(8,128)(2,1)S(1)} %collective-permute-done.7.refs_5_), channel_id=1, source_target_pairs={{8,16},{10,18},{12,20},{14,22},{16,8},{18,10},{20,12},{22,14},{9,1... | collective-permute-start | bytes 1572872 | tf_op jit(solution)/shard_map/ppermute | solution.py:423
  48.3 13.5 %collective-permute-start.18 = (bf16[512,512]{1,0:T(8,128)(2,1)}, bf16[512,512]{1,0:T(8,128)(2,1)S(1)}, u32[]{:S(2)}, u32[]{:S(2)}) collective-permute-start(bf16[512,512]{1,0:T(8,128)(2,1)} %refs_2_.3), channel_id=1, source_target_pairs={{8,0},{10,2},{12,4},{14,6},{16,24},{18,26},{20,28},{22,30},{9,1},{... | collective-permute-start | bytes 1572872 | tf_op jit(solution)/shard_map/ppermute | solution.py:423
  49.8 7.9 %collective-permute-start.16 = (bf16[160,128]{1,0:T(8,128)(2,1)S(1)}, bf16[160,128]{1,0:T(8,128)(2,1)S(1)}, u32[]{:S(2)}, u32[]{:S(2)}) collective-permute-start(bf16[160,128]{1,0:T(8,128)(2,1)S(1)} %state_summed.1.refs_0_), channel_id=1, source_target_pairs={{0,6},{2,4},{4,2},{6,0},{8,14},{10,12},{12,10},{14,8},{16,22},{18,... | collective-permute-start | bytes 122888 | tf_op jit(solution)/shard_map/ppermute | solution.py:418
  52.2 5.5 %collective-permute-start.15 = (bf16[160,128]{1,0:T(8,128)(2,1)S(1)}, bf16[160,128]{1,0:T(8,128)(2,1)S(1)}, u32[]{:S(2)}, u32[]{:S(2)}) collective-permute-start(bf16[160,128]{1,0:T(8,128)(2,1)S(1)} %state_summed.1.refs_0_), channel_id=1, source_target_pairs={{0,4},{2,6},{4,0},{6,2},{8,12},{10,14},{12,8},{14,10},{16,20},{18,... | collective-permute-start | bytes 122888 | tf_op jit(solution)/shard_map/ppermute | solution.py:418
  52.8 5.0 %collective-permute-start.14 = (bf16[160,128]{1,0:T(8,128)(2,1)S(1)}, bf16[160,128]{1,0:T(8,128)(2,1)S(1)}, u32[]{:S(2)}, u32[]{:S(2)}) collective-permute-start(bf16[160,128]{1,0:T(8,128)(2,1)S(1)} %state_summed.1.refs_0_), channel_id=1, source_target_pairs={{0,2},{2,0},{4,6},{6,4},{8,10},{10,8},{12,14},{14,12},{16,18},{18,... | collective-permute-start | bytes 122888 | tf_op jit(solution)/shard_map/ppermute | solution.py:418
  55.2 2.6 %copy-start.5 = (bf16[64,128]{1,0:T(8,128)(2,1)S(1)}, bf16[64,128]{1,0:T(8,128)(2,1)}, u32[]{:S(2)}) copy-start(bf16[64,128]{1,0:T(8,128)(2,1)} %feat_ref.1) | copy-start | bytes 49156
  62.6 1.6 %collective-permute-start.20 = (bf16[512,256]{1,0:T(8,128)(2,1)S(1)}, bf16[512,256]{1,0:T(8,128)(2,1)S(1)}, u32[]{:S(2)}, u32[]{:S(2)}) collective-permute-start(bf16[512,256]{1,0:T(8,128)(2,1)S(1)} %gather_a.1.refs_0_), channel_id=1, source_target_pairs={{0,1},{1,0},{2,3},{3,2},{4,5},{5,4},{6,7},{7,6},{8,9},{9,8},{10,11... | collective-permute-start | bytes 786440 | tf_op jit(solution)/shard_map/ppermute | solution.py:418
  63.5 1.7 %collective-permute-start.19 = (bf16[512,256]{1,0:T(8,128)(2,1)S(1)}, bf16[512,256]{1,0:T(8,128)(2,1)S(1)}, u32[]{:S(2)}, u32[]{:S(2)}) collective-permute-start(bf16[512,256]{1,0:T(8,128)(2,1)S(1)} %gather_b.1.refs_4_), channel_id=1, source_target_pairs={{0,1},{1,0},{2,3},{3,2},{4,5},{5,4},{6,7},{7,6},{8,9},{9,8},{10,11... | collective-permute-start | bytes 786440 | tf_op jit(solution)/shard_map/ppermute | solution.py:418

commit v4 on v3

--- a/solution.py
+++ b/solution.py
@@ -450,31 +450,32 @@
     got = swapped(state, "seq", 4)
     sums = attend(q, [(whole(k), whole(v))], None, "attend_own")
     first = weigh(q, [[whole(k_1)]], "weigh_first")
-    first, w = after((first, w))
+    first, w, v_next = after((first, w, v))
+    v_near = swapped(v_next, "seq", 1)
     w_own, w_sent = parted(w, core, 0, 1, "weights_parted")
-    w_far = swapped(w_sent, "head", 1)
-
-    got, k_1, k_near, v_1, w_far, sums, k_next, v_next = after(
-        (got, k_1, k_near, v_1, w_far, sums, k, v)
-    )
+
+    got, k_1, v_1, w_sent, sums, k_next, v_next = after((got, k_1, v_1, w_sent, sums, k, v))
     state = added([state, got], "state_line")
     got = swapped(state, "seq", 8)
     k_2 = moved(k_1, second_steps)
     k_3 = moved(k_next, edge_steps)
-    v_near = [swapped(v_next, "seq", d) for d in (1, 2)]
+    v_last = swapped(v_next, "seq", 2)
     everyone = range(pairs)
     sums = gather(sums, first, [[whole(v_1)]], None, everyone, "gather_first")
     near = weigh(q, [[whole(far)] for far in k_near], "weigh_near")
 
-    got, v_1, v_last, near, sums = after((got, v_1, v, near, sums))
+    got, v_1 = after((got, v_1))
     v_2 = moved(v_1, second_steps)
-    v_3 = moved(v_last, edge_steps)
+    v_next, near, sums, v_near = after((v, near, sums, v_near))
+    v_3 = moved(v_next, edge_steps)
+    v_near = [v_near, v_last]
     v_near, got, sums, near, k_2, k_3 = after((v_near, got, sums, near, k_2, k_3))
     last = weigh(q, [[whole(k_2), whole(k_3)]], "weigh_last")
     state = added([state, got], "state_summed")
     got = [swapped(state, "seq", d) for d in (1, 2, 3)]
     sums = gather(sums, near, [[whole(far)] for far in v_near], None, everyone, "gather_near")
-    got, sums, last = after((got, sums, last))
+    got, sums, last, w_sent = after((got, sums, last, w_sent))
+    w_far = swapped(w_sent, "head", 1)
     state = whole_state([state] + got, index, "state_whole")
     low = low_rank_rows(q, feat, state)
 

time: 66.8 us -> 66 us (0.988)
  waiting for transfers between devices: 11.8 us -> 14.6 us
  local copies, waits for them, and re-layouts: 4.02 us -> 1.77 us
  starting transfers between devices: 26.2 us -> 25 us
    ppermute x15, waiting for transfers between devices: 9.11 us -> 12.1 us  [swapped(): lax.ppermute(shard, axis, [(i, i ^ distance) for i in range(lax.axis_size...]
    unnamed x12 -> x10, local copies, waits for them, and re-layouts: 4.02 us -> 1.77 us
    ppermute x15, starting transfers between devices: 16.2 us -> 15 us  [swapped(): lax.ppermute(shard, axis, [(i, i ^ distance) for i in range(lax.axis_size...]
  transfers between devices with their start and end apart: 21 -> 21, of which waited for: 9 -> 10; matrix products, arithmetic and copies ran while one was open for 0% -> 0% of each run, Pallas kernels for 33% -> 35%
where the time goes in v4:
time: 66 us; the launch traced here: 65.7 us
  starting transfers between devices  25 us (38%)
  Pallas kernels  24.1 us (37%)
  waiting for transfers between devices  14.6 us (22%)
  local copies, waits for them, and re-layouts  1.77 us (3%)
    pallas_call x17, Pallas kernels, kernel_call(): pl.pallas_call(body, out_shape=[pltpu.VMEM(o.shape, o.dtype) for o in out...  23 us
    ppermute x15, starting transfers between devices, swapped(): lax.ppermute(shard, axis, [(i, i ^ distance) for i in range(lax.axis_size...  15 us
    ppermute x15, waiting for transfers between devices, swapped(): lax.ppermute(shard, axis, [(i, i ^ distance) for i in range(lax.axis_size...  12.1 us
    ppermute x6, starting transfers between devices, moved(): lax.ppermute(shard, 'seq', [(a * span + r, b * span + r) for a, b in step...  9.96 us
    ppermute x6, waiting for transfers between devices, moved(): lax.ppermute(shard, 'seq', [(a * span + r, b * span + r) for a, b in step...  2.55 us
    unnamed x10, local copies, waits for them, and re-layouts  1.77 us
  transfers between devices with their start and end apart: 21, of which 10 were waited for; matrix products, arithmetic and copies ran while one was open for 0% of the time, Pallas kernels for 35%

profile of v4, /device:TPU:0, one launch (start us, length us, event | category | flops | bytes accessed | tf_op | source)
XLA Modules:
  0.0 65.7 jit_solution(4689864236736760611)
XLA Ops:
  0.0 3.0 %collective-permute-start.3 = (bf16[512,512]{1,0:T(8,128)(2,1)}, bf16[512,512]{1,0:T(8,128)(2,1)S(1)}, u32[]{:S(2)}, u32[]{:S(2)}) collective-permute-start(bf16[512,512]{1,0:T(8,128)(2,1)} %refs_1_.2), channel_id=1, source_target_pairs={{8,24},{10,26},{12,28},{14,30},{16,0},{18,2},{20,4},{22,6},{0,8},{... | collective-permute-start | bytes 1572872 | tf_op jit(solution)/shard_map/ppermute | solution.py:423
  3.0 0.7 %copy-done.3 = bf16[64,128]{1,0:T(8,128)(2,1)S(1)} copy-done((bf16[64,128]{1,0:T(8,128)(2,1)S(1)}, bf16[64,128]{1,0:T(8,128)(2,1)}, u32[]{:S(2)}) %copy-start.3) | copy-done | bytes 16408
  3.7 3.5 %key_state.1.ref = bf16[640,128]{1,0:T(8,128)(2,1)S(1)} custom-call(bf16[512,512]{1,0:T(8,128)(2,1)} %refs_1_.2, bf16[512,512]{1,0:T(8,128)(2,1)} %refs_2_.3, bf16[64,128]{1,0:T(8,128)(2,1)S(1)} %copy-done.3), custom_call_target="tpu_custom_call" | custom-call | flops 1000 | tf_op jit(solution)/shard_map/key_state/pallas_call | solution.py:72
  7.3 1.6 %collective-permute-start = (bf16[160,128]{1,0:T(8,128)(2,1)S(1)}, bf16[160,128]{1,0:T(8,128)(2,1)S(1)}, u32[]{:S(2)}, u32[]{:S(2)}) collective-permute-start(bf16[160,128]{1,0:T(8,128)(2,1)S(1)} %get-tuple-element.80), channel_id=1, source_target_pairs={{0,2},{2,0},{4,6},{6,4},{8,10},{10,8},{12,14},{14,12},{16,18},{18,... | collective-permute-start | bytes 122888 | tf_op jit(solution)/shard_map/ppermute | solution.py:418
  8.8 1.5 %collective-permute-start.1 = (bf16[160,128]{1,0:T(8,128)(2,1)S(1)}, bf16[160,128]{1,0:T(8,128)(2,1)S(1)}, u32[]{:S(2)}, u32[]{:S(2)}) collective-permute-start(bf16[160,128]{1,0:T(8,128)(2,1)S(1)} %get-tuple-element.81), channel_id=1, source_target_pairs={{0,4},{2,6},{4,0},{6,2},{8,12},{10,14},{12,8},{14,10},{16,20},{18,... | collective-permute-start | bytes 122888 | tf_op jit(solution)/shard_map/ppermute | solution.py:418
  10.4 0.5 collective-permute-start.2
  10.8 0.5 collective-permute-done.refs_1_
  11.4 1.5 %collective-permute-done.1.refs_2_ = bf16[160,128]{1,0:T(8,128)(2,1)S(1)} collective-permute-done((bf16[160,128]{1,0:T(8,128)(2,1)S(1)}, bf16[160,128]{1,0:T(8,128)(2,1)S(1)}, u32[]{:S(2)}, u32[]{:S(2)}) %collective-permute-start.1) | collective-permute-done | bytes 40992 | tf_op jit(solution)/shard_map/ppermute | solution.py:418
  12.9 2.4 %collective-permute-done.2.refs_3_ = bf16[160,128]{1,0:T(8,128)(2,1)S(1)} collective-permute-done((bf16[160,128]{1,0:T(8,128)(2,1)S(1)}, bf16[160,128]{1,0:T(8,128)(2,1)S(1)}, u32[]{:S(2)}, u32[]{:S(2)}) %collective-permute-start.2) | collective-permute-done | bytes 40992 | tf_op jit(solution)/shard_map/ppermute | solution.py:418
  15.3 2.6 %collective-permute-start.5 = (bf16[512,512]{1,0:T(8,128)(2,1)}, bf16[512,512]{1,0:T(8,128)(2,1)S(1)}, u32[]{:S(2)}, u32[]{:S(2)}) collective-permute-start(bf16[512,512]{1,0:T(8,128)(2,1)} %refs_2_.3), channel_id=1, source_target_pairs={{8,24},{10,26},{12,28},{14,30},{16,0},{18,2},{20,4},{22,6},{0,8},{... | collective-permute-start | bytes 1572872 | tf_op jit(solution)/shard_map/ppermute | solution.py:423
  17.9 0.5 collective-permute-start.7
  18.4 0.5 collective-permute-start.6
  18.9 0.0 copy-start
  18.9 1.0 %copy-done = bf16[512,512]{1,0:T(8,128)(2,1)S(1)} copy-done((bf16[512,512]{1,0:T(8,128)(2,1)S(1)}, bf16[512,512]{1,0:T(8,128)(2,1)}, u32[]{:S(2)}) %copy-start) | copy-done | bytes 524312
  20.0 1.7 %weigh_first.1 = (bf16[512,4096]{1,0:T(8,128)(2,1)S(1)}, f32[512,512]{1,0:T(8,128)S(1)}) custom-call(bf16[512,512]{1,0:T(8,128)(2,1)S(1)} %copy-done, bf16[512,512]{1,0:T(8,128)(2,1)S(1)} %collective-permute-done.3.refs_1_), custom_call_target="tpu_custom_call" | custom-call | flops 1000 | tf_op jit(solution)/shard_map/weigh_first/pallas_call | solution.py:72
  21.7 1.6 %collective-permute-start.8 = (bf16[512,512]{1,0:T(8,128)(2,1)}, bf16[512,512]{1,0:T(8,128)(2,1)S(1)}, u32[]{:S(2)}, u32[]{:S(2)}) collective-permute-start(bf16[512,512]{1,0:T(8,128)(2,1)} %refs_2_.3), channel_id=1, source_target_pairs={{0,2},{2,0},{4,6},{6,4},{8,10},{10,8},{12,14},{14,12},{16,18},{18,... | collective-permute-start | bytes 1572872 | tf_op jit(solution)/shard_map/ppermute | solution.py:418
  23.2 0.5 collective-permute-start.4
  23.7 4.1 %attend_own.1 = (f32[512,512]{1,0:T(8,128)S(1)}, f32[512,512]{1,0:T(8,128)S(1)}, f32[512,512]{1,0:T(8,128)S(1)}) custom-call(bf16[512,512]{1,0:T(8,128)(2,1)S(1)} %copy-done, bf16[512,512]{1,0:T(8,128)(2,1)} %refs_1_.2, bf16[512,512]{1,0:T(8,128)(2,1)} %refs_2_.3), custom_call_target="tpu_custom_call" | custom-call | flops 1000 | tf_op jit(solution)/shard_map/attend_own/pallas_call | solution.py:72
  27.8 0.1 weights_parted.1
  27.9 0.5 collective-permute-done.5.refs_5_
  28.4 0.8 %collective-permute-done.4.refs_1_ = bf16[160,128]{1,0:T(8,128)(2,1)S(1)} collective-permute-done((bf16[160,128]{1,0:T(8,128)(2,1)S(1)}, bf16[160,128]{1,0:T(8,128)(2,1)S(1)}, u32[]{:S(2)}, u32[]{:S(2)}) %collective-permute-start.4) | collective-permute-done | bytes 40992 | tf_op jit(solution)/shard_map/ppermute | solution.py:418
  29.2 0.6 collective-permute-start.9
  29.9 0.7 %collective-permute-start.11 = (bf16[512,512]{1,0:T(8,128)(2,1)S(1)}, bf16[512,512]{1,0:T(8,128)(2,1)S(1)}, u32[]{:S(2)}, u32[]{:S(2)}) collective-permute-start(bf16[512,512]{1,0:T(8,128)(2,1)S(1)} %collective-permute-done.3.refs_1_), channel_id=1, source_target_pairs={{8,16},{10,18},{12,20},{14,22},{16,8},{18,10},{20,12},{22,14},{9,1... | collective-permute-start | bytes 1572872 | tf_op jit(solution)/shard_map/ppermute | solution.py:423
  30.6 1.5 %collective-permute-start.12 = (bf16[512,512]{1,0:T(8,128)(2,1)}, bf16[512,512]{1,0:T(8,128)(2,1)S(1)}, u32[]{:S(2)}, u32[]{:S(2)}) collective-permute-start(bf16[512,512]{1,0:T(8,128)(2,1)} %refs_1_.2), channel_id=1, source_target_pairs={{8,0},{10,2},{12,4},{14,6},{16,24},{18,26},{20,28},{22,30},{9,1},{... | collective-permute-start | bytes 1572872 | tf_op jit(solution)/shard_map/ppermute | solution.py:423
  32.1 1.4 %collective-permute-done.6.refs_1_ = bf16[512,512]{1,0:T(8,128)(2,1)S(1)} collective-permute-done((bf16[512,512]{1,0:T(8,128)(2,1)}, bf16[512,512]{1,0:T(8,128)(2,1)S(1)}, u32[]{:S(2)}, u32[]{:S(2)}) %collective-permute-start.6) | collective-permute-done | bytes 524320 | tf_op jit(solution)/shard_map/ppermute | solution.py:418
  33.4 3.5 %collective-permute-start.10 = (bf16[160,128]{1,0:T(8,128)(2,1)S(1)}, bf16[160,128]{1,0:T(8,128)(2,1)S(1)}, u32[]{:S(2)}, u32[]{:S(2)}) collective-permute-start(bf16[160,128]{1,0:T(8,128)(2,1)S(1)} %state_line.1.refs_0_), channel_id=1, source_target_pairs={{0,16},{2,18},{4,20},{6,22},{8,24},{10,26},{12,28},{14,30},{16,0},... | collective-permute-start | bytes 122888 | tf_op jit(solution)/shard_map/ppermute | solution.py:418
  37.0 1.4 %gather_first.1 = (f32[512,512]{1,0:T(8,128)S(1)}, f32[512,512]{1,0:T(8,128)S(1)}, f32[512,512]{1,0:T(8,128)S(1)}) custom-call(f32[512,512]{1,0:T(8,128)S(1)} %get-tuple-element.101.refs_0_, f32[512,512]{1,0:T(8,128)S(1)} %get-tuple-element.102.refs_1_, f32[512,512]{1,0:T(8,128)S(1)} %get-tuple-element.103.refs_2_, ...), custom_call_target="tpu_custom_call" | custom-call | flops 1000 | tf_op jit(solution)/shard_map/gather_first/pallas_call | solution.py:72
  38.4 3.7 %weigh_near.1 = (bf16[512,8192]{1,0:T(8,128)(2,1)S(1)}, f32[512,512]{1,0:T(8,128)S(1)}) custom-call(bf16[512,512]{1,0:T(8,128)(2,1)S(1)} %copy-done.1, bf16[512,512]{1,0:T(8,128)(2,1)S(1)} %collective-permute-done.6.refs_1_, bf16[512,512]{1,0:T(8,128)(2,1)S(1)} %collective-permute-done.7.refs_2_), custom_call_target="tpu_custom_call" | custom-call | flops 1000 | tf_op jit(solution)/shard_map/weigh_near/pallas_call | solution.py:72
  42.1 4.9 %collective-permute-done.10.refs_1_ = bf16[160,128]{1,0:T(8,128)(2,1)S(1)} collective-permute-done((bf16[160,128]{1,0:T(8,128)(2,1)S(1)}, bf16[160,128]{1,0:T(8,128)(2,1)S(1)}, u32[]{:S(2)}, u32[]{:S(2)}) %collective-permute-start.10) | collective-permute-done | bytes 40992 | tf_op jit(solution)/shard_map/ppermute | solution.py:418
  47.0 0.7 %collective-permute-start.16 = (bf16[512,512]{1,0:T(8,128)(2,1)S(1)}, bf16[512,512]{1,0:T(8,128)(2,1)S(1)}, u32[]{:S(2)}, u32[]{:S(2)}) collective-permute-start(bf16[512,512]{1,0:T(8,128)(2,1)S(1)} %collective-permute-done.5.refs_5_), channel_id=1, source_target_pairs={{8,16},{10,18},{12,20},{14,22},{16,8},{18,10},{20,12},{22,14},{9,1... | collective-permute-start | bytes 1572872 | tf_op jit(solution)/shard_map/ppermute | solution.py:423
  47.7 1.5 %collective-permute-start.17 = (bf16[512,512]{1,0:T(8,128)(2,1)}, bf16[512,512]{1,0:T(8,128)(2,1)S(1)}, u32[]{:S(2)}, u32[]{:S(2)}) collective-permute-start(bf16[512,512]{1,0:T(8,128)(2,1)} %refs_2_.3), channel_id=1, source_target_pairs={{8,0},{10,2},{12,4},{14,6},{16,24},{18,26},{20,28},{22,30},{9,1},{... | collective-permute-start | bytes 1572872 | tf_op jit(solution)/shard_map/ppermute | solution.py:423
  49.3 1.5 %collective-permute-start.15 = (bf16[160,128]{1,0:T(8,128)(2,1)S(1)}, bf16[160,128]{1,0:T(8,128)(2,1)S(1)}, u32[]{:S(2)}, u32[]{:S(2)}) collective-permute-start(bf16[160,128]{1,0:T(8,128)(2,1)S(1)} %state_summed.1.refs_0_), channel_id=1, source_target_pairs={{0,6},{2,4},{4,2},{6,0},{8,14},{10,12},{12,10},{14,8},{16,22},{18,... | collective-permute-start | bytes 122888 | tf_op jit(solution)/shard_map/ppermute | solution.py:418
  50.8 1.5 %collective-permute-start.14 = (bf16[160,128]{1,0:T(8,128)(2,1)S(1)}, bf16[160,128]{1,0:T(8,128)(2,1)S(1)}, u32[]{:S(2)}, u32[]{:S(2)}) collective-permute-start(bf16[160,128]{1,0:T(8,128)(2,1)S(1)} %state_summed.1.refs_0_), channel_id=1, source_target_pairs={{0,4},{2,6},{4,0},{6,2},{8,12},{10,14},{12,8},{14,10},{16,20},{18,... | collective-permute-start | bytes 122888 | tf_op jit(solution)/shard_map/ppermute | solution.py:418
  52.3 0.5 collective-permute-start.13
  52.8 1.7 %weigh_last.1 = (bf16[512,4096]{1,0:T(8,128)(2,1)S(1)}, f32[512,512]{1,0:T(8,128)S(1)}) custom-call(bf16[512,512]{1,0:T(8,128)(2,1)S(1)} %copy-done.1, bf16[512,512]{1,0:T(8,128)(2,1)S(1)} %collective-permute-done.11.refs_1_, bf16[512,512]{1,0:T(8,128)(2,1)S(1)} %collective-permute-done.12.refs_2_), custom_call_target="tpu_custom_call" | custom-call | flops 1000 | tf_op jit(solution)/shard_map/weigh_last/pallas_call | solution.py:72
  54.6 0.0 copy-start.4
  54.6 2.5 %gather_near.1 = (f32[512,512]{1,0:T(8,128)S(1)}, f32[512,512]{1,0:T(8,128)S(1)}, f32[512,512]{1,0:T(8,128)S(1)}) custom-call(f32[512,512]{1,0:T(8,128)S(1)} %get-tuple-element.122.refs_0_, f32[512,512]{1,0:T(8,128)S(1)} %get-tuple-element.123.refs_1_, f32[512,512]{1,0:T(8,128)S(1)} %get-tuple-element.124.refs_2_, ...), custom_call_target="tpu_custom_call" | custom-call | flops 1000 | tf_op jit(solution)/shard_map/gather_near/pallas_call | solution.py:72
  57.1 0.1 collective-permute-start.19
  57.2 1.9 %low_rank.1.refs_7_ = f32[512,512]{1,0:T(8,128)S(1)} custom-call(bf16[512,512]{1,0:T(8,128)(2,1)S(1)} %copy-done.1, bf16[64,128]{1,0:T(8,128)(2,1)S(1)} %copy-done.4, bf16[640,128]{1,0:T(8,128)(2,1)S(1)} %state_whole.1.state_ref), custom_call_target="tpu_custom_call" | custom-call | flops 1000 | tf_op jit(solution)/shard_map/low_rank/pallas_call | solution.py:72
  59.1 2.0 %collective-permute-done.17.refs_6_ = bf16[512,512]{1,0:T(8,128)(2,1)S(1)} collective-permute-done((bf16[512,512]{1,0:T(8,128)(2,1)}, bf16[512,512]{1,0:T(8,128)(2,1)S(1)}, u32[]{:S(2)}, u32[]{:S(2)}) %collective-permute-start.17) | collective-permute-done | bytes 524320 | tf_op jit(solution)/shard_map/ppermute | solution.py:423
  61.1 0.8 %gather_a.1.refs_0_ = bf16[512,256]{1,0:T(8,128)(2,1)S(1)} custom-call(f32[512,512]{1,0:T(8,128)S(1)} %get-tuple-element.137.refs_0_, f32[512,512]{1,0:T(8,128)S(1)} %get-tuple-element.138.refs_1_, f32[512,512]{1,0:T(8,128)S(1)} %get-tuple-element.139.refs_2_, bf16[512,4096]{1,0:T(8,128)(2,1)S(1)} %get-tuple-element.140.refs_3_, ...), custom_call_target="tpu_custom_call" | custom-call | flops 1000 | tf_op jit(solution)/shard_map/gather_a/pallas_call | solution.py:72
  62.0 0.1 collective-permute-start.20
  62.1 0.8 %gather_b.1.refs_4_ = bf16[512,256]{1,0:T(8,128)(2,1)S(1)} custom-call(f32[512,512]{1,0:T(8,128)S(1)} %get-tuple-element.137.refs_0_, f32[512,512]{1,0:T(8,128)S(1)} %get-tuple-element.138.refs_1_, f32[512,512]{1,0:T(8,128)S(1)} %get-tuple-element.139.refs_2_, bf16[512,4096]{1,0:T(8,128)(2,1)S(1)} %get-tuple-element.140.refs_3_, ...), custom_call_target="tpu_custom_call" | custom-call | flops 1000 | tf_op jit(solution)/shard_map/gather_b/pallas_call | solution.py:72
  62.9 0.6 collective-permute-start.18
  63.5 0.1 collective-permute-done.20.refs_2_
  63.6 0.6 project_a.1.refs_2_
  64.1 0.5 collective-permute-done.18.refs_0_
  64.6 1.1 %project_b.1 = bf16[512,512]{1,0:T(8,128)(2,1)} custom-call(bf16[512,256]{1,0:T(8,128)(2,1)S(1)} %collective-permute-done.18.refs_0_, bf16[512,512]{1,0:T(8,128)(2,1)S(1)} %collective-permute-done.19.refs_3_.refs_1_, f32[512,512]{1,0:T(8,128)S(1)} %project_a.1.refs_2_), custom_call_target="tpu_custom_call" | custom-call | flops 1000 | tf_op jit(solution)/shard_map/project_b/pallas_call | solution.py:332
  (22 shorter events, 0.1 us)
Async XLA Ops:
  0.0 27.8 %copy-start.2 = (bf16[512,1024]{1,0:T(8,128)(2,1)S(1)}, bf16[512,1024]{1,0:T(8,128)(2,1)}, u32[]{:S(2)}) copy-start(bf16[512,1024]{1,0:T(8,128)(2,1)} %ref) | copy-start | bytes 3145732
  0.0 18.9 %collective-permute-start.3 = (bf16[512,512]{1,0:T(8,128)(2,1)}, bf16[512,512]{1,0:T(8,128)(2,1)S(1)}, u32[]{:S(2)}, u32[]{:S(2)}) collective-permute-start(bf16[512,512]{1,0:T(8,128)(2,1)} %refs_1_.2), channel_id=1, source_target_pairs={{8,24},{10,26},{12,28},{14,30},{16,0},{18,2},{20,4},{22,6},{0,8},{... | collective-permute-start | bytes 1572872 | tf_op jit(solution)/shard_map/ppermute | solution.py:423
  3.0 0.7 %copy-start.3 = (bf16[64,128]{1,0:T(8,128)(2,1)S(1)}, bf16[64,128]{1,0:T(8,128)(2,1)}, u32[]{:S(2)}) copy-start(bf16[64,128]{1,0:T(8,128)(2,1)} %feat_ref.1) | copy-start | bytes 49156
  7.3 4.1 %collective-permute-start = (bf16[160,128]{1,0:T(8,128)(2,1)S(1)}, bf16[160,128]{1,0:T(8,128)(2,1)S(1)}, u32[]{:S(2)}, u32[]{:S(2)}) collective-permute-start(bf16[160,128]{1,0:T(8,128)(2,1)S(1)} %get-tuple-element.80), channel_id=1, source_target_pairs={{0,2},{2,0},{4,6},{6,4},{8,10},{10,8},{12,14},{14,12},{16,18},{18,... | collective-permute-start | bytes 122888 | tf_op jit(solution)/shard_map/ppermute | solution.py:418
  8.8 4.0 %collective-permute-start.1 = (bf16[160,128]{1,0:T(8,128)(2,1)S(1)}, bf16[160,128]{1,0:T(8,128)(2,1)S(1)}, u32[]{:S(2)}, u32[]{:S(2)}) collective-permute-start(bf16[160,128]{1,0:T(8,128)(2,1)S(1)} %get-tuple-element.81), channel_id=1, source_target_pairs={{0,4},{2,6},{4,0},{6,2},{8,12},{10,14},{12,8},{14,10},{16,20},{18,... | collective-permute-start | bytes 122888 | tf_op jit(solution)/shard_map/ppermute | solution.py:418
  10.4 4.9 %collective-permute-start.2 = (bf16[160,128]{1,0:T(8,128)(2,1)S(1)}, bf16[160,128]{1,0:T(8,128)(2,1)S(1)}, u32[]{:S(2)}, u32[]{:S(2)}) collective-permute-start(bf16[160,128]{1,0:T(8,128)(2,1)S(1)} %get-tuple-element.82), channel_id=1, source_target_pairs={{0,6},{2,4},{4,2},{6,0},{8,14},{10,12},{12,10},{14,8},{16,22},{18,... | collective-permute-start | bytes 122888 | tf_op jit(solution)/shard_map/ppermute | solution.py:418
  15.3 13.2 %collective-permute-start.5 = (bf16[512,512]{1,0:T(8,128)(2,1)}, bf16[512,512]{1,0:T(8,128)(2,1)S(1)}, u32[]{:S(2)}, u32[]{:S(2)}) collective-permute-start(bf16[512,512]{1,0:T(8,128)(2,1)} %refs_2_.3), channel_id=1, source_target_pairs={{8,24},{10,26},{12,28},{14,30},{16,0},{18,2},{20,4},{22,6},{0,8},{... | collective-permute-start | bytes 1572872 | tf_op jit(solution)/shard_map/ppermute | solution.py:423
  17.9 12.7 %collective-permute-start.7 = (bf16[512,512]{1,0:T(8,128)(2,1)}, bf16[512,512]{1,0:T(8,128)(2,1)S(1)}, u32[]{:S(2)}, u32[]{:S(2)}) collective-permute-start(bf16[512,512]{1,0:T(8,128)(2,1)} %refs_1_.2), channel_id=1, source_target_pairs={{0,4},{2,6},{4,0},{6,2},{8,12},{10,14},{12,8},{14,10},{16,20},{18,... | collective-permute-start | bytes 1572872 | tf_op jit(solution)/shard_map/ppermute | solution.py:418
  18.4 15.1 %collective-permute-start.6 = (bf16[512,512]{1,0:T(8,128)(2,1)}, bf16[512,512]{1,0:T(8,128)(2,1)S(1)}, u32[]{:S(2)}, u32[]{:S(2)}) collective-permute-start(bf16[512,512]{1,0:T(8,128)(2,1)} %refs_1_.2), channel_id=1, source_target_pairs={{0,2},{2,0},{4,6},{6,4},{8,10},{10,8},{12,14},{14,12},{16,18},{18,... | collective-permute-start | bytes 1572872 | tf_op jit(solution)/shard_map/ppermute | solution.py:418
  18.9 1.0 %copy-start = (bf16[512,512]{1,0:T(8,128)(2,1)S(1)}, bf16[512,512]{1,0:T(8,128)(2,1)}, u32[]{:S(2)}) copy-start(bf16[512,512]{1,0:T(8,128)(2,1)} %q_ref.1) | copy-start | bytes 1572868
  21.7 26.0 %collective-permute-start.8 = (bf16[512,512]{1,0:T(8,128)(2,1)}, bf16[512,512]{1,0:T(8,128)(2,1)S(1)}, u32[]{:S(2)}, u32[]{:S(2)}) collective-permute-start(bf16[512,512]{1,0:T(8,128)(2,1)} %refs_2_.3), channel_id=1, source_target_pairs={{0,2},{2,0},{4,6},{6,4},{8,10},{10,8},{12,14},{14,12},{16,18},{18,... | collective-permute-start | bytes 1572872 | tf_op jit(solution)/shard_map/ppermute | solution.py:418
  23.2 6.0 %collective-permute-start.4 = (bf16[160,128]{1,0:T(8,128)(2,1)S(1)}, bf16[160,128]{1,0:T(8,128)(2,1)S(1)}, u32[]{:S(2)}, u32[]{:S(2)}) collective-permute-start(bf16[160,128]{1,0:T(8,128)(2,1)S(1)} %state_plane.1.refs_0_), channel_id=1, source_target_pairs={{0,8},{2,10},{4,12},{6,14},{8,0},{10,2},{12,4},{14,6},{16,24},{18,... | collective-permute-start | bytes 122888 | tf_op jit(solution)/shard_map/ppermute | solution.py:418
  29.2 20.0 %collective-permute-start.9 = (bf16[512,512]{1,0:T(8,128)(2,1)}, bf16[512,512]{1,0:T(8,128)(2,1)S(1)}, u32[]{:S(2)}, u32[]{:S(2)}) collective-permute-start(bf16[512,512]{1,0:T(8,128)(2,1)} %refs_2_.3), channel_id=1, source_target_pairs={{0,4},{2,6},{4,0},{6,2},{8,12},{10,14},{12,8},{14,10},{16,20},{18,... | collective-permute-start | bytes 1572872 | tf_op jit(solution)/shard_map/ppermute | solution.py:418
  29.9 19.4 %collective-permute-start.11 = (bf16[512,512]{1,0:T(8,128)(2,1)S(1)}, bf16[512,512]{1,0:T(8,128)(2,1)S(1)}, u32[]{:S(2)}, u32[]{:S(2)}) collective-permute-start(bf16[512,512]{1,0:T(8,128)(2,1)S(1)} %collective-permute-done.3.refs_1_), channel_id=1, source_target_pairs={{8,16},{10,18},{12,20},{14,22},{16,8},{18,10},{20,12},{22,14},{9,1... | collective-permute-start | bytes 1572872 | tf_op jit(solution)/shard_map/ppermute | solution.py:423
  30.6 18.7 %collective-permute-start.12 = (bf16[512,512]{1,0:T(8,128)(2,1)}, bf16[512,512]{1,0:T(8,128)(2,1)S(1)}, u32[]{:S(2)}, u32[]{:S(2)}) collective-permute-start(bf16[512,512]{1,0:T(8,128)(2,1)} %refs_1_.2), channel_id=1, source_target_pairs={{8,0},{10,2},{12,4},{14,6},{16,24},{18,26},{20,28},{22,30},{9,1},{... | collective-permute-start | bytes 1572872 | tf_op jit(solution)/shard_map/ppermute | solution.py:423
  32.1 6.3 %copy-start.1 = (bf16[512,512]{1,0:T(8,128)(2,1)S(1)}, bf16[512,512]{1,0:T(8,128)(2,1)}, u32[]{:S(2)}) copy-start(bf16[512,512]{1,0:T(8,128)(2,1)} %q_ref.1) | copy-start | bytes 1572868
  33.4 13.5 %collective-permute-start.10 = (bf16[160,128]{1,0:T(8,128)(2,1)S(1)}, bf16[160,128]{1,0:T(8,128)(2,1)S(1)}, u32[]{:S(2)}, u32[]{:S(2)}) collective-permute-start(bf16[160,128]{1,0:T(8,128)(2,1)S(1)} %state_line.1.refs_0_), channel_id=1, source_target_pairs={{0,16},{2,18},{4,20},{6,22},{8,24},{10,26},{12,28},{14,30},{16,0},... | collective-permute-start | bytes 122888 | tf_op jit(solution)/shard_map/ppermute | solution.py:418
  47.0 12.1 %collective-permute-start.16 = (bf16[512,512]{1,0:T(8,128)(2,1)S(1)}, bf16[512,512]{1,0:T(8,128)(2,1)S(1)}, u32[]{:S(2)}, u32[]{:S(2)}) collective-permute-start(bf16[512,512]{1,0:T(8,128)(2,1)S(1)} %collective-permute-done.5.refs_5_), channel_id=1, source_target_pairs={{8,16},{10,18},{12,20},{14,22},{16,8},{18,10},{20,12},{22,14},{9,1... | collective-permute-start | bytes 1572872 | tf_op jit(solution)/shard_map/ppermute | solution.py:423
  47.7 13.5 %collective-permute-start.17 = (bf16[512,512]{1,0:T(8,128)(2,1)}, bf16[512,512]{1,0:T(8,128)(2,1)S(1)}, u32[]{:S(2)}, u32[]{:S(2)}) collective-permute-start(bf16[512,512]{1,0:T(8,128)(2,1)} %refs_2_.3), channel_id=1, source_target_pairs={{8,0},{10,2},{12,4},{14,6},{16,24},{18,26},{20,28},{22,30},{9,1},{... | collective-permute-start | bytes 1572872 | tf_op jit(solution)/shard_map/ppermute | solution.py:423
  49.3 7.8 %collective-permute-start.15 = (bf16[160,128]{1,0:T(8,128)(2,1)S(1)}, bf16[160,128]{1,0:T(8,128)(2,1)S(1)}, u32[]{:S(2)}, u32[]{:S(2)}) collective-permute-start(bf16[160,128]{1,0:T(8,128)(2,1)S(1)} %state_summed.1.refs_0_), channel_id=1, source_target_pairs={{0,6},{2,4},{4,2},{6,0},{8,14},{10,12},{12,10},{14,8},{16,22},{18,... | collective-permute-start | bytes 122888 | tf_op jit(solution)/shard_map/ppermute | solution.py:418
  50.8 6.3 %collective-permute-start.14 = (bf16[160,128]{1,0:T(8,128)(2,1)S(1)}, bf16[160,128]{1,0:T(8,128)(2,1)S(1)}, u32[]{:S(2)}, u32[]{:S(2)}) collective-permute-start(bf16[160,128]{1,0:T(8,128)(2,1)S(1)} %state_summed.1.refs_0_), channel_id=1, source_target_pairs={{0,4},{2,6},{4,0},{6,2},{8,12},{10,14},{12,8},{14,10},{16,20},{18,... | collective-permute-start | bytes 122888 | tf_op jit(solution)/shard_map/ppermute | solution.py:418
  52.3 4.8 %collective-permute-start.13 = (bf16[160,128]{1,0:T(8,128)(2,1)S(1)}, bf16[160,128]{1,0:T(8,128)(2,1)S(1)}, u32[]{:S(2)}, u32[]{:S(2)}) collective-permute-start(bf16[160,128]{1,0:T(8,128)(2,1)S(1)} %state_summed.1.refs_0_), channel_id=1, source_target_pairs={{0,2},{2,0},{4,6},{6,4},{8,10},{10,8},{12,14},{14,12},{16,18},{18,... | collective-permute-start | bytes 122888 | tf_op jit(solution)/shard_map/ppermute | solution.py:418
  54.6 2.7 %copy-start.4 = (bf16[64,128]{1,0:T(8,128)(2,1)S(1)}, bf16[64,128]{1,0:T(8,128)(2,1)}, u32[]{:S(2)}) copy-start(bf16[64,128]{1,0:T(8,128)(2,1)} %feat_ref.1) | copy-start | bytes 49156
  57.1 6.4 %collective-permute-start.19 = (bf16[512,512]{1,0:T(8,128)(2,1)S(1)}, bf16[512,512]{1,0:T(8,128)(2,1)S(1)}, u32[]{:S(2)}, u32[]{:S(2)}) collective-permute-start(bf16[512,512]{1,0:T(8,128)(2,1)S(1)} %get-tuple-element.147), channel_id=1, source_target_pairs={{0,1},{1,0},{2,3},{3,2},{4,5},{5,4},{6,7},{7,6},{8,9},{9,8},{10,11... | collective-permute-start | bytes 1572872 | tf_op jit(solution)/shard_map/ppermute | solution.py:418
  62.0 1.6 %collective-permute-start.20 = (bf16[512,256]{1,0:T(8,128)(2,1)S(1)}, bf16[512,256]{1,0:T(8,128)(2,1)S(1)}, u32[]{:S(2)}, u32[]{:S(2)}) collective-permute-start(bf16[512,256]{1,0:T(8,128)(2,1)S(1)} %gather_a.1.refs_0_), channel_id=1, source_target_pairs={{0,1},{1,0},{2,3},{3,2},{4,5},{5,4},{6,7},{7,6},{8,9},{9,8},{10,11... | collective-permute-start | bytes 786440 | tf_op jit(solution)/shard_map/ppermute | solution.py:418
  62.9 1.7 %collective-permute-start.18 = (bf16[512,256]{1,0:T(8,128)(2,1)S(1)}, bf16[512,256]{1,0:T(8,128)(2,1)S(1)}, u32[]{:S(2)}, u32[]{:S(2)}) collective-permute-start(bf16[512,256]{1,0:T(8,128)(2,1)S(1)} %gather_b.1.refs_4_), channel_id=1, source_target_pairs={{0,1},{1,0},{2,3},{3,2},{4,5},{5,4},{6,7},{7,6},{8,9},{9,8},{10,11... | collective-permute-start | bytes 786440 | tf_op jit(solution)/shard_map/ppermute | solution.py:418

commit v5 on v4

--- a/solution.py
+++ b/solution.py
@@ -241,12 +241,31 @@
                 return refs[index][:, first + at:first + at + PAIR]
             at -= count
 
+    count = len(arrays) + 1
+
     def body(*refs):
-        feat_ref, out = refs[-2:]
+        out, done = refs[count], refs[-1]
+        copies = []
+        for c in range(pairs):
+            part = pl.ds(c * PAIR, PAIR)
+            copies.append([
+                pltpu.make_async_copy(refs[i].at[:, part], refs[count + 1 + i].at[:, part], done.at[i, c])
+                for i in range(count - 1)
+            ])
+        copies[0].append(pltpu.make_async_copy(refs[count - 1], refs[2 * count], done.at[count - 1, 0]))
+        for group in copies:
+            for copy in group:
+                copy.start()
+        for copy in copies[0]:
+            copy.wait()
+        refs = refs[count + 1:-1]
+        feat_ref = refs[-1]
         feat_t = twice(feat_ref[...].astype(jnp.float32)).T.astype(jnp.bfloat16)
         lane = lax.broadcasted_iota(jnp.int32, (features, PAIR), 1)
         norms = jnp.zeros((features, PAIR), jnp.float32)
         for c in range(pairs):
+            for copy in copies[c] if c else []:
+                copy.wait()
             k_pair, v_pair = pair_of(refs, k, c), pair_of(refs, v, c)
             k_float = k_pair.astype(jnp.float32)
             square = k_float * k_float
@@ -276,7 +295,18 @@
         out[pairs * features:, :] = norms.astype(jnp.bfloat16)
 
     outs = jax.ShapeDtypeStruct((state_rows(pairs, features), PAIR), jnp.bfloat16)
-    return kernel_call(body, [outs], arrays + [feat], "key_state")[0]
+    args = arrays + [feat]
+    return pl.pallas_call(
+        body,
+        out_shape=pltpu.VMEM(outs.shape, outs.dtype),
+        in_specs=[pl.BlockSpec(memory_space=pl.ANY)] * count,
+        out_specs=VMEM,
+        scratch_shapes=[pltpu.VMEM(x.shape, x.dtype) for x in args]
+        + [pltpu.SemaphoreType.DMA((count, pairs))],
+        compiler_params=pltpu.CompilerParams(vmem_limit_bytes=VMEM_LIMIT),
+        cost_estimate=COST,
+        name="key_state",
+    )(*args)
 
 
 def low_rank_rows(q, feat, state):

time: 66 us -> 65.6 us (level)
  starting transfers between devices: 25 us -> 24.3 us
    pallas_call x0 -> x1, Pallas kernels: none -> 4.06 us  [key_state(): pl.pallas_call(body, out_shape=pltpu.VMEM(outs.shape, outs.dtype), in_spe...]
    pallas_call x17 -> x16, Pallas kernels: 23 us -> 19.5 us  [kernel_call(): pl.pallas_call(body, out_shape=[pltpu.VMEM(o.shape, o.dtype) for o in out...]
    ppermute x15, starting transfers between devices: 15 us -> 14.3 us  [swapped(): lax.ppermute(shard, axis, [(i, i ^ distance) for i in range(lax.axis_size...]
  transfers between devices with their start and end apart: 21 -> 21, of which waited for: 10 -> 10; matrix products, arithmetic and copies ran while one was open for 0% -> 0% of each run, Pallas kernels for 35% -> 36%
where the time goes in v5:
time: 65.6 us; the launch traced here: 65.3 us
  Pallas kernels  24.6 us (38%)
  starting transfers between devices  24.3 us (37%)
  waiting for transfers between devices  14.3 us (22%)
  local copies, waits for them, and re-layouts  1.77 us (3%)
    pallas_call x16, Pallas kernels, kernel_call(): pl.pallas_call(body, out_shape=[pltpu.VMEM(o.shape, o.dtype) for o in out...  19.5 us
    ppermute x15, starting transfers between devices, swapped(): lax.ppermute(shard, axis, [(i, i ^ distance) for i in range(lax.axis_size...  14.3 us
    ppermute x15, waiting for transfers between devices, swapped(): lax.ppermute(shard, axis, [(i, i ^ distance) for i in range(lax.axis_size...  12.2 us
    ppermute x6, starting transfers between devices, moved(): lax.ppermute(shard, 'seq', [(a * span + r, b * span + r) for a, b in step...  9.96 us
    pallas_call x1, Pallas kernels, key_state(): pl.pallas_call(body, out_shape=pltpu.VMEM(outs.shape, outs.dtype), in_spe...  4.06 us
    ppermute x6, waiting for transfers between devices, moved(): lax.ppermute(shard, 'seq', [(a * span + r, b * span + r) for a, b in step...  2.16 us
    unnamed x10, local copies, waits for them, and re-layouts  1.77 us
  transfers between devices with their start and end apart: 21, of which 10 were waited for; matrix products, arithmetic and copies ran while one was open for 0% of the time, Pallas kernels for 36%

profile of v5, /device:TPU:0, one launch (start us, length us, event | category | flops | bytes accessed | tf_op | source)
XLA Modules:
  0.0 65.3 jit_solution(9655357955645822539)
XLA Ops:
  0.0 3.0 %collective-permute-start.3 = (bf16[512,512]{1,0:T(8,128)(2,1)}, bf16[512,512]{1,0:T(8,128)(2,1)S(1)}, u32[]{:S(2)}, u32[]{:S(2)}) collective-permute-start(bf16[512,512]{1,0:T(8,128)(2,1)} %refs_1_.2), channel_id=1, source_target_pairs={{8,24},{10,26},{12,28},{14,30},{16,0},{18,2},{20,4},{22,6},{0,8},{... | collective-permute-start | bytes 1572872 | tf_op jit(solution)/shard_map/ppermute | solution.py:453
  3.0 0.7 %copy-done.3 = bf16[64,128]{1,0:T(8,128)(2,1)S(1)} copy-done((bf16[64,128]{1,0:T(8,128)(2,1)S(1)}, bf16[64,128]{1,0:T(8,128)(2,1)}, u32[]{:S(2)}) %copy-start.3) | copy-done | bytes 16408
  3.7 4.1 %key_state.1.ref = bf16[640,128]{1,0:T(8,128)(2,1)S(1)} custom-call(bf16[512,512]{1,0:T(8,128)(2,1)} %refs_1_.2, bf16[512,512]{1,0:T(8,128)(2,1)} %refs_2_.3, bf16[64,128]{1,0:T(8,128)(2,1)S(1)} %copy-done.3), custom_call_target="tpu_custom_call" | custom-call | flops 1000 | tf_op jit(solution)/shard_map/key_state/pallas_call | solution.py:299
  7.8 1.6 %collective-permute-start = (bf16[160,128]{1,0:T(8,128)(2,1)S(1)}, bf16[160,128]{1,0:T(8,128)(2,1)S(1)}, u32[]{:S(2)}, u32[]{:S(2)}) collective-permute-start(bf16[160,128]{1,0:T(8,128)(2,1)S(1)} %get-tuple-element.80), channel_id=1, source_target_pairs={{0,2},{2,0},{4,6},{6,4},{8,10},{10,8},{12,14},{14,12},{16,18},{18,... | collective-permute-start | bytes 122888 | tf_op jit(solution)/shard_map/ppermute | solution.py:448
  9.4 1.5 %collective-permute-start.1 = (bf16[160,128]{1,0:T(8,128)(2,1)S(1)}, bf16[160,128]{1,0:T(8,128)(2,1)S(1)}, u32[]{:S(2)}, u32[]{:S(2)}) collective-permute-start(bf16[160,128]{1,0:T(8,128)(2,1)S(1)} %get-tuple-element.81), channel_id=1, source_target_pairs={{0,4},{2,6},{4,0},{6,2},{8,12},{10,14},{12,8},{14,10},{16,20},{18,... | collective-permute-start | bytes 122888 | tf_op jit(solution)/shard_map/ppermute | solution.py:448
  10.9 0.5 collective-permute-start.2
  11.4 0.5 collective-permute-done.refs_1_
  11.9 1.5 %collective-permute-done.1.refs_2_ = bf16[160,128]{1,0:T(8,128)(2,1)S(1)} collective-permute-done((bf16[160,128]{1,0:T(8,128)(2,1)S(1)}, bf16[160,128]{1,0:T(8,128)(2,1)S(1)}, u32[]{:S(2)}, u32[]{:S(2)}) %collective-permute-start.1) | collective-permute-done | bytes 40992 | tf_op jit(solution)/shard_map/ppermute | solution.py:448
  13.4 2.4 %collective-permute-done.2.refs_3_ = bf16[160,128]{1,0:T(8,128)(2,1)S(1)} collective-permute-done((bf16[160,128]{1,0:T(8,128)(2,1)S(1)}, bf16[160,128]{1,0:T(8,128)(2,1)S(1)}, u32[]{:S(2)}, u32[]{:S(2)}) %collective-permute-start.2) | collective-permute-done | bytes 40992 | tf_op jit(solution)/shard_map/ppermute | solution.py:448
  15.8 2.6 %collective-permute-start.5 = (bf16[512,512]{1,0:T(8,128)(2,1)}, bf16[512,512]{1,0:T(8,128)(2,1)S(1)}, u32[]{:S(2)}, u32[]{:S(2)}) collective-permute-start(bf16[512,512]{1,0:T(8,128)(2,1)} %refs_2_.3), channel_id=1, source_target_pairs={{8,24},{10,26},{12,28},{14,30},{16,0},{18,2},{20,4},{22,6},{0,8},{... | collective-permute-start | bytes 1572872 | tf_op jit(solution)/shard_map/ppermute | solution.py:453
  18.4 0.5 collective-permute-start.7
  18.9 0.5 collective-permute-start.6
  19.5 1.0 %copy-done = bf16[512,512]{1,0:T(8,128)(2,1)S(1)} copy-done((bf16[512,512]{1,0:T(8,128)(2,1)S(1)}, bf16[512,512]{1,0:T(8,128)(2,1)}, u32[]{:S(2)}) %copy-start) | copy-done | bytes 524312
  20.5 1.7 %weigh_first.1 = (bf16[512,4096]{1,0:T(8,128)(2,1)S(1)}, f32[512,512]{1,0:T(8,128)S(1)}) custom-call(bf16[512,512]{1,0:T(8,128)(2,1)S(1)} %copy-done, bf16[512,512]{1,0:T(8,128)(2,1)S(1)} %collective-permute-done.3.refs_1_), custom_call_target="tpu_custom_call" | custom-call | flops 1000 | tf_op jit(solution)/shard_map/weigh_first/pallas_call | solution.py:72
  22.2 1.6 %collective-permute-start.8 = (bf16[512,512]{1,0:T(8,128)(2,1)}, bf16[512,512]{1,0:T(8,128)(2,1)S(1)}, u32[]{:S(2)}, u32[]{:S(2)}) collective-permute-start(bf16[512,512]{1,0:T(8,128)(2,1)} %refs_2_.3), channel_id=1, source_target_pairs={{0,2},{2,0},{4,6},{6,4},{8,10},{10,8},{12,14},{14,12},{16,18},{18,... | collective-permute-start | bytes 1572872 | tf_op jit(solution)/shard_map/ppermute | solution.py:448
  23.8 0.5 collective-permute-start.4
  24.2 4.1 %attend_own.1 = (f32[512,512]{1,0:T(8,128)S(1)}, f32[512,512]{1,0:T(8,128)S(1)}, f32[512,512]{1,0:T(8,128)S(1)}) custom-call(bf16[512,512]{1,0:T(8,128)(2,1)S(1)} %copy-done, bf16[512,512]{1,0:T(8,128)(2,1)} %refs_1_.2, bf16[512,512]{1,0:T(8,128)(2,1)} %refs_2_.3), custom_call_target="tpu_custom_call" | custom-call | flops 1000 | tf_op jit(solution)/shard_map/attend_own/pallas_call | solution.py:72
  28.4 0.1 weights_parted.1
  28.5 0.5 collective-permute-done.5.refs_5_
  29.0 0.8 %collective-permute-done.4.refs_1_ = bf16[160,128]{1,0:T(8,128)(2,1)S(1)} collective-permute-done((bf16[160,128]{1,0:T(8,128)(2,1)S(1)}, bf16[160,128]{1,0:T(8,128)(2,1)S(1)}, u32[]{:S(2)}, u32[]{:S(2)}) %collective-permute-start.4) | collective-permute-done | bytes 40992 | tf_op jit(solution)/shard_map/ppermute | solution.py:448
  29.8 0.5 collective-permute-start.9
  30.3 0.7 %collective-permute-start.11 = (bf16[512,512]{1,0:T(8,128)(2,1)S(1)}, bf16[512,512]{1,0:T(8,128)(2,1)S(1)}, u32[]{:S(2)}, u32[]{:S(2)}) collective-permute-start(bf16[512,512]{1,0:T(8,128)(2,1)S(1)} %collective-permute-done.3.refs_1_), channel_id=1, source_target_pairs={{8,16},{10,18},{12,20},{14,22},{16,8},{18,10},{20,12},{22,14},{9,1... | collective-permute-start | bytes 1572872 | tf_op jit(solution)/shard_map/ppermute | solution.py:453
  31.0 1.5 %collective-permute-start.12 = (bf16[512,512]{1,0:T(8,128)(2,1)}, bf16[512,512]{1,0:T(8,128)(2,1)S(1)}, u32[]{:S(2)}, u32[]{:S(2)}) collective-permute-start(bf16[512,512]{1,0:T(8,128)(2,1)} %refs_1_.2), channel_id=1, source_target_pairs={{8,0},{10,2},{12,4},{14,6},{16,24},{18,26},{20,28},{22,30},{9,1},{... | collective-permute-start | bytes 1572872 | tf_op jit(solution)/shard_map/ppermute | solution.py:453
  32.5 0.0 copy-start.1
  32.5 1.5 %collective-permute-done.6.refs_1_ = bf16[512,512]{1,0:T(8,128)(2,1)S(1)} collective-permute-done((bf16[512,512]{1,0:T(8,128)(2,1)}, bf16[512,512]{1,0:T(8,128)(2,1)S(1)}, u32[]{:S(2)}, u32[]{:S(2)}) %collective-permute-start.6) | collective-permute-done | bytes 524320 | tf_op jit(solution)/shard_map/ppermute | solution.py:448
  34.0 3.0 %collective-permute-start.10 = (bf16[160,128]{1,0:T(8,128)(2,1)S(1)}, bf16[160,128]{1,0:T(8,128)(2,1)S(1)}, u32[]{:S(2)}, u32[]{:S(2)}) collective-permute-start(bf16[160,128]{1,0:T(8,128)(2,1)S(1)} %state_line.1.refs_0_), channel_id=1, source_target_pairs={{0,16},{2,18},{4,20},{6,22},{8,24},{10,26},{12,28},{14,30},{16,0},... | collective-permute-start | bytes 122888 | tf_op jit(solution)/shard_map/ppermute | solution.py:448
  37.0 1.4 %gather_first.1 = (f32[512,512]{1,0:T(8,128)S(1)}, f32[512,512]{1,0:T(8,128)S(1)}, f32[512,512]{1,0:T(8,128)S(1)}) custom-call(f32[512,512]{1,0:T(8,128)S(1)} %get-tuple-element.101.refs_0_, f32[512,512]{1,0:T(8,128)S(1)} %get-tuple-element.102.refs_1_, f32[512,512]{1,0:T(8,128)S(1)} %get-tuple-element.103.refs_2_, ...), custom_call_target="tpu_custom_call" | custom-call | flops 1000 | tf_op jit(solution)/shard_map/gather_first/pallas_call | solution.py:72
  38.4 3.7 %weigh_near.1 = (bf16[512,8192]{1,0:T(8,128)(2,1)S(1)}, f32[512,512]{1,0:T(8,128)S(1)}) custom-call(bf16[512,512]{1,0:T(8,128)(2,1)S(1)} %copy-done.1, bf16[512,512]{1,0:T(8,128)(2,1)S(1)} %collective-permute-done.6.refs_1_, bf16[512,512]{1,0:T(8,128)(2,1)S(1)} %collective-permute-done.7.refs_2_), custom_call_target="tpu_custom_call" | custom-call | flops 1000 | tf_op jit(solution)/shard_map/weigh_near/pallas_call | solution.py:72
  42.1 4.9 %collective-permute-done.10.refs_1_ = bf16[160,128]{1,0:T(8,128)(2,1)S(1)} collective-permute-done((bf16[160,128]{1,0:T(8,128)(2,1)S(1)}, bf16[160,128]{1,0:T(8,128)(2,1)S(1)}, u32[]{:S(2)}, u32[]{:S(2)}) %collective-permute-start.10) | collective-permute-done | bytes 40992 | tf_op jit(solution)/shard_map/ppermute | solution.py:448
  47.0 0.7 %collective-permute-start.16 = (bf16[512,512]{1,0:T(8,128)(2,1)S(1)}, bf16[512,512]{1,0:T(8,128)(2,1)S(1)}, u32[]{:S(2)}, u32[]{:S(2)}) collective-permute-start(bf16[512,512]{1,0:T(8,128)(2,1)S(1)} %collective-permute-done.5.refs_5_), channel_id=1, source_target_pairs={{8,16},{10,18},{12,20},{14,22},{16,8},{18,10},{20,12},{22,14},{9,1... | collective-permute-start | bytes 1572872 | tf_op jit(solution)/shard_map/ppermute | solution.py:453
  47.7 1.5 %collective-permute-start.17 = (bf16[512,512]{1,0:T(8,128)(2,1)}, bf16[512,512]{1,0:T(8,128)(2,1)S(1)}, u32[]{:S(2)}, u32[]{:S(2)}) collective-permute-start(bf16[512,512]{1,0:T(8,128)(2,1)} %refs_2_.3), channel_id=1, source_target_pairs={{8,0},{10,2},{12,4},{14,6},{16,24},{18,26},{20,28},{22,30},{9,1},{... | collective-permute-start | bytes 1572872 | tf_op jit(solution)/shard_map/ppermute | solution.py:453
  49.3 1.5 %collective-permute-start.15 = (bf16[160,128]{1,0:T(8,128)(2,1)S(1)}, bf16[160,128]{1,0:T(8,128)(2,1)S(1)}, u32[]{:S(2)}, u32[]{:S(2)}) collective-permute-start(bf16[160,128]{1,0:T(8,128)(2,1)S(1)} %state_summed.1.refs_0_), channel_id=1, source_target_pairs={{0,6},{2,4},{4,2},{6,0},{8,14},{10,12},{12,10},{14,8},{16,22},{18,... | collective-permute-start | bytes 122888 | tf_op jit(solution)/shard_map/ppermute | solution.py:448
  50.7 1.5 %collective-permute-start.14 = (bf16[160,128]{1,0:T(8,128)(2,1)S(1)}, bf16[160,128]{1,0:T(8,128)(2,1)S(1)}, u32[]{:S(2)}, u32[]{:S(2)}) collective-permute-start(bf16[160,128]{1,0:T(8,128)(2,1)S(1)} %state_summed.1.refs_0_), channel_id=1, source_target_pairs={{0,4},{2,6},{4,0},{6,2},{8,12},{10,14},{12,8},{14,10},{16,20},{18,... | collective-permute-start | bytes 122888 | tf_op jit(solution)/shard_map/ppermute | solution.py:448
  52.3 0.5 collective-permute-start.13
  52.8 1.7 %weigh_last.1 = (bf16[512,4096]{1,0:T(8,128)(2,1)S(1)}, f32[512,512]{1,0:T(8,128)S(1)}) custom-call(bf16[512,512]{1,0:T(8,128)(2,1)S(1)} %copy-done.1, bf16[512,512]{1,0:T(8,128)(2,1)S(1)} %collective-permute-done.11.refs_1_, bf16[512,512]{1,0:T(8,128)(2,1)S(1)} %collective-permute-done.12.refs_2_), custom_call_target="tpu_custom_call" | custom-call | flops 1000 | tf_op jit(solution)/shard_map/weigh_last/pallas_call | solution.py:72
  54.6 0.0 copy-start.4
  54.6 2.5 %gather_near.1 = (f32[512,512]{1,0:T(8,128)S(1)}, f32[512,512]{1,0:T(8,128)S(1)}, f32[512,512]{1,0:T(8,128)S(1)}) custom-call(f32[512,512]{1,0:T(8,128)S(1)} %get-tuple-element.122.refs_0_, f32[512,512]{1,0:T(8,128)S(1)} %get-tuple-element.123.refs_1_, f32[512,512]{1,0:T(8,128)S(1)} %get-tuple-element.124.refs_2_, ...), custom_call_target="tpu_custom_call" | custom-call | flops 1000 | tf_op jit(solution)/shard_map/gather_near/pallas_call | solution.py:72
  57.1 0.1 collective-permute-start.19
  57.2 1.9 %low_rank.1.refs_7_ = f32[512,512]{1,0:T(8,128)S(1)} custom-call(bf16[512,512]{1,0:T(8,128)(2,1)S(1)} %copy-done.1, bf16[64,128]{1,0:T(8,128)(2,1)S(1)} %copy-done.4, bf16[640,128]{1,0:T(8,128)(2,1)S(1)} %state_whole.1.state_ref), custom_call_target="tpu_custom_call" | custom-call | flops 1000 | tf_op jit(solution)/shard_map/low_rank/pallas_call | solution.py:72
  59.1 1.6 %collective-permute-done.17.refs_6_ = bf16[512,512]{1,0:T(8,128)(2,1)S(1)} collective-permute-done((bf16[512,512]{1,0:T(8,128)(2,1)}, bf16[512,512]{1,0:T(8,128)(2,1)S(1)}, u32[]{:S(2)}, u32[]{:S(2)}) %collective-permute-start.17) | collective-permute-done | bytes 524320 | tf_op jit(solution)/shard_map/ppermute | solution.py:453
  60.7 0.8 %gather_a.1.refs_0_ = bf16[512,256]{1,0:T(8,128)(2,1)S(1)} custom-call(f32[512,512]{1,0:T(8,128)S(1)} %get-tuple-element.137.refs_0_, f32[512,512]{1,0:T(8,128)S(1)} %get-tuple-element.138.refs_1_, f32[512,512]{1,0:T(8,128)S(1)} %get-tuple-element.139.refs_2_, bf16[512,4096]{1,0:T(8,128)(2,1)S(1)} %get-tuple-element.140.refs_3_, ...), custom_call_target="tpu_custom_call" | custom-call | flops 1000 | tf_op jit(solution)/shard_map/gather_a/pallas_call | solution.py:72
  61.6 0.1 collective-permute-start.20
  61.7 0.8 %gather_b.1.refs_4_ = bf16[512,256]{1,0:T(8,128)(2,1)S(1)} custom-call(f32[512,512]{1,0:T(8,128)S(1)} %get-tuple-element.137.refs_0_, f32[512,512]{1,0:T(8,128)S(1)} %get-tuple-element.138.refs_1_, f32[512,512]{1,0:T(8,128)S(1)} %get-tuple-element.139.refs_2_, bf16[512,4096]{1,0:T(8,128)(2,1)S(1)} %get-tuple-element.140.refs_3_, ...), custom_call_target="tpu_custom_call" | custom-call | flops 1000 | tf_op jit(solution)/shard_map/gather_b/pallas_call | solution.py:72
  62.5 0.6 collective-permute-start.18
  63.1 0.1 collective-permute-done.20.refs_2_
  63.2 0.6 project_a.1.refs_2_
  63.7 0.5 collective-permute-done.18.refs_0_
  64.2 1.1 %project_b.1 = bf16[512,512]{1,0:T(8,128)(2,1)} custom-call(bf16[512,256]{1,0:T(8,128)(2,1)S(1)} %collective-permute-done.18.refs_0_, bf16[512,512]{1,0:T(8,128)(2,1)S(1)} %collective-permute-done.19.refs_3_.refs_1_, f32[512,512]{1,0:T(8,128)S(1)} %project_a.1.refs_2_), custom_call_target="tpu_custom_call" | custom-call | flops 1000 | tf_op jit(solution)/shard_map/project_b/pallas_call | solution.py:362
  (22 shorter events, 0.1 us)
Async XLA Ops:
  0.0 28.4 %copy-start.2 = (bf16[512,1024]{1,0:T(8,128)(2,1)S(1)}, bf16[512,1024]{1,0:T(8,128)(2,1)}, u32[]{:S(2)}) copy-start(bf16[512,1024]{1,0:T(8,128)(2,1)} %ref) | copy-start | bytes 3145732
  0.0 19.5 %collective-permute-start.3 = (bf16[512,512]{1,0:T(8,128)(2,1)}, bf16[512,512]{1,0:T(8,128)(2,1)S(1)}, u32[]{:S(2)}, u32[]{:S(2)}) collective-permute-start(bf16[512,512]{1,0:T(8,128)(2,1)} %refs_1_.2), channel_id=1, source_target_pairs={{8,24},{10,26},{12,28},{14,30},{16,0},{18,2},{20,4},{22,6},{0,8},{... | collective-permute-start | bytes 1572872 | tf_op jit(solution)/shard_map/ppermute | solution.py:453
  3.0 0.7 %copy-start.3 = (bf16[64,128]{1,0:T(8,128)(2,1)S(1)}, bf16[64,128]{1,0:T(8,128)(2,1)}, u32[]{:S(2)}) copy-start(bf16[64,128]{1,0:T(8,128)(2,1)} %feat_ref.1) | copy-start | bytes 49156
  7.8 4.1 %collective-permute-start = (bf16[160,128]{1,0:T(8,128)(2,1)S(1)}, bf16[160,128]{1,0:T(8,128)(2,1)S(1)}, u32[]{:S(2)}, u32[]{:S(2)}) collective-permute-start(bf16[160,128]{1,0:T(8,128)(2,1)S(1)} %get-tuple-element.80), channel_id=1, source_target_pairs={{0,2},{2,0},{4,6},{6,4},{8,10},{10,8},{12,14},{14,12},{16,18},{18,... | collective-permute-start | bytes 122888 | tf_op jit(solution)/shard_map/ppermute | solution.py:448
  9.4 4.0 %collective-permute-start.1 = (bf16[160,128]{1,0:T(8,128)(2,1)S(1)}, bf16[160,128]{1,0:T(8,128)(2,1)S(1)}, u32[]{:S(2)}, u32[]{:S(2)}) collective-permute-start(bf16[160,128]{1,0:T(8,128)(2,1)S(1)} %get-tuple-element.81), channel_id=1, source_target_pairs={{0,4},{2,6},{4,0},{6,2},{8,12},{10,14},{12,8},{14,10},{16,20},{18,... | collective-permute-start | bytes 122888 | tf_op jit(solution)/shard_map/ppermute | solution.py:448
  10.9 4.9 %collective-permute-start.2 = (bf16[160,128]{1,0:T(8,128)(2,1)S(1)}, bf16[160,128]{1,0:T(8,128)(2,1)S(1)}, u32[]{:S(2)}, u32[]{:S(2)}) collective-permute-start(bf16[160,128]{1,0:T(8,128)(2,1)S(1)} %get-tuple-element.82), channel_id=1, source_target_pairs={{0,6},{2,4},{4,2},{6,0},{8,14},{10,12},{12,10},{14,8},{16,22},{18,... | collective-permute-start | bytes 122888 | tf_op jit(solution)/shard_map/ppermute | solution.py:448
  15.8 13.2 %collective-permute-start.5 = (bf16[512,512]{1,0:T(8,128)(2,1)}, bf16[512,512]{1,0:T(8,128)(2,1)S(1)}, u32[]{:S(2)}, u32[]{:S(2)}) collective-permute-start(bf16[512,512]{1,0:T(8,128)(2,1)} %refs_2_.3), channel_id=1, source_target_pairs={{8,24},{10,26},{12,28},{14,30},{16,0},{18,2},{20,4},{22,6},{0,8},{... | collective-permute-start | bytes 1572872 | tf_op jit(solution)/shard_map/ppermute | solution.py:453
  18.4 12.6 %collective-permute-start.7 = (bf16[512,512]{1,0:T(8,128)(2,1)}, bf16[512,512]{1,0:T(8,128)(2,1)S(1)}, u32[]{:S(2)}, u32[]{:S(2)}) collective-permute-start(bf16[512,512]{1,0:T(8,128)(2,1)} %refs_1_.2), channel_id=1, source_target_pairs={{0,4},{2,6},{4,0},{6,2},{8,12},{10,14},{12,8},{14,10},{16,20},{18,... | collective-permute-start | bytes 1572872 | tf_op jit(solution)/shard_map/ppermute | solution.py:448
  18.9 15.1 %collective-permute-start.6 = (bf16[512,512]{1,0:T(8,128)(2,1)}, bf16[512,512]{1,0:T(8,128)(2,1)S(1)}, u32[]{:S(2)}, u32[]{:S(2)}) collective-permute-start(bf16[512,512]{1,0:T(8,128)(2,1)} %refs_1_.2), channel_id=1, source_target_pairs={{0,2},{2,0},{4,6},{6,4},{8,10},{10,8},{12,14},{14,12},{16,18},{18,... | collective-permute-start | bytes 1572872 | tf_op jit(solution)/shard_map/ppermute | solution.py:448
  19.5 1.0 %copy-start = (bf16[512,512]{1,0:T(8,128)(2,1)S(1)}, bf16[512,512]{1,0:T(8,128)(2,1)}, u32[]{:S(2)}) copy-start(bf16[512,512]{1,0:T(8,128)(2,1)} %q_ref.1) | copy-start | bytes 1572868
  22.2 25.4 %collective-permute-start.8 = (bf16[512,512]{1,0:T(8,128)(2,1)}, bf16[512,512]{1,0:T(8,128)(2,1)S(1)}, u32[]{:S(2)}, u32[]{:S(2)}) collective-permute-start(bf16[512,512]{1,0:T(8,128)(2,1)} %refs_2_.3), channel_id=1, source_target_pairs={{0,2},{2,0},{4,6},{6,4},{8,10},{10,8},{12,14},{14,12},{16,18},{18,... | collective-permute-start | bytes 1572872 | tf_op jit(solution)/shard_map/ppermute | solution.py:448
  23.8 6.0 %collective-permute-start.4 = (bf16[160,128]{1,0:T(8,128)(2,1)S(1)}, bf16[160,128]{1,0:T(8,128)(2,1)S(1)}, u32[]{:S(2)}, u32[]{:S(2)}) collective-permute-start(bf16[160,128]{1,0:T(8,128)(2,1)S(1)} %state_plane.1.refs_0_), channel_id=1, source_target_pairs={{0,8},{2,10},{4,12},{6,14},{8,0},{10,2},{12,4},{14,6},{16,24},{18,... | collective-permute-start | bytes 122888 | tf_op jit(solution)/shard_map/ppermute | solution.py:448
  29.8 19.4 %collective-permute-start.9 = (bf16[512,512]{1,0:T(8,128)(2,1)}, bf16[512,512]{1,0:T(8,128)(2,1)S(1)}, u32[]{:S(2)}, u32[]{:S(2)}) collective-permute-start(bf16[512,512]{1,0:T(8,128)(2,1)} %refs_2_.3), channel_id=1, source_target_pairs={{0,4},{2,6},{4,0},{6,2},{8,12},{10,14},{12,8},{14,10},{16,20},{18,... | collective-permute-start | bytes 1572872 | tf_op jit(solution)/shard_map/ppermute | solution.py:448
  30.3 18.9 %collective-permute-start.11 = (bf16[512,512]{1,0:T(8,128)(2,1)S(1)}, bf16[512,512]{1,0:T(8,128)(2,1)S(1)}, u32[]{:S(2)}, u32[]{:S(2)}) collective-permute-start(bf16[512,512]{1,0:T(8,128)(2,1)S(1)} %collective-permute-done.3.refs_1_), channel_id=1, source_target_pairs={{8,16},{10,18},{12,20},{14,22},{16,8},{18,10},{20,12},{22,14},{9,1... | collective-permute-start | bytes 1572872 | tf_op jit(solution)/shard_map/ppermute | solution.py:453
  31.0 18.2 %collective-permute-start.12 = (bf16[512,512]{1,0:T(8,128)(2,1)}, bf16[512,512]{1,0:T(8,128)(2,1)S(1)}, u32[]{:S(2)}, u32[]{:S(2)}) collective-permute-start(bf16[512,512]{1,0:T(8,128)(2,1)} %refs_1_.2), channel_id=1, source_target_pairs={{8,0},{10,2},{12,4},{14,6},{16,24},{18,26},{20,28},{22,30},{9,1},{... | collective-permute-start | bytes 1572872 | tf_op jit(solution)/shard_map/ppermute | solution.py:453
  32.5 5.9 %copy-start.1 = (bf16[512,512]{1,0:T(8,128)(2,1)S(1)}, bf16[512,512]{1,0:T(8,128)(2,1)}, u32[]{:S(2)}) copy-start(bf16[512,512]{1,0:T(8,128)(2,1)} %q_ref.1) | copy-start | bytes 1572868
  34.0 13.0 %collective-permute-start.10 = (bf16[160,128]{1,0:T(8,128)(2,1)S(1)}, bf16[160,128]{1,0:T(8,128)(2,1)S(1)}, u32[]{:S(2)}, u32[]{:S(2)}) collective-permute-start(bf16[160,128]{1,0:T(8,128)(2,1)S(1)} %state_line.1.refs_0_), channel_id=1, source_target_pairs={{0,16},{2,18},{4,20},{6,22},{8,24},{10,26},{12,28},{14,30},{16,0},... | collective-permute-start | bytes 122888 | tf_op jit(solution)/shard_map/ppermute | solution.py:448
  47.0 12.1 %collective-permute-start.16 = (bf16[512,512]{1,0:T(8,128)(2,1)S(1)}, bf16[512,512]{1,0:T(8,128)(2,1)S(1)}, u32[]{:S(2)}, u32[]{:S(2)}) collective-permute-start(bf16[512,512]{1,0:T(8,128)(2,1)S(1)} %collective-permute-done.5.refs_5_), channel_id=1, source_target_pairs={{8,16},{10,18},{12,20},{14,22},{16,8},{18,10},{20,12},{22,14},{9,1... | collective-permute-start | bytes 1572872 | tf_op jit(solution)/shard_map/ppermute | solution.py:453
  47.7 13.1 %collective-permute-start.17 = (bf16[512,512]{1,0:T(8,128)(2,1)}, bf16[512,512]{1,0:T(8,128)(2,1)S(1)}, u32[]{:S(2)}, u32[]{:S(2)}) collective-permute-start(bf16[512,512]{1,0:T(8,128)(2,1)} %refs_2_.3), channel_id=1, source_target_pairs={{8,0},{10,2},{12,4},{14,6},{16,24},{18,26},{20,28},{22,30},{9,1},{... | collective-permute-start | bytes 1572872 | tf_op jit(solution)/shard_map/ppermute | solution.py:453
  49.3 7.8 %collective-permute-start.15 = (bf16[160,128]{1,0:T(8,128)(2,1)S(1)}, bf16[160,128]{1,0:T(8,128)(2,1)S(1)}, u32[]{:S(2)}, u32[]{:S(2)}) collective-permute-start(bf16[160,128]{1,0:T(8,128)(2,1)S(1)} %state_summed.1.refs_0_), channel_id=1, source_target_pairs={{0,6},{2,4},{4,2},{6,0},{8,14},{10,12},{12,10},{14,8},{16,22},{18,... | collective-permute-start | bytes 122888 | tf_op jit(solution)/shard_map/ppermute | solution.py:448
  50.7 6.3 %collective-permute-start.14 = (bf16[160,128]{1,0:T(8,128)(2,1)S(1)}, bf16[160,128]{1,0:T(8,128)(2,1)S(1)}, u32[]{:S(2)}, u32[]{:S(2)}) collective-permute-start(bf16[160,128]{1,0:T(8,128)(2,1)S(1)} %state_summed.1.refs_0_), channel_id=1, source_target_pairs={{0,4},{2,6},{4,0},{6,2},{8,12},{10,14},{12,8},{14,10},{16,20},{18,... | collective-permute-start | bytes 122888 | tf_op jit(solution)/shard_map/ppermute | solution.py:448
  52.3 4.8 %collective-permute-start.13 = (bf16[160,128]{1,0:T(8,128)(2,1)S(1)}, bf16[160,128]{1,0:T(8,128)(2,1)S(1)}, u32[]{:S(2)}, u32[]{:S(2)}) collective-permute-start(bf16[160,128]{1,0:T(8,128)(2,1)S(1)} %state_summed.1.refs_0_), channel_id=1, source_target_pairs={{0,2},{2,0},{4,6},{6,4},{8,10},{10,8},{12,14},{14,12},{16,18},{18,... | collective-permute-start | bytes 122888 | tf_op jit(solution)/shard_map/ppermute | solution.py:448
  54.6 2.7 %copy-start.4 = (bf16[64,128]{1,0:T(8,128)(2,1)S(1)}, bf16[64,128]{1,0:T(8,128)(2,1)}, u32[]{:S(2)}) copy-start(bf16[64,128]{1,0:T(8,128)(2,1)} %feat_ref.1) | copy-start | bytes 49156
  57.1 6.0 %collective-permute-start.19 = (bf16[512,512]{1,0:T(8,128)(2,1)S(1)}, bf16[512,512]{1,0:T(8,128)(2,1)S(1)}, u32[]{:S(2)}, u32[]{:S(2)}) collective-permute-start(bf16[512,512]{1,0:T(8,128)(2,1)S(1)} %get-tuple-element.147), channel_id=1, source_target_pairs={{0,1},{1,0},{2,3},{3,2},{4,5},{5,4},{6,7},{7,6},{8,9},{9,8},{10,11... | collective-permute-start | bytes 1572872 | tf_op jit(solution)/shard_map/ppermute | solution.py:448
  61.6 1.6 %collective-permute-start.20 = (bf16[512,256]{1,0:T(8,128)(2,1)S(1)}, bf16[512,256]{1,0:T(8,128)(2,1)S(1)}, u32[]{:S(2)}, u32[]{:S(2)}) collective-permute-start(bf16[512,256]{1,0:T(8,128)(2,1)S(1)} %gather_a.1.refs_0_), channel_id=1, source_target_pairs={{0,1},{1,0},{2,3},{3,2},{4,5},{5,4},{6,7},{7,6},{8,9},{9,8},{10,11... | collective-permute-start | bytes 786440 | tf_op jit(solution)/shard_map/ppermute | solution.py:448
  62.5 1.7 %collective-permute-start.18 = (bf16[512,256]{1,0:T(8,128)(2,1)S(1)}, bf16[512,256]{1,0:T(8,128)(2,1)S(1)}, u32[]{:S(2)}, u32[]{:S(2)}) collective-permute-start(bf16[512,256]{1,0:T(8,128)(2,1)S(1)} %gather_b.1.refs_4_), channel_id=1, source_target_pairs={{0,1},{1,0},{2,3},{3,2},{4,5},{5,4},{6,7},{7,6},{8,9},{9,8},{10,11... | collective-permute-start | bytes 786440 | tf_op jit(solution)/shard_map/ppermute | solution.py:448

commit v6 on v5

--- a/solution.py
+++ b/solution.py
@@ -252,7 +252,7 @@
                 pltpu.make_async_copy(refs[i].at[:, part], refs[count + 1 + i].at[:, part], done.at[i, c])
                 for i in range(count - 1)
             ])
-        copies[0].append(pltpu.make_async_copy(refs[count - 1], refs[2 * count], done.at[count - 1, 0]))
+        copies[0].insert(0, pltpu.make_async_copy(refs[count - 1], refs[2 * count], done.at[count - 1, 0]))
         for group in copies:
             for copy in group:
                 copy.start()

time: 65.6 us -> 65.6 us (level)
  no operation moved by 1% of the time
where the time goes in v6:
time: 65.6 us; the launch traced here: 65.3 us
  Pallas kernels  24.6 us (38%)
  starting transfers between devices  24.3 us (37%)
  waiting for transfers between devices  14.3 us (22%)
  local copies, waits for them, and re-layouts  1.77 us (3%)
    pallas_call x16, Pallas kernels, kernel_call(): pl.pallas_call(body, out_shape=[pltpu.VMEM(o.shape, o.dtype) for o in out...  19.5 us
    ppermute x15, starting transfers between devices, swapped(): lax.ppermute(shard, axis, [(i, i ^ distance) for i in range(lax.axis_size...  14.3 us
    ppermute x15, waiting for transfers between devices, swapped(): lax.ppermute(shard, axis, [(i, i ^ distance) for i in range(lax.axis_size...  12.2 us
    ppermute x6, starting transfers between devices, moved(): lax.ppermute(shard, 'seq', [(a * span + r, b * span + r) for a, b in step...  9.97 us
    pallas_call x1, Pallas kernels, key_state(): pl.pallas_call(body, out_shape=pltpu.VMEM(outs.shape, outs.dtype), in_spe...  4.06 us
    ppermute x6, waiting for transfers between devices, moved(): lax.ppermute(shard, 'seq', [(a * span + r, b * span + r) for a, b in step...  2.15 us
    unnamed x10, local copies, waits for them, and re-layouts  1.77 us
  transfers between devices with their start and end apart: 21, of which 10 were waited for; matrix products, arithmetic and copies ran while one was open for 0% of the time, Pallas kernels for 36%

profile of v6, /device:TPU:0, one launch (start us, length us, event | category | flops | bytes accessed | tf_op | source)
XLA Modules:
  0.0 65.3 jit_solution(519075496427670135)
XLA Ops:
  0.0 3.0 %collective-permute-start.3 = (bf16[512,512]{1,0:T(8,128)(2,1)}, bf16[512,512]{1,0:T(8,128)(2,1)S(1)}, u32[]{:S(2)}, u32[]{:S(2)}) collective-permute-start(bf16[512,512]{1,0:T(8,128)(2,1)} %refs_1_.2), channel_id=1, source_target_pairs={{8,24},{10,26},{12,28},{14,30},{16,0},{18,2},{20,4},{22,6},{0,8},{... | collective-permute-start | bytes 1572872 | tf_op jit(solution)/shard_map/ppermute | solution.py:453
  3.0 0.7 %copy-done.3 = bf16[64,128]{1,0:T(8,128)(2,1)S(1)} copy-done((bf16[64,128]{1,0:T(8,128)(2,1)S(1)}, bf16[64,128]{1,0:T(8,128)(2,1)}, u32[]{:S(2)}) %copy-start.3) | copy-done | bytes 16408
  3.7 4.1 %key_state.1.ref = bf16[640,128]{1,0:T(8,128)(2,1)S(1)} custom-call(bf16[512,512]{1,0:T(8,128)(2,1)} %refs_1_.2, bf16[512,512]{1,0:T(8,128)(2,1)} %refs_2_.3, bf16[64,128]{1,0:T(8,128)(2,1)S(1)} %copy-done.3), custom_call_target="tpu_custom_call" | custom-call | flops 1000 | tf_op jit(solution)/shard_map/key_state/pallas_call | solution.py:299
  7.8 1.6 %collective-permute-start = (bf16[160,128]{1,0:T(8,128)(2,1)S(1)}, bf16[160,128]{1,0:T(8,128)(2,1)S(1)}, u32[]{:S(2)}, u32[]{:S(2)}) collective-permute-start(bf16[160,128]{1,0:T(8,128)(2,1)S(1)} %get-tuple-element.80), channel_id=1, source_target_pairs={{0,2},{2,0},{4,6},{6,4},{8,10},{10,8},{12,14},{14,12},{16,18},{18,... | collective-permute-start | bytes 122888 | tf_op jit(solution)/shard_map/ppermute | solution.py:448
  9.4 1.5 %collective-permute-start.1 = (bf16[160,128]{1,0:T(8,128)(2,1)S(1)}, bf16[160,128]{1,0:T(8,128)(2,1)S(1)}, u32[]{:S(2)}, u32[]{:S(2)}) collective-permute-start(bf16[160,128]{1,0:T(8,128)(2,1)S(1)} %get-tuple-element.81), channel_id=1, source_target_pairs={{0,4},{2,6},{4,0},{6,2},{8,12},{10,14},{12,8},{14,10},{16,20},{18,... | collective-permute-start | bytes 122888 | tf_op jit(solution)/shard_map/ppermute | solution.py:448
  10.9 0.5 collective-permute-start.2
  11.4 0.5 collective-permute-done.refs_1_
  11.9 1.5 %collective-permute-done.1.refs_2_ = bf16[160,128]{1,0:T(8,128)(2,1)S(1)} collective-permute-done((bf16[160,128]{1,0:T(8,128)(2,1)S(1)}, bf16[160,128]{1,0:T(8,128)(2,1)S(1)}, u32[]{:S(2)}, u32[]{:S(2)}) %collective-permute-start.1) | collective-permute-done | bytes 40992 | tf_op jit(solution)/shard_map/ppermute | solution.py:448
  13.4 2.4 %collective-permute-done.2.refs_3_ = bf16[160,128]{1,0:T(8,128)(2,1)S(1)} collective-permute-done((bf16[160,128]{1,0:T(8,128)(2,1)S(1)}, bf16[160,128]{1,0:T(8,128)(2,1)S(1)}, u32[]{:S(2)}, u32[]{:S(2)}) %collective-permute-start.2) | collective-permute-done | bytes 40992 | tf_op jit(solution)/shard_map/ppermute | solution.py:448
  15.8 2.6 %collective-permute-start.5 = (bf16[512,512]{1,0:T(8,128)(2,1)}, bf16[512,512]{1,0:T(8,128)(2,1)S(1)}, u32[]{:S(2)}, u32[]{:S(2)}) collective-permute-start(bf16[512,512]{1,0:T(8,128)(2,1)} %refs_2_.3), channel_id=1, source_target_pairs={{8,24},{10,26},{12,28},{14,30},{16,0},{18,2},{20,4},{22,6},{0,8},{... | collective-permute-start | bytes 1572872 | tf_op jit(solution)/shard_map/ppermute | solution.py:453
  18.4 0.5 collective-permute-start.7
  18.9 0.5 collective-permute-start.6
  19.5 1.0 %copy-done = bf16[512,512]{1,0:T(8,128)(2,1)S(1)} copy-done((bf16[512,512]{1,0:T(8,128)(2,1)S(1)}, bf16[512,512]{1,0:T(8,128)(2,1)}, u32[]{:S(2)}) %copy-start) | copy-done | bytes 524312
  20.5 1.7 %weigh_first.1 = (bf16[512,4096]{1,0:T(8,128)(2,1)S(1)}, f32[512,512]{1,0:T(8,128)S(1)}) custom-call(bf16[512,512]{1,0:T(8,128)(2,1)S(1)} %copy-done, bf16[512,512]{1,0:T(8,128)(2,1)S(1)} %collective-permute-done.3.refs_1_), custom_call_target="tpu_custom_call" | custom-call | flops 1000 | tf_op jit(solution)/shard_map/weigh_first/pallas_call | solution.py:72
  22.2 1.6 %collective-permute-start.8 = (bf16[512,512]{1,0:T(8,128)(2,1)}, bf16[512,512]{1,0:T(8,128)(2,1)S(1)}, u32[]{:S(2)}, u32[]{:S(2)}) collective-permute-start(bf16[512,512]{1,0:T(8,128)(2,1)} %refs_2_.3), channel_id=1, source_target_pairs={{0,2},{2,0},{4,6},{6,4},{8,10},{10,8},{12,14},{14,12},{16,18},{18,... | collective-permute-start | bytes 1572872 | tf_op jit(solution)/shard_map/ppermute | solution.py:448
  23.8 0.5 collective-permute-start.4
  24.3 4.1 %attend_own.1 = (f32[512,512]{1,0:T(8,128)S(1)}, f32[512,512]{1,0:T(8,128)S(1)}, f32[512,512]{1,0:T(8,128)S(1)}) custom-call(bf16[512,512]{1,0:T(8,128)(2,1)S(1)} %copy-done, bf16[512,512]{1,0:T(8,128)(2,1)} %refs_1_.2, bf16[512,512]{1,0:T(8,128)(2,1)} %refs_2_.3), custom_call_target="tpu_custom_call" | custom-call | flops 1000 | tf_op jit(solution)/shard_map/attend_own/pallas_call | solution.py:72
  28.4 0.1 weights_parted.1
  28.5 0.5 collective-permute-done.5.refs_5_
  29.0 0.8 %collective-permute-done.4.refs_1_ = bf16[160,128]{1,0:T(8,128)(2,1)S(1)} collective-permute-done((bf16[160,128]{1,0:T(8,128)(2,1)S(1)}, bf16[160,128]{1,0:T(8,128)(2,1)S(1)}, u32[]{:S(2)}, u32[]{:S(2)}) %collective-permute-start.4) | collective-permute-done | bytes 40992 | tf_op jit(solution)/shard_map/ppermute | solution.py:448
  29.8 0.5 collective-permute-start.9
  30.3 0.7 %collective-permute-start.11 = (bf16[512,512]{1,0:T(8,128)(2,1)S(1)}, bf16[512,512]{1,0:T(8,128)(2,1)S(1)}, u32[]{:S(2)}, u32[]{:S(2)}) collective-permute-start(bf16[512,512]{1,0:T(8,128)(2,1)S(1)} %collective-permute-done.3.refs_1_), channel_id=1, source_target_pairs={{8,16},{10,18},{12,20},{14,22},{16,8},{18,10},{20,12},{22,14},{9,1... | collective-permute-start | bytes 1572872 | tf_op jit(solution)/shard_map/ppermute | solution.py:453
  31.0 1.5 %collective-permute-start.12 = (bf16[512,512]{1,0:T(8,128)(2,1)}, bf16[512,512]{1,0:T(8,128)(2,1)S(1)}, u32[]{:S(2)}, u32[]{:S(2)}) collective-permute-start(bf16[512,512]{1,0:T(8,128)(2,1)} %refs_1_.2), channel_id=1, source_target_pairs={{8,0},{10,2},{12,4},{14,6},{16,24},{18,26},{20,28},{22,30},{9,1},{... | collective-permute-start | bytes 1572872 | tf_op jit(solution)/shard_map/ppermute | solution.py:453
  32.5 0.0 copy-start.1
  32.5 1.5 %collective-permute-done.6.refs_1_ = bf16[512,512]{1,0:T(8,128)(2,1)S(1)} collective-permute-done((bf16[512,512]{1,0:T(8,128)(2,1)}, bf16[512,512]{1,0:T(8,128)(2,1)S(1)}, u32[]{:S(2)}, u32[]{:S(2)}) %collective-permute-start.6) | collective-permute-done | bytes 524320 | tf_op jit(solution)/shard_map/ppermute | solution.py:448
  34.0 3.0 %collective-permute-start.10 = (bf16[160,128]{1,0:T(8,128)(2,1)S(1)}, bf16[160,128]{1,0:T(8,128)(2,1)S(1)}, u32[]{:S(2)}, u32[]{:S(2)}) collective-permute-start(bf16[160,128]{1,0:T(8,128)(2,1)S(1)} %state_line.1.refs_0_), channel_id=1, source_target_pairs={{0,16},{2,18},{4,20},{6,22},{8,24},{10,26},{12,28},{14,30},{16,0},... | collective-permute-start | bytes 122888 | tf_op jit(solution)/shard_map/ppermute | solution.py:448
  37.0 1.4 %gather_first.1 = (f32[512,512]{1,0:T(8,128)S(1)}, f32[512,512]{1,0:T(8,128)S(1)}, f32[512,512]{1,0:T(8,128)S(1)}) custom-call(f32[512,512]{1,0:T(8,128)S(1)} %get-tuple-element.101.refs_0_, f32[512,512]{1,0:T(8,128)S(1)} %get-tuple-element.102.refs_1_, f32[512,512]{1,0:T(8,128)S(1)} %get-tuple-element.103.refs_2_, ...), custom_call_target="tpu_custom_call" | custom-call | flops 1000 | tf_op jit(solution)/shard_map/gather_first/pallas_call | solution.py:72
  38.4 3.7 %weigh_near.1 = (bf16[512,8192]{1,0:T(8,128)(2,1)S(1)}, f32[512,512]{1,0:T(8,128)S(1)}) custom-call(bf16[512,512]{1,0:T(8,128)(2,1)S(1)} %copy-done.1, bf16[512,512]{1,0:T(8,128)(2,1)S(1)} %collective-permute-done.6.refs_1_, bf16[512,512]{1,0:T(8,128)(2,1)S(1)} %collective-permute-done.7.refs_2_), custom_call_target="tpu_custom_call" | custom-call | flops 1000 | tf_op jit(solution)/shard_map/weigh_near/pallas_call | solution.py:72
  42.1 4.9 %collective-permute-done.10.refs_1_ = bf16[160,128]{1,0:T(8,128)(2,1)S(1)} collective-permute-done((bf16[160,128]{1,0:T(8,128)(2,1)S(1)}, bf16[160,128]{1,0:T(8,128)(2,1)S(1)}, u32[]{:S(2)}, u32[]{:S(2)}) %collective-permute-start.10) | collective-permute-done | bytes 40992 | tf_op jit(solution)/shard_map/ppermute | solution.py:448
  47.0 0.7 %collective-permute-start.16 = (bf16[512,512]{1,0:T(8,128)(2,1)S(1)}, bf16[512,512]{1,0:T(8,128)(2,1)S(1)}, u32[]{:S(2)}, u32[]{:S(2)}) collective-permute-start(bf16[512,512]{1,0:T(8,128)(2,1)S(1)} %collective-permute-done.5.refs_5_), channel_id=1, source_target_pairs={{8,16},{10,18},{12,20},{14,22},{16,8},{18,10},{20,12},{22,14},{9,1... | collective-permute-start | bytes 1572872 | tf_op jit(solution)/shard_map/ppermute | solution.py:453
  47.7 1.5 %collective-permute-start.17 = (bf16[512,512]{1,0:T(8,128)(2,1)}, bf16[512,512]{1,0:T(8,128)(2,1)S(1)}, u32[]{:S(2)}, u32[]{:S(2)}) collective-permute-start(bf16[512,512]{1,0:T(8,128)(2,1)} %refs_2_.3), channel_id=1, source_target_pairs={{8,0},{10,2},{12,4},{14,6},{16,24},{18,26},{20,28},{22,30},{9,1},{... | collective-permute-start | bytes 1572872 | tf_op jit(solution)/shard_map/ppermute | solution.py:453
  49.3 1.5 %collective-permute-start.15 = (bf16[160,128]{1,0:T(8,128)(2,1)S(1)}, bf16[160,128]{1,0:T(8,128)(2,1)S(1)}, u32[]{:S(2)}, u32[]{:S(2)}) collective-permute-start(bf16[160,128]{1,0:T(8,128)(2,1)S(1)} %state_summed.1.refs_0_), channel_id=1, source_target_pairs={{0,6},{2,4},{4,2},{6,0},{8,14},{10,12},{12,10},{14,8},{16,22},{18,... | collective-permute-start | bytes 122888 | tf_op jit(solution)/shard_map/ppermute | solution.py:448
  50.8 1.5 %collective-permute-start.14 = (bf16[160,128]{1,0:T(8,128)(2,1)S(1)}, bf16[160,128]{1,0:T(8,128)(2,1)S(1)}, u32[]{:S(2)}, u32[]{:S(2)}) collective-permute-start(bf16[160,128]{1,0:T(8,128)(2,1)S(1)} %state_summed.1.refs_0_), channel_id=1, source_target_pairs={{0,4},{2,6},{4,0},{6,2},{8,12},{10,14},{12,8},{14,10},{16,20},{18,... | collective-permute-start | bytes 122888 | tf_op jit(solution)/shard_map/ppermute | solution.py:448
  52.3 0.5 collective-permute-start.13
  52.8 1.7 %weigh_last.1 = (bf16[512,4096]{1,0:T(8,128)(2,1)S(1)}, f32[512,512]{1,0:T(8,128)S(1)}) custom-call(bf16[512,512]{1,0:T(8,128)(2,1)S(1)} %copy-done.1, bf16[512,512]{1,0:T(8,128)(2,1)S(1)} %collective-permute-done.11.refs_1_, bf16[512,512]{1,0:T(8,128)(2,1)S(1)} %collective-permute-done.12.refs_2_), custom_call_target="tpu_custom_call" | custom-call | flops 1000 | tf_op jit(solution)/shard_map/weigh_last/pallas_call | solution.py:72
  54.6 0.0 copy-start.4
  54.6 2.5 %gather_near.1 = (f32[512,512]{1,0:T(8,128)S(1)}, f32[512,512]{1,0:T(8,128)S(1)}, f32[512,512]{1,0:T(8,128)S(1)}) custom-call(f32[512,512]{1,0:T(8,128)S(1)} %get-tuple-element.122.refs_0_, f32[512,512]{1,0:T(8,128)S(1)} %get-tuple-element.123.refs_1_, f32[512,512]{1,0:T(8,128)S(1)} %get-tuple-element.124.refs_2_, ...), custom_call_target="tpu_custom_call" | custom-call | flops 1000 | tf_op jit(solution)/shard_map/gather_near/pallas_call | solution.py:72
  57.1 0.1 collective-permute-start.19
  57.2 1.9 %low_rank.1.refs_7_ = f32[512,512]{1,0:T(8,128)S(1)} custom-call(bf16[512,512]{1,0:T(8,128)(2,1)S(1)} %copy-done.1, bf16[64,128]{1,0:T(8,128)(2,1)S(1)} %copy-done.4, bf16[640,128]{1,0:T(8,128)(2,1)S(1)} %state_whole.1.state_ref), custom_call_target="tpu_custom_call" | custom-call | flops 1000 | tf_op jit(solution)/shard_map/low_rank/pallas_call | solution.py:72
  59.1 1.6 %collective-permute-done.17.refs_6_ = bf16[512,512]{1,0:T(8,128)(2,1)S(1)} collective-permute-done((bf16[512,512]{1,0:T(8,128)(2,1)}, bf16[512,512]{1,0:T(8,128)(2,1)S(1)}, u32[]{:S(2)}, u32[]{:S(2)}) %collective-permute-start.17) | collective-permute-done | bytes 524320 | tf_op jit(solution)/shard_map/ppermute | solution.py:453
  60.7 0.8 %gather_a.1.refs_0_ = bf16[512,256]{1,0:T(8,128)(2,1)S(1)} custom-call(f32[512,512]{1,0:T(8,128)S(1)} %get-tuple-element.137.refs_0_, f32[512,512]{1,0:T(8,128)S(1)} %get-tuple-element.138.refs_1_, f32[512,512]{1,0:T(8,128)S(1)} %get-tuple-element.139.refs_2_, bf16[512,4096]{1,0:T(8,128)(2,1)S(1)} %get-tuple-element.140.refs_3_, ...), custom_call_target="tpu_custom_call" | custom-call | flops 1000 | tf_op jit(solution)/shard_map/gather_a/pallas_call | solution.py:72
  61.6 0.1 collective-permute-start.20
  61.7 0.8 %gather_b.1.refs_4_ = bf16[512,256]{1,0:T(8,128)(2,1)S(1)} custom-call(f32[512,512]{1,0:T(8,128)S(1)} %get-tuple-element.137.refs_0_, f32[512,512]{1,0:T(8,128)S(1)} %get-tuple-element.138.refs_1_, f32[512,512]{1,0:T(8,128)S(1)} %get-tuple-element.139.refs_2_, bf16[512,4096]{1,0:T(8,128)(2,1)S(1)} %get-tuple-element.140.refs_3_, ...), custom_call_target="tpu_custom_call" | custom-call | flops 1000 | tf_op jit(solution)/shard_map/gather_b/pallas_call | solution.py:72
  62.5 0.6 collective-permute-start.18
  63.1 0.1 collective-permute-done.20.refs_2_
  63.2 0.6 project_a.1.refs_2_
  63.7 0.5 collective-permute-done.18.refs_0_
  64.2 1.1 %project_b.1 = bf16[512,512]{1,0:T(8,128)(2,1)} custom-call(bf16[512,256]{1,0:T(8,128)(2,1)S(1)} %collective-permute-done.18.refs_0_, bf16[512,512]{1,0:T(8,128)(2,1)S(1)} %collective-permute-done.19.refs_3_.refs_1_, f32[512,512]{1,0:T(8,128)S(1)} %project_a.1.refs_2_), custom_call_target="tpu_custom_call" | custom-call | flops 1000 | tf_op jit(solution)/shard_map/project_b/pallas_call | solution.py:362
  (22 shorter events, 0.1 us)
Async XLA Ops:
  0.0 28.4 %copy-start.2 = (bf16[512,1024]{1,0:T(8,128)(2,1)S(1)}, bf16[512,1024]{1,0:T(8,128)(2,1)}, u32[]{:S(2)}) copy-start(bf16[512,1024]{1,0:T(8,128)(2,1)} %ref) | copy-start | bytes 3145732
  0.0 19.5 %collective-permute-start.3 = (bf16[512,512]{1,0:T(8,128)(2,1)}, bf16[512,512]{1,0:T(8,128)(2,1)S(1)}, u32[]{:S(2)}, u32[]{:S(2)}) collective-permute-start(bf16[512,512]{1,0:T(8,128)(2,1)} %refs_1_.2), channel_id=1, source_target_pairs={{8,24},{10,26},{12,28},{14,30},{16,0},{18,2},{20,4},{22,6},{0,8},{... | collective-permute-start | bytes 1572872 | tf_op jit(solution)/shard_map/ppermute | solution.py:453
  3.0 0.7 %copy-start.3 = (bf16[64,128]{1,0:T(8,128)(2,1)S(1)}, bf16[64,128]{1,0:T(8,128)(2,1)}, u32[]{:S(2)}) copy-start(bf16[64,128]{1,0:T(8,128)(2,1)} %feat_ref.1) | copy-start | bytes 49156
  7.8 4.1 %collective-permute-start = (bf16[160,128]{1,0:T(8,128)(2,1)S(1)}, bf16[160,128]{1,0:T(8,128)(2,1)S(1)}, u32[]{:S(2)}, u32[]{:S(2)}) collective-permute-start(bf16[160,128]{1,0:T(8,128)(2,1)S(1)} %get-tuple-element.80), channel_id=1, source_target_pairs={{0,2},{2,0},{4,6},{6,4},{8,10},{10,8},{12,14},{14,12},{16,18},{18,... | collective-permute-start | bytes 122888 | tf_op jit(solution)/shard_map/ppermute | solution.py:448
  9.4 4.0 %collective-permute-start.1 = (bf16[160,128]{1,0:T(8,128)(2,1)S(1)}, bf16[160,128]{1,0:T(8,128)(2,1)S(1)}, u32[]{:S(2)}, u32[]{:S(2)}) collective-permute-start(bf16[160,128]{1,0:T(8,128)(2,1)S(1)} %get-tuple-element.81), channel_id=1, source_target_pairs={{0,4},{2,6},{4,0},{6,2},{8,12},{10,14},{12,8},{14,10},{16,20},{18,... | collective-permute-start | bytes 122888 | tf_op jit(solution)/shard_map/ppermute | solution.py:448
  10.9 4.9 %collective-permute-start.2 = (bf16[160,128]{1,0:T(8,128)(2,1)S(1)}, bf16[160,128]{1,0:T(8,128)(2,1)S(1)}, u32[]{:S(2)}, u32[]{:S(2)}) collective-permute-start(bf16[160,128]{1,0:T(8,128)(2,1)S(1)} %get-tuple-element.82), channel_id=1, source_target_pairs={{0,6},{2,4},{4,2},{6,0},{8,14},{10,12},{12,10},{14,8},{16,22},{18,... | collective-permute-start | bytes 122888 | tf_op jit(solution)/shard_map/ppermute | solution.py:448
  15.8 13.2 %collective-permute-start.5 = (bf16[512,512]{1,0:T(8,128)(2,1)}, bf16[512,512]{1,0:T(8,128)(2,1)S(1)}, u32[]{:S(2)}, u32[]{:S(2)}) collective-permute-start(bf16[512,512]{1,0:T(8,128)(2,1)} %refs_2_.3), channel_id=1, source_target_pairs={{8,24},{10,26},{12,28},{14,30},{16,0},{18,2},{20,4},{22,6},{0,8},{... | collective-permute-start | bytes 1572872 | tf_op jit(solution)/shard_map/ppermute | solution.py:453
  18.4 12.6 %collective-permute-start.7 = (bf16[512,512]{1,0:T(8,128)(2,1)}, bf16[512,512]{1,0:T(8,128)(2,1)S(1)}, u32[]{:S(2)}, u32[]{:S(2)}) collective-permute-start(bf16[512,512]{1,0:T(8,128)(2,1)} %refs_1_.2), channel_id=1, source_target_pairs={{0,4},{2,6},{4,0},{6,2},{8,12},{10,14},{12,8},{14,10},{16,20},{18,... | collective-permute-start | bytes 1572872 | tf_op jit(solution)/shard_map/ppermute | solution.py:448
  18.9 15.1 %collective-permute-start.6 = (bf16[512,512]{1,0:T(8,128)(2,1)}, bf16[512,512]{1,0:T(8,128)(2,1)S(1)}, u32[]{:S(2)}, u32[]{:S(2)}) collective-permute-start(bf16[512,512]{1,0:T(8,128)(2,1)} %refs_1_.2), channel_id=1, source_target_pairs={{0,2},{2,0},{4,6},{6,4},{8,10},{10,8},{12,14},{14,12},{16,18},{18,... | collective-permute-start | bytes 1572872 | tf_op jit(solution)/shard_map/ppermute | solution.py:448
  19.5 1.0 %copy-start = (bf16[512,512]{1,0:T(8,128)(2,1)S(1)}, bf16[512,512]{1,0:T(8,128)(2,1)}, u32[]{:S(2)}) copy-start(bf16[512,512]{1,0:T(8,128)(2,1)} %q_ref.1) | copy-start | bytes 1572868
  22.2 25.4 %collective-permute-start.8 = (bf16[512,512]{1,0:T(8,128)(2,1)}, bf16[512,512]{1,0:T(8,128)(2,1)S(1)}, u32[]{:S(2)}, u32[]{:S(2)}) collective-permute-start(bf16[512,512]{1,0:T(8,128)(2,1)} %refs_2_.3), channel_id=1, source_target_pairs={{0,2},{2,0},{4,6},{6,4},{8,10},{10,8},{12,14},{14,12},{16,18},{18,... | collective-permute-start | bytes 1572872 | tf_op jit(solution)/shard_map/ppermute | solution.py:448
  23.8 6.0 %collective-permute-start.4 = (bf16[160,128]{1,0:T(8,128)(2,1)S(1)}, bf16[160,128]{1,0:T(8,128)(2,1)S(1)}, u32[]{:S(2)}, u32[]{:S(2)}) collective-permute-start(bf16[160,128]{1,0:T(8,128)(2,1)S(1)} %state_plane.1.refs_0_), channel_id=1, source_target_pairs={{0,8},{2,10},{4,12},{6,14},{8,0},{10,2},{12,4},{14,6},{16,24},{18,... | collective-permute-start | bytes 122888 | tf_op jit(solution)/shard_map/ppermute | solution.py:448
  29.8 19.4 %collective-permute-start.9 = (bf16[512,512]{1,0:T(8,128)(2,1)}, bf16[512,512]{1,0:T(8,128)(2,1)S(1)}, u32[]{:S(2)}, u32[]{:S(2)}) collective-permute-start(bf16[512,512]{1,0:T(8,128)(2,1)} %refs_2_.3), channel_id=1, source_target_pairs={{0,4},{2,6},{4,0},{6,2},{8,12},{10,14},{12,8},{14,10},{16,20},{18,... | collective-permute-start | bytes 1572872 | tf_op jit(solution)/shard_map/ppermute | solution.py:448
  30.3 18.9 %collective-permute-start.11 = (bf16[512,512]{1,0:T(8,128)(2,1)S(1)}, bf16[512,512]{1,0:T(8,128)(2,1)S(1)}, u32[]{:S(2)}, u32[]{:S(2)}) collective-permute-start(bf16[512,512]{1,0:T(8,128)(2,1)S(1)} %collective-permute-done.3.refs_1_), channel_id=1, source_target_pairs={{8,16},{10,18},{12,20},{14,22},{16,8},{18,10},{20,12},{22,14},{9,1... | collective-permute-start | bytes 1572872 | tf_op jit(solution)/shard_map/ppermute | solution.py:453
  31.0 18.2 %collective-permute-start.12 = (bf16[512,512]{1,0:T(8,128)(2,1)}, bf16[512,512]{1,0:T(8,128)(2,1)S(1)}, u32[]{:S(2)}, u32[]{:S(2)}) collective-permute-start(bf16[512,512]{1,0:T(8,128)(2,1)} %refs_1_.2), channel_id=1, source_target_pairs={{8,0},{10,2},{12,4},{14,6},{16,24},{18,26},{20,28},{22,30},{9,1},{... | collective-permute-start | bytes 1572872 | tf_op jit(solution)/shard_map/ppermute | solution.py:453
  32.5 5.9 %copy-start.1 = (bf16[512,512]{1,0:T(8,128)(2,1)S(1)}, bf16[512,512]{1,0:T(8,128)(2,1)}, u32[]{:S(2)}) copy-start(bf16[512,512]{1,0:T(8,128)(2,1)} %q_ref.1) | copy-start | bytes 1572868
  34.0 13.0 %collective-permute-start.10 = (bf16[160,128]{1,0:T(8,128)(2,1)S(1)}, bf16[160,128]{1,0:T(8,128)(2,1)S(1)}, u32[]{:S(2)}, u32[]{:S(2)}) collective-permute-start(bf16[160,128]{1,0:T(8,128)(2,1)S(1)} %state_line.1.refs_0_), channel_id=1, source_target_pairs={{0,16},{2,18},{4,20},{6,22},{8,24},{10,26},{12,28},{14,30},{16,0},... | collective-permute-start | bytes 122888 | tf_op jit(solution)/shard_map/ppermute | solution.py:448
  47.0 12.1 %collective-permute-start.16 = (bf16[512,512]{1,0:T(8,128)(2,1)S(1)}, bf16[512,512]{1,0:T(8,128)(2,1)S(1)}, u32[]{:S(2)}, u32[]{:S(2)}) collective-permute-start(bf16[512,512]{1,0:T(8,128)(2,1)S(1)} %collective-permute-done.5.refs_5_), channel_id=1, source_target_pairs={{8,16},{10,18},{12,20},{14,22},{16,8},{18,10},{20,12},{22,14},{9,1... | collective-permute-start | bytes 1572872 | tf_op jit(solution)/shard_map/ppermute | solution.py:453
  47.7 13.1 %collective-permute-start.17 = (bf16[512,512]{1,0:T(8,128)(2,1)}, bf16[512,512]{1,0:T(8,128)(2,1)S(1)}, u32[]{:S(2)}, u32[]{:S(2)}) collective-permute-start(bf16[512,512]{1,0:T(8,128)(2,1)} %refs_2_.3), channel_id=1, source_target_pairs={{8,0},{10,2},{12,4},{14,6},{16,24},{18,26},{20,28},{22,30},{9,1},{... | collective-permute-start | bytes 1572872 | tf_op jit(solution)/shard_map/ppermute | solution.py:453
  49.3 7.8 %collective-permute-start.15 = (bf16[160,128]{1,0:T(8,128)(2,1)S(1)}, bf16[160,128]{1,0:T(8,128)(2,1)S(1)}, u32[]{:S(2)}, u32[]{:S(2)}) collective-permute-start(bf16[160,128]{1,0:T(8,128)(2,1)S(1)} %state_summed.1.refs_0_), channel_id=1, source_target_pairs={{0,6},{2,4},{4,2},{6,0},{8,14},{10,12},{12,10},{14,8},{16,22},{18,... | collective-permute-start | bytes 122888 | tf_op jit(solution)/shard_map/ppermute | solution.py:448
  50.8 6.3 %collective-permute-start.14 = (bf16[160,128]{1,0:T(8,128)(2,1)S(1)}, bf16[160,128]{1,0:T(8,128)(2,1)S(1)}, u32[]{:S(2)}, u32[]{:S(2)}) collective-permute-start(bf16[160,128]{1,0:T(8,128)(2,1)S(1)} %state_summed.1.refs_0_), channel_id=1, source_target_pairs={{0,4},{2,6},{4,0},{6,2},{8,12},{10,14},{12,8},{14,10},{16,20},{18,... | collective-permute-start | bytes 122888 | tf_op jit(solution)/shard_map/ppermute | solution.py:448
  52.3 4.8 %collective-permute-start.13 = (bf16[160,128]{1,0:T(8,128)(2,1)S(1)}, bf16[160,128]{1,0:T(8,128)(2,1)S(1)}, u32[]{:S(2)}, u32[]{:S(2)}) collective-permute-start(bf16[160,128]{1,0:T(8,128)(2,1)S(1)} %state_summed.1.refs_0_), channel_id=1, source_target_pairs={{0,2},{2,0},{4,6},{6,4},{8,10},{10,8},{12,14},{14,12},{16,18},{18,... | collective-permute-start | bytes 122888 | tf_op jit(solution)/shard_map/ppermute | solution.py:448
  54.6 2.7 %copy-start.4 = (bf16[64,128]{1,0:T(8,128)(2,1)S(1)}, bf16[64,128]{1,0:T(8,128)(2,1)}, u32[]{:S(2)}) copy-start(bf16[64,128]{1,0:T(8,128)(2,1)} %feat_ref.1) | copy-start | bytes 49156
  57.1 6.0 %collective-permute-start.19 = (bf16[512,512]{1,0:T(8,128)(2,1)S(1)}, bf16[512,512]{1,0:T(8,128)(2,1)S(1)}, u32[]{:S(2)}, u32[]{:S(2)}) collective-permute-start(bf16[512,512]{1,0:T(8,128)(2,1)S(1)} %get-tuple-element.147), channel_id=1, source_target_pairs={{0,1},{1,0},{2,3},{3,2},{4,5},{5,4},{6,7},{7,6},{8,9},{9,8},{10,11... | collective-permute-start | bytes 1572872 | tf_op jit(solution)/shard_map/ppermute | solution.py:448
  61.6 1.6 %collective-permute-start.20 = (bf16[512,256]{1,0:T(8,128)(2,1)S(1)}, bf16[512,256]{1,0:T(8,128)(2,1)S(1)}, u32[]{:S(2)}, u32[]{:S(2)}) collective-permute-start(bf16[512,256]{1,0:T(8,128)(2,1)S(1)} %gather_a.1.refs_0_), channel_id=1, source_target_pairs={{0,1},{1,0},{2,3},{3,2},{4,5},{5,4},{6,7},{7,6},{8,9},{9,8},{10,11... | collective-permute-start | bytes 786440 | tf_op jit(solution)/shard_map/ppermute | solution.py:448
  62.5 1.7 %collective-permute-start.18 = (bf16[512,256]{1,0:T(8,128)(2,1)S(1)}, bf16[512,256]{1,0:T(8,128)(2,1)S(1)}, u32[]{:S(2)}, u32[]{:S(2)}) collective-permute-start(bf16[512,256]{1,0:T(8,128)(2,1)S(1)} %gather_b.1.refs_4_), channel_id=1, source_target_pairs={{0,1},{1,0},{2,3},{3,2},{4,5},{5,4},{6,7},{7,6},{8,9},{9,8},{10,11... | collective-permute-start | bytes 786440 | tf_op jit(solution)/shard_map/ppermute | solution.py:448
